TPU v7x, 256 devices: a whole 4x4x8 slice. The times are simulated.
256 devices in a mesh: ctx: 32 (over x, y, core), head: 8 (over z).
Axes of the slice: x: 4, y: 4, z: 8, core: 2. Of those that a mesh axis runs over, the one named last changes fastest.
Arguments:
- queries: bfloat16 [4096, 16384], P(('ctx', 'head')), may hold values from -12 to 12
- keys: bfloat16 [4096, 1024], P(('ctx', 'head')), may hold values from -4.5 to 4.5
- values: bfloat16 [4096, 1024], P(('ctx', 'head')), may hold values from -5 to 5
- grad_out: bfloat16 [4096, 16384], P(('ctx', 'head')), may hold values from -5 to 5
- doc_lengths: int32 [8], replicated, may hold values from 1 to 2048, 4096 in all
- block_pairs: int32 [248, 2], replicated, may hold values from 0 to 31, as said below
- scale_index: int32 [2, 32, 8], replicated, may hold values from 0 to 15
- scale_table: float32 [2, 16], replicated, may hold values from 0.5 to 1.5
Outputs:
- attn_out: bfloat16 [4096, 16384], P(('ctx', 'head'))
- grad_queries: bfloat16 [4096, 16384], P(('ctx', 'head'))
- grad_keys: bfloat16 [4096, 1024], P(('ctx', 'head'))
- grad_values: bfloat16 [4096, 1024], P(('ctx', 'head'))
Inputs may be any that keep to these rules, and one draw needn't show every extreme that they name: `doc_lengths`: the 8 lengths sum to 4096; the longest is exactly 2048. `block_pairs`: each row is a pair (query block, key block) of blocks of 128 tokens with the key block below the query block; the 248 rows are distinct.
All inputs are finite; a program needn't handle non-finite values.
Results may differ from a plain program's by a relative error of at most 0.014.
Values may be sent and summed in bfloat16 or wider, within the bound.
A program may use at most 64 MiB of HBM per device.

v0:
```python
import math

import jax
import jax.numpy as jnp
from jax import lax
from jax.sharding import PartitionSpec as P

QH = 128
KVH = 8
HD = 128
BLK = 128


neg_big = -1e30
rope_base = 500000.0


def rotate(vectors, position, turning):
    half_width = vectors.shape[-1] // 2
    frequency = jnp.exp(
        jnp.arange(half_width, dtype=jnp.float32) * (-2.0 * math.log(rope_base) / vectors.shape[-1])
    )
    angles = position.astype(jnp.float32)[:, None] * frequency[None, :]
    cosine = jnp.cos(angles)[:, None, :]
    sine_part = turning * jnp.sin(angles)[:, None, :]
    first_half = vectors[..., :half_width]
    second = vectors[..., half_width:]
    return jnp.concatenate(
        [first_half * cosine - second * sine_part, second * cosine + first_half * sine_part],
        axis=-1,
    )


def doc_and_pos(token_index, doc_lengths):
    doc_ends = jnp.cumsum(doc_lengths)
    before = (doc_ends[None, :] <= token_index[:, None]).astype(jnp.int32)
    doc_id = jnp.sum(before, axis=1)
    doc_start = jnp.sum(before * doc_lengths[None, :], axis=1)
    return (doc_id, token_index - doc_start)


def block_scales(scale_index, scale_table, table_row):
    options = jnp.arange(scale_table.shape[1], dtype=jnp.int32)
    one_hot = (scale_index[table_row][..., None] == options).astype(jnp.float32)
    return jnp.sum(one_hot * scale_table[table_row], axis=-1)


def visible(q_index, q_doc, row_listed, k_index, k_doc, blocks):
    key_hot = ((k_index // BLK)[:, None] == blocks[None, :]).astype(jnp.bfloat16)
    listed = (
        lax.dot_general(
            row_listed, key_hot, (((1,), (1,)), ((), ())), preferred_element_type=jnp.float32
        )
        > 0.5
    )
    diagonal = (q_index // BLK)[:, None] == (k_index // BLK)[None, :]
    causal = k_index[None, :] <= q_index[:, None]
    same_doc = q_doc[:, None] == k_doc[None, :]
    return causal & same_doc & (listed | diagonal)


def body(queries, keys, values, grad_out, doc_lengths, block_pairs, scale_index, scale_table):
    ctx_count = lax.axis_size("ctx")
    head_count = lax.axis_size("head")
    per_group = QH // KVH
    score_scale = 1.0 / math.sqrt(HD)
    q_mid, k_mid, v_mid, go_mid = (
        lax.all_to_all(queries, "head", split_axis=1, concat_axis=0, tiled=True),
        lax.all_to_all(keys, "head", split_axis=1, concat_axis=0, tiled=True),
        lax.all_to_all(values, "head", split_axis=1, concat_axis=0, tiled=True),
        lax.all_to_all(grad_out, "head", split_axis=1, concat_axis=0, tiled=True),
    )
    local_rows = q_mid.shape[0]
    kv_dev = k_mid.shape[1] // HD
    seq_len = local_rows * ctx_count
    k_full, v_full = (
        lax.all_gather(k_mid, "ctx", axis=0, tiled=True),
        lax.all_gather(v_mid, "ctx", axis=0, tiled=True),
    )
    offsets = jnp.arange(local_rows, dtype=jnp.int32)
    ctx_index = lax.axis_index("ctx")
    q_index = ctx_index * local_rows + offsets
    key_index = jnp.arange(seq_len, dtype=jnp.int32)
    key_doc, key_pos = doc_and_pos(key_index, doc_lengths)
    q_doc, q_pos = doc_and_pos(q_index, doc_lengths)
    block_count = seq_len // BLK
    blocks = jnp.arange(block_count, dtype=jnp.int32)
    pair_query = (block_pairs[:, 0:1] == blocks[None, :]).astype(jnp.bfloat16)
    pair_key = (block_pairs[:, 1:2] == blocks[None, :]).astype(jnp.bfloat16)
    listed = lax.dot_general(
        pair_query, pair_key, (((0,), (0,)), ((), ())), preferred_element_type=jnp.float32
    )
    row_hot = ((q_index // BLK)[:, None] == blocks[None, :]).astype(jnp.bfloat16)
    row_listed = jnp.dot(
        row_hot, listed.astype(jnp.bfloat16), preferred_element_type=jnp.float32
    ).astype(jnp.bfloat16)
    head_first = lax.axis_index("head") * kv_dev
    key_scale = jnp.repeat(
        lax.dynamic_slice_in_dim(block_scales(scale_index, scale_table, 0), head_first, kv_dev, 1),
        BLK,
        axis=0,
    )
    value_scale = jnp.repeat(
        lax.dynamic_slice_in_dim(block_scales(scale_index, scale_table, 1), head_first, kv_dev, 1),
        BLK,
        axis=0,
    )
    q_rot = rotate(
        q_mid.reshape(local_rows, kv_dev * per_group, HD).astype(jnp.float32), q_pos, 1.0
    )
    q_rot = q_rot.astype(jnp.bfloat16).reshape(local_rows, kv_dev, per_group, HD)
    k_rot = rotate(
        k_full.reshape(seq_len, kv_dev, HD).astype(jnp.float32) * key_scale[:, :, None],
        key_pos,
        1.0,
    ).astype(jnp.bfloat16)
    v_scaled = (
        v_full.reshape(seq_len, kv_dev, HD).astype(jnp.float32) * value_scale[:, :, None]
    ).astype(jnp.bfloat16)
    go_four = go_mid.reshape(local_rows, kv_dev, per_group, HD)
    key_width = math.gcd(seq_len, 512)
    key_count = seq_len // key_width
    key_blocks = (
        k_rot.reshape(key_count, key_width, kv_dev, HD),
        v_scaled.reshape(key_count, key_width, kv_dev, HD),
        key_index.reshape(key_count, key_width),
        key_doc.reshape(key_count, key_width),
    )

    def masked_scores(k_block, allowed):
        scores = (
            jnp.einsum("qjgd,kjd->jgqk", q_rot, k_block, preferred_element_type=jnp.float32)
            * score_scale
        )
        return jnp.where(allowed[None, None], scores, neg_big)

    def stats_step(running, key_block):
        k_block, v_block, k_idx, k_doc = key_block
        allowed = visible(q_index, q_doc, row_listed, k_idx, k_doc, blocks)

        def stats_compute(state_in):
            row_max, row_sum = state_in
            scores = masked_scores(k_block, allowed)
            new_max = jnp.maximum(row_max, jnp.max(scores, axis=-1))
            weights = jnp.where(allowed[None, None], jnp.exp(scores - new_max[..., None]), 0.0)
            return (new_max, row_sum * jnp.exp(row_max - new_max) + jnp.sum(weights, axis=-1))

        return (lax.cond(jnp.any(allowed), stats_compute, lambda state_in: state_in, running), None)

    start_max = jnp.full((kv_dev, per_group, local_rows), neg_big, jnp.float32)
    start_sum = jnp.zeros((kv_dev, per_group, local_rows), jnp.float32)
    (row_max, row_sum), _ = lax.scan(stats_step, (start_max, start_sum), key_blocks)
    lse = row_max + jnp.log(row_sum)

    def probs_of(k_block, allowed):
        scores = masked_scores(k_block, allowed)
        return jnp.where(allowed[None, None], jnp.exp(scores - lse[..., None]), 0.0)

    def out_step(accum, key_block):
        k_block, v_block, k_idx, k_doc = key_block
        allowed = visible(q_index, q_doc, row_listed, k_idx, k_doc, blocks)

        def out_compute(accum_in):
            probs_b = probs_of(k_block, allowed).astype(jnp.bfloat16)
            return accum_in + jnp.einsum(
                "jgqk,kjd->qjgd", probs_b, v_block, preferred_element_type=jnp.float32
            )

        return (lax.cond(jnp.any(allowed), out_compute, lambda accum_in: accum_in, accum), None)

    zero_rows = jnp.zeros((local_rows, kv_dev, per_group, HD), jnp.float32)
    out_accum, _ = lax.scan(out_step, zero_rows, key_blocks)
    out_four = out_accum.astype(jnp.bfloat16)
    delta = jnp.einsum("qjgd,qjgd->jgq", go_four, out_four, preferred_element_type=jnp.float32)

    def grad_step(accum, key_block):
        k_block, v_block, k_idx, k_doc = key_block
        allowed = visible(q_index, q_doc, row_listed, k_idx, k_doc, blocks)

        def grad_compute(accum_in):
            probs = probs_of(k_block, allowed)
            grad_probs = jnp.einsum(
                "qjgd,kjd->jgqk", go_four, v_block, preferred_element_type=jnp.float32
            )
            grad_scores = probs * (grad_probs - delta[..., None])
            probs_b = probs.astype(jnp.bfloat16)
            grad_sb = grad_scores.astype(jnp.bfloat16)
            dv_block = jnp.einsum(
                "jgqk,qjgd->kjd", probs_b, go_four, preferred_element_type=jnp.float32
            )
            dk_block = (
                jnp.einsum("jgqk,qjgd->kjd", grad_sb, q_rot, preferred_element_type=jnp.float32)
                * score_scale
            )
            accum_out = (
                accum_in
                + jnp.einsum("jgqk,kjd->qjgd", grad_sb, k_block, preferred_element_type=jnp.float32)
                * score_scale
            )
            return (accum_out, jnp.stack([dk_block, dv_block], axis=1))

        def passing(accum_in):
            return (accum_in, jnp.zeros((key_width, 2, kv_dev, HD), jnp.float32))

        return lax.cond(jnp.any(allowed), grad_compute, passing, accum)

    dq_accum, key_terms = lax.scan(grad_step, zero_rows, key_blocks)
    key_terms = key_terms.reshape(seq_len, 2, kv_dev, HD)
    key_part = key_scale[:, :, None] * rotate(key_terms[:, 0], key_pos, -1.0)
    value_part = value_scale[:, :, None] * key_terms[:, 1]
    term_width = 2 * kv_dev * HD
    terms = jnp.stack([key_part, value_part], axis=1).reshape(seq_len, term_width)
    dq_mid = rotate(dq_accum.reshape(local_rows, kv_dev * per_group, HD), q_pos, -1.0).astype(
        jnp.bfloat16
    )
    dq_mid = dq_mid.reshape(local_rows, kv_dev * per_group * HD)
    out_mid = out_four.reshape(local_rows, kv_dev * per_group * HD)
    entry_rows = local_rows // head_count
    summed = lax.psum_scatter(terms, "ctx", scatter_dimension=0, tiled=True).astype(jnp.bfloat16)
    out_back, dq_back, kv_back = (
        lax.all_to_all(out_mid, "head", split_axis=0, concat_axis=1, tiled=True),
        lax.all_to_all(dq_mid, "head", split_axis=0, concat_axis=1, tiled=True),
        lax.all_to_all(summed, "head", split_axis=0, concat_axis=1, tiled=True),
    )
    kv_back = kv_back.reshape(entry_rows, head_count, 2, kv_dev, HD)
    grad_keys = kv_back[:, :, 0].reshape(entry_rows, head_count * kv_dev * HD)
    grad_values = kv_back[:, :, 1].reshape(entry_rows, head_count * kv_dev * HD)
    return (out_back, dq_back, grad_keys, grad_values)


def solution(mesh):
    in_specs = (
        P(("ctx", "head"), None),
        P(("ctx", "head"), None),
        P(("ctx", "head"), None),
        P(("ctx", "head"), None),
        P(),
        P(),
        P(),
        P(),
    )
    out_specs = (
        P(("ctx", "head"), None),
        P(("ctx", "head"), None),
        P(("ctx", "head"), None),
        P(("ctx", "head"), None),
    )
    return jax.shard_map(body, mesh=mesh, in_specs=in_specs, out_specs=out_specs, check_vma=False)
```

profile of v0, /device:TPU:1, one launch (start us, length us, event | category | flops | bytes accessed | tf_op | source)
XLA Modules:
  0.0 388.4 jit_solution(8030466777180596732)
XLA Ops:
  8.6 9.0 %all-to-all-start = ((bf16[16,8,128]{2,0,1:T(8,128)(2,1)}), bf16[16,8,128]{2,0,1:T(8,128)(2,1)S(1)}, u32[]{:S(2)}, u32[]{:S(2)}) async-start(bf16[16,8,128]{2,0,1:T(8,128)(2,1)} %copy_bitcast_fusion.6), calls=%async_computation | async-start | bytes 65536 | tf_op jit(solution)/shard_map/all_to_all | solution.py:70
  17.6 1.4 copy_bitcast_fusion.5
  19.8 4.7 %all-to-all-done = bf16[16,8,128]{2,0,1:T(8,128)(2,1)S(1)} async-done(((bf16[16,8,128]{2,0,1:T(8,128)(2,1)}), bf16[16,8,128]{2,0,1:T(8,128)(2,1)S(1)}, u32[]{:S(2)}, u32[]{:S(2)}) %all-to-all-start) | async-done | bytes 32800 | tf_op jit(solution)/shard_map/all_to_all | solution.py:70
  24.4 3.3 all-to-all-start.1
  32.0 1.9 copy.202
  34.6 5.8 %all-to-all-start.2 = ((bf16[16,8,2048]{2,0,1:T(8,128)(2,1)}), bf16[16,8,2048]{2,0,1:T(8,128)(2,1)S(1)}, u32[]{:S(2)}, u32[]{:S(2)}) async-start(bf16[16,8,2048]{2,0,1:T(8,128)(2,1)} %bitcast.349), calls=%async_computation.2 | async-start | bytes 1048576 | tf_op jit(solution)/shard_map/all_to_all | solution.py:68
  41.9 13.2 %all-to-all-done.2 = bf16[16,8,2048]{2,0,1:T(8,128)(2,1)S(1)} async-done(((bf16[16,8,2048]{2,0,1:T(8,128)(2,1)}), bf16[16,8,2048]{2,0,1:T(8,128)(2,1)S(1)}, u32[]{:S(2)}, u32[]{:S(2)}) %all-to-all-start.2) | async-done | bytes 524320 | tf_op jit(solution)/shard_map/all_to_all | solution.py:68
  55.1 3.5 all-to-all-start.4
  60.3 12.2 %all-to-all-done.4 = bf16[16,8,2048]{2,0,1:T(8,128)(2,1)S(1)} async-done(((bf16[16,8,2048]{2,0,1:T(8,128)(2,1)}), bf16[16,8,2048]{2,0,1:T(8,128)(2,1)S(1)}, u32[]{:S(2)}, u32[]{:S(2)}) %all-to-all-start.4) | async-done | bytes 524320 | tf_op jit(solution)/shard_map/all_to_all | solution.py:71
  73.6 9.5 %all-gather.3.cloned.1.call-done = bf16[4096,128]{1,0:T(8,128)(2,1)} async-done(((bf16[128,128]{1,0:T(8,128)(2,1)}), bf16[4096,128]{1,0:T(8,128)(2,1)}) %all-gather.3.cloned.1.call-update) | async-done | bytes 1048592 | tf_op jit(solution)/shard_map/all_gather | solution.py:78
  83.1 1.7 multiply_convert_fusion
  84.8 1.3 copy.152
  86.2 47.2 %all-gather.5.cloned.1.call-done = bf16[4096,128]{1,0:T(8,128)(2,1)} async-done(((bf16[128,128]{1,0:T(8,128)(2,1)}), bf16[4096,128]{1,0:T(8,128)(2,1)}) %all-gather.5.cloned.1.call-update) | async-done | bytes 1048592 | tf_op jit(solution)/shard_map/all_gather | solution.py:77
  133.4 1.8 multiply_bitcast_fusion
  135.2 8.9 %fusion.142 = (bf16[4096,1,64]{2,0,1:T(8,128)(2,1)S(1)}, bf16[4096,1,64]{2,0,1:T(8,128)(2,1)S(1)}) fusion(f32[4096,1,128]{2,0,1:T(8,128)S(1)} %multiply_bitcast_fusion, f32[64]{0:T(128)S(1)} %multiply_exponential_fusion, f32[4096]{0:T(1024)S(1)} %subtract_convert_fusion.2), kind=kLoop, calls=%fused_computation.176 | loop fusion | flops 2359296 | bytes 3162368 | tf_op jit(solution)/shard_map/convert.11
  144.8 15.6 %while.55 = (s32[]{:T(128)}, f32[1,16,128]{2,1,0:T(8,128)S(1)}, f32[1,16,128]{2,1,0:T(8,128)S(1)}, s32[8,512]{1,0:T(8,128)S(1)}, s32[128]{0:T(128)S(1)}, /*index...) while((s32[]{:T(128)}, f32[1,16,128]{2,1,0:T(8,128)S(1)}, ...), condition=%wide.region_13.14_spmd.clone.clone, body=%wide.region_7.13_spmd.clone.clone.sunk | while | flops 281580672 | bytes 9380575 | solution.py:152
  144.9 1.0 fusion.175
  146.5 1.8 conditional.12
  147.3 1.0 select_reduce_fusion
  148.4 1.0 fusion.175
  150.1 1.0 fusion.175
  151.8 1.0 fusion.175
  153.6 1.0 fusion.175
  155.3 1.0 fusion.175
  158.7 1.0 fusion.175
  160.5 21.4 %while.56 = (s32[]{:T(128)}, f32[128,1,16,128]{0,3,2,1:T(8,128)S(1)}, s32[8,512]{1,0:T(8,128)S(1)}, s32[128]{0:T(128)S(1)}, s32[8,512]{1,0:T(8,128)S(1)}, /*inde...) while((s32[]{:T(128)}, ...), condition=%wide.region_18.19_spmd.clone.clone, body=%wide.region_14.18_spmd.clone.clone.sunk | while | flops 547128448 | bytes 3057355 | solution.py:172
  160.6 1.6 fusion.178
  162.9 2.5 conditional.13
  162.9 2.5 fusion.39
  165.5 1.6 fusion.178
  167.8 1.6 fusion.178
  170.2 1.6 fusion.178
  172.6 1.6 fusion.178
  174.9 1.6 fusion.178
  177.3 1.6 fusion.178
  179.6 1.6 fusion.178
  181.9 1.3 bitcast_convert_fusion
  183.2 1.7 copy.176
  185.5 31.7 %while.57 = (s32[]{:T(128)}, f32[128,1,16,128]{0,3,2,1:T(8,128)S(1)}, f32[8,512,2,1,128]{4,1,0,2,3:T(8,128)}, s32[8,512]{1,0:T(8,128)S(1)}, s32[128]{0:T(128)S(1...) while((s32[]{:T(128)}, ...), condition=%wide.region_23.24_spmd.clone.clone, body=%wide.region_19.23_spmd.clone.clone.sunk | while | flops 1360233600 | bytes 28698428 | solution.py:207
  185.7 1.6 fusion.181
  188.0 5.8 %conditional.14 = (f32[128,1,16,128]{0,3,2,1:T(8,128)S(1)}, f32[1,512,2,1,128]{4,1,2,3,0:T(8,128)S(1)}) conditional(s32[]{:T(128)} %convert_element_type.181, f32[128,1,16,128]{0,3,2,1:T(8,128)S(1)} %get-tuple-element.1726, (bf16[8,512,1,128]{3,1,2,0:T(8,128)(2,1)S(1)}, s32[]{:T(128)}, pred[128,512]{0,1:T(8,128)(4,1)}, ...), branch_computations={%region_21.21_spmd, %region_22.22_spmd} | conditional | flops 1355481088 | bytes 27550288 | solution.py:205
  189.1 1.0 fusion.78
  190.1 2.5 fusion.56
  194.7 1.6 fusion.181
  198.0 1.6 fusion.181
  201.2 1.6 fusion.181
  204.4 1.6 fusion.181
  207.6 1.6 fusion.181
  210.8 1.6 fusion.181
  214.0 1.6 fusion.181
  217.2 2.1 slice_multiply_fusion
  220.1 8.2 %fusion.138 = (f32[4096,1,1,64]{3,0,1,2:T(8,128)S(1)}, f32[4096,1,1,64]{3,0,1,2:T(8,128)S(1)}) fusion(f32[4096,1,128]{2,0,1:T(8,128)S(1)} %slice_bitcast_fusion, f32[64]{0:T(128)S(1)} %multiply_exponential_fusion, f32[4096]{0:T(1024)S(1)} %subtract_convert_fusion.2), kind=kLoop, calls=%fused_computation.172 | loop fusion | flops 2097152 | bytes 4210944 | tf_op jit(solution)/shard_map/concatenate | solution.py:28
  228.3 1.3 maximum_multiply_fusion
  229.6 2.3 pad_maximum_fusion
  231.9 5.6 %copy.165 = f32[4096,2,1,128]{0,3,1,2:T(8,128)} copy(f32[4096,2,1,128]{3,0,1,2:T(8,128)} %pad_maximum_fusion) | data formatting | bytes 8388608 | tf_op jit(solution)/shard_map/stack | solution.py:212
  237.5 1.0 copy-done.3
  239.0 1.0 all_to_all.98
  240.0 6.7 %all-to-all-start.3 = ((bf16[8,16,2048]{2,1,0:T(8,128)(2,1)}), bf16[8,16,2048]{2,1,0:T(8,128)(2,1)S(1)}, u32[]{:S(2)}, u32[]{:S(2)}) async-start(bf16[8,16,2048]{2,1,0:T(8,128)(2,1)} %all_to_all.98), calls=%async_computation.3 | async-start | bytes 1048576 | tf_op jit(solution)/shard_map/all_to_all | solution.py:221
  248.0 1.0 convert_element_type.136
  249.0 15.6 %all-to-all-done.3 = bf16[8,16,2048]{2,1,0:T(8,128)(2,1)S(1)} async-done(((bf16[8,16,2048]{2,1,0:T(8,128)(2,1)}), bf16[8,16,2048]{2,1,0:T(8,128)(2,1)S(1)}, u32[]{:S(2)}, u32[]{:S(2)}) %all-to-all-start.3) | async-done | bytes 524320 | tf_op jit(solution)/shard_map/all_to_all | solution.py:221
  264.7 3.5 all-to-all-start.5
  268.2 96.8 %reduce-scatter.2.cloned.1.call-done = f32[128,256]{0,1:T(8,128)} async-done(((f32[4096,256]{0,1:T(8,128)}), f32[128,256]{0,1:T(8,128)}) %reduce-scatter.2.cloned.1.call-update) | async-done | bytes 131088 | tf_op jit(solution)/shard_map/reduce_scatter | solution.py:219
  366.7 6.7 %all-to-all-start.6 = ((bf16[8,16,256]{2,1,0:T(8,128)(2,1)}), bf16[8,16,256]{2,1,0:T(8,128)(2,1)S(1)}, u32[]{:S(2)}, u32[]{:S(2)}) async-start(bf16[8,16,256]{2,1,0:T(8,128)(2,1)} %bitcast.88), calls=%async_computation.7 | async-start | bytes 131072 | tf_op jit(solution)/shard_map/all_to_all | solution.py:223
  375.0 5.6 %all-to-all-done.6 = bf16[8,16,256]{2,1,0:T(8,128)(2,1)S(1)} async-done(((bf16[8,16,256]{2,1,0:T(8,128)(2,1)}), bf16[8,16,256]{2,1,0:T(8,128)(2,1)S(1)}, u32[]{:S(2)}, u32[]{:S(2)}) %all-to-all-start.6) | async-done | bytes 65568 | tf_op jit(solution)/shard_map/all_to_all | solution.py:223
  (195 shorter events, 32.2 us)
Async XLA Ops:
  7.2 0.8 copy-start
  7.2 33.3 %copy-start.8 = (s32[8]{0:T(128)S(1)}, s32[8]{0:T(128)}, u32[]{:S(2)}) copy-start(s32[8]{0:T(128)} %param.24) | copy-start | bytes 100
  7.9 32.8 %copy-start.4 = (bf16[16,16384]{1,0:T(8,128)(2,1)S(1)}, bf16[16,16384]{1,0:T(8,128)(2,1)}, u32[]{:S(2)}) copy-start(bf16[16,16384]{1,0:T(8,128)(2,1)} %param.23) | copy-start | bytes 1572868
  8.6 15.9 %all-to-all-start = ((bf16[16,8,128]{2,0,1:T(8,128)(2,1)}), bf16[16,8,128]{2,0,1:T(8,128)(2,1)S(1)}, u32[]{:S(2)}, u32[]{:S(2)}) async-start(bf16[16,8,128]{2,0,1:T(8,128)(2,1)} %copy_bitcast_fusion.6), calls=%async_computation | async-start | bytes 65536 | tf_op jit(solution)/shard_map/all_to_all | solution.py:70
  24.4 3.4 copy-start.6
  24.4 10.1 %all-to-all-start.1 = ((bf16[16,8,128]{2,0,1:T(8,128)(2,1)}), bf16[16,8,128]{2,0,1:T(8,128)(2,1)S(1)}, u32[]{:S(2)}, u32[]{:S(2)}) async-start(bf16[16,8,128]{2,0,1:T(8,128)(2,1)} %copy_bitcast_fusion.5), calls=%async_computation.1 | async-start | bytes 65536 | tf_op jit(solution)/shard_map/all_to_all | solution.py:69
  27.8 55.3 %all-gather.3.cloned.1.call-start = ((), (), s32[]{:S(2)}) async-start(), calls=%async_computation.8 | async-start | bytes 1081344 | tf_op jit(solution)/shard_map/all_gather | solution.py:78
  34.6 7.3 %copy-start.7 = (bf16[16,8,128]{2,0,1:T(8,128)(2,1)}, bf16[16,8,128]{2,0,1:T(8,128)(2,1)S(1)}, u32[]{:S(2)}) copy-start(bf16[16,8,128]{2,0,1:T(8,128)(2,1)S(1)} %all-to-all-done.1) | copy-start | bytes 98308
  34.6 20.5 %all-to-all-start.2 = ((bf16[16,8,2048]{2,0,1:T(8,128)(2,1)}), bf16[16,8,2048]{2,0,1:T(8,128)(2,1)S(1)}, u32[]{:S(2)}, u32[]{:S(2)}) async-start(bf16[16,8,2048]{2,0,1:T(8,128)(2,1)} %bitcast.349), calls=%async_computation.2 | async-start | bytes 1048576 | tf_op jit(solution)/shard_map/all_to_all | solution.py:68
  40.4 93.0 %all-gather.5.cloned.1.call-start = ((), (), s32[]{:S(2)}) async-start(), calls=%async_computation.9 | async-start | bytes 1081344 | tf_op jit(solution)/shard_map/all_gather | solution.py:77
  55.1 17.4 %all-to-all-start.4 = ((bf16[16,8,2048]{2,0,1:T(8,128)(2,1)}), bf16[16,8,2048]{2,0,1:T(8,128)(2,1)S(1)}, u32[]{:S(2)}, u32[]{:S(2)}) async-start(bf16[16,8,2048]{2,0,1:T(8,128)(2,1)} %bitcast.348), calls=%async_computation.4 | async-start | bytes 1048576 | tf_op jit(solution)/shard_map/all_to_all | solution.py:71
  58.6 306.4 %reduce-scatter.2.cloned.1.call-start = ((), (), s32[]{:S(2)}) async-start(), calls=%async_computation.10 | async-start | bytes 4325376 | tf_op jit(solution)/shard_map/reduce_scatter | solution.py:219
  84.8 50.4 %copy-start.2 = (bf16[4096,128]{1,0:T(8,128)(2,1)}, bf16[4096,128]{1,0:T(8,128)(2,1)S(1)}, u32[]{:S(2)}) copy-start(bf16[4096,128]{1,0:T(8,128)(2,1)S(1)} %multiply_convert_fusion) | copy-start | bytes 3145732
  188.0 1.0 copy-start.5
  188.0 1.0 copy-start.9
  217.2 2.8 copy-start.1
  237.5 1.0 copy-start.3
  240.0 24.7 %all-to-all-start.3 = ((bf16[8,16,2048]{2,1,0:T(8,128)(2,1)}), bf16[8,16,2048]{2,1,0:T(8,128)(2,1)S(1)}, u32[]{:S(2)}, u32[]{:S(2)}) async-start(bf16[8,16,2048]{2,1,0:T(8,128)(2,1)} %all_to_all.98), calls=%async_computation.3 | async-start | bytes 1048576 | tf_op jit(solution)/shard_map/all_to_all | solution.py:221
  264.7 102.0 %all-to-all-start.5 = ((bf16[8,16,2048]{2,1,0:T(8,128)(2,1)}), bf16[8,16,2048]{2,1,0:T(8,128)(2,1)S(1)}, u32[]{:S(2)}, u32[]{:S(2)}) async-start(bf16[8,16,2048]{2,1,0:T(8,128)(2,1)} %convert_element_type.136), calls=%async_computation.5 | async-start | bytes 1048576 | tf_op jit(solution)/shard_map/all_to_all | solution.py:222
  366.7 14.0 %all-to-all-start.6 = ((bf16[8,16,256]{2,1,0:T(8,128)(2,1)}), bf16[8,16,256]{2,1,0:T(8,128)(2,1)S(1)}, u32[]{:S(2)}, u32[]{:S(2)}) async-start(bf16[8,16,256]{2,1,0:T(8,128)(2,1)} %bitcast.88), calls=%async_computation.7 | async-start | bytes 131072 | tf_op jit(solution)/shard_map/all_to_all | solution.py:223
Sparse Core Ops, SparseCore 0:
  31.8 51.2 all-gather.2
  86.2 47.1 all-gather.4
  237.6 127.3 reduce-scatter.1
where the time goes:
time: 391 us; the launch traced here: 388 us
  waiting for transfers between devices  206 us (53%)
  matrix products  42.5 us (11%)
  starting transfers between devices  38.7 us (10%)
  other arithmetic  35.4 us (9%)
  local copies, waits for them, and re-layouts  34.1 us (9%)
  loops' own time  17.2 us (4%)
  between operations  14.1 us (4%)
    reduce_scatter x1, waiting for transfers between devices, body(): lax.psum_scatter(terms, 'ctx', scatter_dimension=0, tiled=True)  96.8 us
    all_gather x1, waiting for transfers between devices, body(): lax.all_gather(k_mid, 'ctx', axis=0, tiled=True)  47.2 us
    dot_general x24, matrix products, visible(): lax.dot_general(row_listed, key_hot, (((1,), (1,)), ((), ())), preferred_...  33.4 us
    all_to_all x1, waiting for transfers between devices, body(): lax.all_to_all(out_mid, 'head', split_axis=0, concat_axis=1, tiled=True)  15.6 us
    all_to_all x1, waiting for transfers between devices, body(): lax.all_to_all(queries, 'head', split_axis=1, concat_axis=0, tiled=True)  13.2 us
    all_to_all x1, waiting for transfers between devices, body(): lax.all_to_all(grad_out, 'head', split_axis=1, concat_axis=0, tiled=True)  12.2 us
    another operation x3, other arithmetic  10.2 us
    concatenate x5, other arithmetic, rotate(): jnp.concatenate([first_half * cosine - second * sine_part, second * cosin...  9.89 us
  transfers between devices with their start and end apart: 10, of which 9 were waited for; matrix products, arithmetic and copies ran while one was open for 5% of the time, Pallas kernels for 0%

commit v1 on v0

v1 whole, which is shorter than its diff:
```python
import functools
import math

import jax
import jax.numpy as jnp
import numpy as np
from jax import lax
from jax.experimental import pallas as pl
from jax.experimental.pallas import tpu as pltpu
from jax.sharding import PartitionSpec as P

HD = 128
BLK = 128
ROWS = 16
GRP = 16
NX, NY, NC, NZ = 4, 4, 2, 8
NP = NX * NC
NBLK = 32
NDOC = 8
WIDE = GRP * HD
NEG = -1e30
SCALE = 1.0 / math.sqrt(HD)
EXP2_SCALE = SCALE * math.log2(math.e)
MESH = pl.DeviceIdType.MESH
BF = jnp.bfloat16
F32 = jnp.float32
VMEM_LIMIT = 56 * 1024 * 1024


def place():
    ctx = lax.axis_index("ctx")
    return ctx // (NY * NC), (ctx // NC) % NY, ctx % NC, lax.axis_index("head")


def device(xx, yy, cc, zz):
    return {"ctx": xx * (NY * NC) + yy * NC + cc, "head": zz}


def peer(p, y, z):
    return device(p // NC, y, p % NC, z)


def remote(src, dst, send_sem, recv_sem, dev):
    return pltpu.make_async_remote_copy(
        src_ref=src, dst_ref=dst, send_sem=send_sem, recv_sem=recv_sem, device_id=dev, device_id_type=MESH
    )


def enter(me, y, z, x, c):
    barrier = pltpu.get_barrier_semaphore()
    for d in range(1, NP):
        pl.semaphore_signal(barrier, inc=1, device_id=peer((me + d) % NP, y, z), device_id_type=MESH)
    for d in range(1, NY):
        pl.semaphore_signal(barrier, inc=1, device_id=device(x, (y + d) % NY, c, z), device_id_type=MESH)
    for d in (1, NZ - 1):
        pl.semaphore_signal(barrier, inc=1, device_id=device(x, y, c, (z + d) % NZ), device_id_type=MESH)
    return barrier


N_PARTNERS = NP - 1 + NY - 1 + 2


def turn(x, cosine, sine):
    return x * cosine + pltpu.roll(x, HD // 2, 1) * sine


def gather_kernel(
    q_ref, k_ref, v_ref, go_ref, doc_ref, pairs_ref, sidx_ref, stab_ref, freq_ref,
    qx_ref, gox_ref, ka_ref, va_ref, lists_ref, cs_ref,
    qs, ks, vs,
    q_s, q_r, go_s, go_r, k_s, k_r, v_s, v_r, ky_s, ky_r, kzr_s, kzr_r, kzl_s, kzl_r,
    vzr_s, vzr_r, vzl_s, vzl_r, vy_s, vy_r, own_s,
):
    x, y, c, z = place()
    me = NC * x + c
    block = lax.axis_index("ctx")
    barrier = enter(me, y, z, x, c)

    token = BLK * block + ROWS * z + lax.broadcasted_iota(jnp.int32, (ROWS, HD), 0)
    start = jnp.zeros((ROWS, HD), jnp.int32)
    end = 0
    for d in range(NDOC):
        end = end + doc_ref[d]
        start = start + jnp.where(token >= end, doc_ref[d], 0)
    angle = (token - start).astype(F32) * freq_ref[0:1, :]
    cosine = jnp.cos(angle)
    sine = jnp.sin(angle)
    sine = jnp.where(lax.broadcasted_iota(jnp.int32, (ROWS, HD), 1) < HD // 2, -sine, sine)
    cs_ref[0] = cosine
    cs_ref[1] = sine

    for h in range(NP):
        cols = slice(h * HD, (h + 1) * HD)
        key_scale = stab_ref[0, sidx_ref[0, block, h]]
        value_scale = stab_ref[1, sidx_ref[1, block, h]]
        ks[h] = turn(k_ref[:, cols].astype(F32) * key_scale, cosine, sine).astype(BF)
        vs[h] = (v_ref[:, cols].astype(F32) * value_scale).astype(BF)

    pl.semaphore_wait(barrier, N_PARTNERS)

    def kv_copies(p):
        return (
            remote(ks.at[p], ka_ref.at[z, y, me], k_s.at[p], k_r.at[me], peer(p, y, z)),
            remote(vs.at[p], va_ref.at[y, z, me], v_s.at[p], v_r.at[me], peer(p, y, z)),
        )

    def kv_arrivals(p):
        return (
            remote(ks.at[p], ka_ref.at[z, y, p], k_s.at[p], k_r.at[p], peer(p, y, z)),
            remote(vs.at[p], va_ref.at[y, z, p], v_s.at[p], v_r.at[p], peer(p, y, z)),
        )

    def go_cols(p):
        return go_ref.at[:, pl.ds(pl.multiple_of(p * WIDE, WIDE), WIDE)]

    def go_copy(p, slot):
        return remote(go_cols(p), gox_ref.at[slot], go_s.at[p], go_r.at[slot], peer(p, y, z))

    def q_copy(p, slot):
        return remote(qs.at[p], qx_ref.at[slot], q_s.at[p], q_r.at[slot], peer(p, y, z))

    def each_peer(fn):
        def step(d, carry):
            fn((me + d) % NP)
            return carry

        lax.fori_loop(1, NP, step, 0)

    def start_kv(p):
        for copy in kv_copies(p):
            copy.start()

    each_peer(start_kv)
    each_peer(lambda p: go_copy(p, me).start())
    own_go = pltpu.make_async_copy(go_cols(me), gox_ref.at[me], own_s)
    own_go.start()
    ka_ref[z, y, me] = ks[me]
    va_ref[y, z, me] = vs[me]

    def rotate_q(p):
        for h in range(GRP):
            cols = pl.ds(pl.multiple_of(p * WIDE + h * HD, HD), HD)
            qs[p, :, h * HD:(h + 1) * HD] = turn(q_ref[:, cols].astype(F32), cosine, sine).astype(BF)

    def rotate_and_send(p):
        rotate_q(p)
        q_copy(p, me).start()

    each_peer(rotate_and_send)
    rotate_q(me)
    qx_ref[me] = qs[me]

    right, left = (z + 1) % NZ, (z + NZ - 1) % NZ
    to_right, to_left = device(x, y, c, right), device(x, y, c, left)

    def k_ring(s, sending):
        zr, zl = ((z + NZ - s) % NZ, (z + s) % NZ) if sending else ((z + NZ - s - 1) % NZ, (z + s + 1) % NZ)
        if s < 3:
            ref_r, ref_l = ka_ref.at[zr], ka_ref.at[zl]
        else:
            ref_r, ref_l = ka_ref.at[zr, pl.ds(0, NY // 2)], ka_ref.at[zl, pl.ds(NY // 2, NY // 2)]
        return (
            remote(ref_r, ref_r, kzr_s.at[s], kzr_r.at[s], to_right),
            remote(ref_l, ref_l, kzl_s.at[s], kzl_r.at[s], to_left),
        )

    def v_ring(s, sending):
        zr, zl = ((z + NZ - s) % NZ, (z + s) % NZ) if sending else ((z + NZ - s - 1) % NZ, (z + s + 1) % NZ)
        if s < 3:
            ref_r, ref_l = va_ref.at[y, zr], va_ref.at[y, zl]
        else:
            ref_r, ref_l = va_ref.at[y, zr, pl.ds(0, NP // 2)], va_ref.at[y, zl, pl.ds(NP // 2, NP // 2)]
        return (
            remote(ref_r, ref_r, vzr_s.at[s], vzr_r.at[s], to_right),
            remote(ref_l, ref_l, vzl_s.at[s], vzl_r.at[s], to_left),
        )

    def v_spread(zz):
        for d in (2, 1, 3):
            remote(
                va_ref.at[y, zz], va_ref.at[y, zz], vy_s.at[d, zz], vy_r.at[y, zz], device(x, (y + d) % NY, c, z)
            ).start()

    def k_spread(d, yy):
        ref = ka_ref.at[z, yy]
        return remote(ref, ref, ky_s.at[d], ky_r.at[yy], device(x, (y + d) % NY, c, z))

    def begin(pair):
        for copy in pair:
            copy.start()

    def arrive(pair):
        for copy in pair:
            copy.wait_recv()

    each_peer(lambda p: arrive(kv_arrivals(p)))
    begin(v_ring(0, True))
    for d in (2, 1, 3):
        k_spread(d, y).start()
    v_spread(z)

    lane = lax.broadcasted_iota(jnp.int32, (NP, BLK), 1)
    row = lax.broadcasted_iota(jnp.int32, (NP, BLK), 0)
    own_block = NY * NC * (row // NC) + NC * y + row % NC
    first = BLK * own_block + ROWS * z
    doc_start = jnp.zeros((NP, BLK), jnp.int32)
    end = 0
    for d in range(NDOC):
        end = end + doc_ref[d]
        doc_start = doc_start + jnp.where(first >= end, doc_ref[d], 0)
    pairs = pairs_ref[...]
    pair_lane = lax.broadcasted_iota(jnp.int32, (pairs.shape[0], BLK), 1)
    lane_block = jnp.where(pair_lane < NP, NY * NC * (pair_lane // NC) + NC * y + pair_lane % NC, -1)
    pair_q = (pairs[:, 0:1] == lane_block).astype(F32)
    pair_k = (pairs[:, 1:2] == pair_lane).astype(F32)
    listed = lax.dot_general(pair_q, pair_k, (((0,), (0,)), ((), ())), preferred_element_type=F32)[:NP]
    wanted = ((listed > 0.5) | (lane == own_block)) & (BLK * lane + BLK - 1 >= doc_start) & (lane <= own_block)
    wanted_f = wanted.astype(F32)
    upper = (
        lax.broadcasted_iota(jnp.int32, (BLK, BLK), 0) <= lax.broadcasted_iota(jnp.int32, (BLK, BLK), 1)
    ).astype(F32)
    rank = jnp.dot(wanted_f, upper, preferred_element_type=F32)
    lane_f = lane.astype(F32)

    def list_step(r, out):
        hit = wanted & (rank.astype(jnp.int32) == r + 1)
        entry = jnp.sum(jnp.where(hit, lane_f, 0.0), axis=1, keepdims=True)
        return jnp.where(lane == r, entry, out)

    out = lax.fori_loop(0, NBLK, list_step, jnp.zeros((NP, BLK), F32))
    out = jnp.where(lane == BLK - 1, jnp.sum(wanted_f, axis=1, keepdims=True), out)
    lists_ref[...] = out.astype(jnp.int32)

    def v_step(s):
        arrive(v_ring(s - 1, False))
        if s < 4:
            begin(v_ring(s, True))
            v_spread((z + NZ - s) % NZ)
            v_spread((z + s) % NZ)
        else:
            v_spread((z + 4) % NZ)

    def k_step(s):
        arrive(k_ring(s - 1, False))
        if s < 4:
            begin(k_ring(s, True))

    v_step(1)
    for d in range(1, NY):
        k_spread(d, (y + d) % NY).wait_recv()
    begin(k_ring(0, True))
    v_step(2)
    v_step(3)
    k_step(1)
    v_step(4)
    k_step(2)
    k_step(3)
    k_step(4)

    def spread_in(zz, carry):
        for d in range(1, NY):
            yy = (y + d) % NY
            remote(
                va_ref.at[yy, zz], va_ref.at[yy, zz], vy_s.at[d, zz], vy_r.at[yy, zz], device(x, yy, c, z)
            ).wait_recv()
        return carry

    lax.fori_loop(0, NZ, spread_in, 0)

    def qgo_in(p):
        go_copy(p, p).wait_recv()
        q_copy(p, p).wait_recv()

    each_peer(qgo_in)
    own_go.wait()

    def sent(p):
        for copy in kv_copies(p):
            copy.wait_send()
        go_copy(p, me).wait_send()
        q_copy(p, me).wait_send()

    each_peer(sent)
    for d in range(1, NY):
        k_spread(d, y).wait_send()
    for s in range(4):
        for copy in k_ring(s, True) + v_ring(s, True):
            copy.wait_send()

    def spread_sent(zz, carry):
        for d in range(1, NY):
            remote(
                va_ref.at[y, zz], va_ref.at[y, zz], vy_s.at[d, zz], vy_r.at[y, zz], device(x, (y + d) % NY, c, z)
            ).wait_send()
        return carry

    lax.fori_loop(0, NZ, spread_sent, 0)


def heads_to_rows(ref, i):
    return jnp.concatenate([ref[i, :, h * HD:(h + 1) * HD] for h in range(GRP)], axis=0)


def rows_to_heads(ref, i, rows):
    for h in range(GRP):
        ref[i, :, h * HD:(h + 1) * HD] = rows[h * ROWS:(h + 1) * ROWS]


def attend_kernel(
    lists_ref, doc_ref, q_ref, go_ref, k_ref, v_ref, o_ref, dq_ref, dk_ref, dv_ref, s_ref, dk_acc, dv_acc
):
    _, y, _, z = place()
    rows = GRP * ROWS
    dk_acc[...] = jnp.zeros_like(dk_acc)
    dv_acc[...] = jnp.zeros_like(dv_acc)
    key_row = lax.broadcasted_iota(jnp.int32, (BLK, rows), 0)
    lane = lax.broadcasted_iota(jnp.int32, (1, rows), 1)
    nt = (((1,), (1,)), ((), ()))
    tn = (((0,), (0,)), ((), ()))

    def group(i, carry):
        own = NY * NC * (i // NC) + NC * y + i % NC
        count = lists_ref[i, BLK - 1]
        queries = heads_to_rows(q_ref, i)
        grads = heads_to_rows(go_ref, i)
        token = BLK * own + ROWS * z + lane % ROWS
        start = jnp.zeros((1, rows), jnp.int32)
        end = 0
        for d in range(NDOC):
            end = end + doc_ref[d]
            start = start + jnp.where(token >= end, doc_ref[d], 0)

        def spot(t):
            b = lists_ref[i, t]
            return b, (b // NC) % NY, (b // (NY * NC)) * NC + b % NC

        def keys_at(yb, ib):
            return k_ref[:, yb, ib].reshape(BLK, HD)

        def values_at(yb, ib):
            return v_ref[yb, :, ib].reshape(BLK, HD)

        def score_step(t, top):
            b, yb, ib = spot(t)
            scores = lax.dot_general(keys_at(yb, ib), queries, nt, preferred_element_type=F32)
            allowed = (key_row >= start - BLK * b) & (key_row <= token - BLK * b)
            scores = jnp.where(allowed, scores, NEG)
            s_ref[t] = scores
            return jnp.maximum(top, jnp.max(scores.reshape(BLK // 8, 8, rows), axis=0))

        top = lax.fori_loop(0, count, score_step, jnp.full((8, rows), NEG, F32))
        top = jnp.max(top, axis=0, keepdims=True)

        def out_step(t, acc):
            total, mixed = acc
            _, yb, ib = spot(t)
            weights = jnp.exp2((s_ref[t] - top) * EXP2_SCALE)
            s_ref[t] = weights
            total = total + jnp.sum(weights.reshape(BLK // 8, 8, rows), axis=0)
            mixed = mixed + lax.dot_general(
                values_at(yb, ib), weights.astype(BF), tn, preferred_element_type=F32
            )
            return total, mixed

        total, mixed = lax.fori_loop(
            0, count, out_step, (jnp.zeros((8, rows), F32), jnp.zeros((HD, rows), F32))
        )
        inverse = 1.0 / jnp.sum(total, axis=0, keepdims=True)
        mixed = (mixed * inverse).astype(BF).astype(F32)
        rows_to_heads(o_ref, i, mixed.T.astype(BF))
        delta = jnp.sum(mixed * grads.astype(F32).T, axis=0, keepdims=True)

        def grad_step(t, dq):
            _, yb, ib = spot(t)
            probs = s_ref[t] * inverse
            grad_probs = lax.dot_general(values_at(yb, ib), grads, nt, preferred_element_type=F32)
            grad_scores = (probs * (grad_probs - delta)).astype(BF)
            dv = jnp.dot(probs.astype(BF), grads, preferred_element_type=F32)
            dk = jnp.dot(grad_scores, queries, preferred_element_type=F32)
            dv_acc[yb, :, ib] += dv.reshape(NZ, ROWS, HD)
            dk_acc[:, yb, ib] += dk.reshape(NZ, ROWS, HD)
            return dq + lax.dot_general(keys_at(yb, ib), grad_scores, tn, preferred_element_type=F32)

        dq = lax.fori_loop(0, count, grad_step, jnp.zeros((HD, rows), F32))
        rows_to_heads(dq_ref, i, (dq * SCALE).T.astype(BF))
        return carry

    lax.fori_loop(0, NP, group, 0)

    def finish(zz, carry):
        dk_ref[zz] = (dk_acc[zz] * SCALE).astype(BF)
        for yy in range(NY):
            dv_ref[yy, zz] = dv_acc[yy, zz].astype(BF)
        return carry

    lax.fori_loop(0, NZ, finish, 0)


def scatter_kernel(
    o_ref, dq_ref, dk_ref, dv_ref, cs_ref, sidx_ref, stab_ref,
    ao_ref, gq_ref, gk_ref, gv_ref,
    dqx, kr_out, kl_out, kr_in, kl_in, vr_out, vl_out, vr_in, vl_in, ky_out, ky_in, vy_in, kv_out, kv_in,
    o_s, o_r, q_s, q_r, kzr_s, kzr_r, kzl_s, kzl_r, vzr_s, vzr_r, vzl_s, vzl_r,
    ky_s, ky_r, vy_s, vy_r, kv_s, kv_r, own_s,
):
    x, y, c, z = place()
    me = NC * x + c
    block = lax.axis_index("ctx")
    barrier = enter(me, y, z, x, c)
    pl.semaphore_wait(barrier, N_PARTNERS)

    def each_peer(fn):
        def step(d, carry):
            fn((me + d) % NP)
            return carry

        lax.fori_loop(1, NP, step, 0)

    right, left = (z + 1) % NZ, (z + NZ - 1) % NZ
    to_right, to_left = device(x, y, c, right), device(x, y, c, left)

    def head_cols(ref, g):
        return ref.at[:, pl.ds(pl.multiple_of(g * WIDE, WIDE), WIDE)]

    def o_copy(p, slot):
        return remote(o_ref.at[p], head_cols(ao_ref, slot), o_s.at[p], o_r.at[slot], peer(p, y, z))

    def q_copy(p, slot):
        return remote(dq_ref.at[p], dqx.at[slot], q_s.at[p], q_r.at[slot], peer(p, y, z))

    def vy_copy(d, zz, slot):
        yy = (y + d) % NY
        return remote(dv_ref.at[yy, zz], vy_in.at[slot, zz], vy_s.at[d, zz], vy_r.at[slot, zz], device(x, yy, c, z))

    def ring(s, out_r, out_l, in_r, in_l, r_s, r_r, l_s, l_r, cut):
        def piece(ref, low):
            return ref.at[s] if s else ref.at[s, pl.ds(0 if low else cut, cut)]

        return (
            remote(piece(out_r, True), piece(in_r, True), r_s.at[s], r_r.at[s], to_right),
            remote(piece(out_l, False), piece(in_l, False), l_s.at[s], l_r.at[s], to_left),
        )

    def k_ring(s):
        return ring(s, kr_out, kl_out, kr_in, kl_in, kzr_s, kzr_r, kzl_s, kzl_r, NY // 2)

    def v_ring(s):
        return ring(s, vr_out, vl_out, vr_in, vl_in, vzr_s, vzr_r, vzl_s, vzl_r, NP // 2)

    def begin(pair):
        for copy in pair:
            copy.start()

    def arrive(pair):
        for copy in pair:
            copy.wait_recv()

    def k_part(zz):
        return dk_ref[zz].astype(F32)

    def v_part(zz):
        total = dv_ref[y, zz].astype(F32)
        for d in range(1, NY):
            total = total + vy_in[(y + d) % NY, zz].astype(F32)
        return total

    def ring_step(s, part, out_r, out_l, in_r, in_l, copies, cut):
        if s == 0:
            whole = part((z + 4) % NZ).astype(BF)
            out_r[0, :cut] = whole[:cut]
            out_l[0, cut:] = whole[cut:]
            begin(copies(0))
            return
        arrive(copies(s - 1))
        mine_r, mine_l = part((z + 4 - s) % NZ), part((z + 4 + s) % NZ)
        if s == 1:
            out_r[1, :cut] = (mine_r[:cut] + in_r[0, :cut].astype(F32)).astype(BF)
            out_r[1, cut:] = mine_r[cut:].astype(BF)
            out_l[1, :cut] = mine_l[:cut].astype(BF)
            out_l[1, cut:] = (mine_l[cut:] + in_l[0, cut:].astype(F32)).astype(BF)
        else:
            out_r[s] = (mine_r + in_r[s - 1].astype(F32)).astype(BF)
            out_l[s] = (mine_l + in_l[s - 1].astype(F32)).astype(BF)
        begin(copies(s))

    def k_step(s):
        ring_step(s, k_part, kr_out, kl_out, kr_in, kl_in, k_ring, NY // 2)

    def wait_vy(zz):
        for d in range(1, NY):
            vy_copy(d, zz, (y + d) % NY).wait_recv()

    def v_step(s):
        if s == 0:
            wait_vy((z + 4) % NZ)
        else:
            wait_vy((z + 4 - s) % NZ)
            wait_vy((z + 4 + s) % NZ)
        ring_step(s, v_part, vr_out, vl_out, vr_in, vl_in, v_ring, NP // 2)

    k_step(0)
    for off in (4, 3, 5, 2, 6, 1, 7, 0):
        for d in (2, 1, 3):
            vy_copy(d, (z + off) % NZ, y).start()

    each_peer(lambda p: o_copy(p, me).start())
    each_peer(lambda p: q_copy(p, me).start())
    own_o = pltpu.make_async_copy(o_ref.at[me], head_cols(ao_ref, me), own_s)
    own_o.start()
    dqx[me] = dq_ref[me]

    k_step(1)
    v_step(0)
    k_step(2)
    v_step(1)
    v_step(2)
    k_step(3)
    v_step(3)

    def ky_copy(d, slot):
        yy = (y + d) % NY
        return remote(ky_out.at[yy], ky_in.at[slot], ky_s.at[d], ky_r.at[slot], device(x, yy, c, z))

    def kv_copy(p, which, slot):
        return remote(
            kv_out.at[which, p], kv_in.at[which, slot], kv_s.at[which, p], kv_r.at[which, slot], peer(p, y, z)
        )

    arrive(k_ring(3))
    k_total = k_part(z) + kr_in[3].astype(F32) + kl_in[3].astype(F32)
    ky_out[...] = k_total.astype(BF)
    for d in (2, 1, 3):
        ky_copy(d, y).start()

    wait_vy(z)
    arrive(v_ring(3))
    v_total = v_part(z) + vr_in[3].astype(F32) + vl_in[3].astype(F32)
    kv_out[1] = v_total.astype(BF)
    each_peer(lambda p: kv_copy(p, 1, me).start())

    cosine, sine = cs_ref[0], -cs_ref[1]

    def rotate_dq(p):
        for h in range(GRP):
            cols = pl.ds(pl.multiple_of(p * WIDE + h * HD, HD), HD)
            gq_ref[:, cols] = turn(dqx[p, :, h * HD:(h + 1) * HD].astype(F32), cosine, sine).astype(BF)

    rotate_dq(me)

    for d in range(1, NY):
        ky_copy(d, (y + d) % NY).wait_recv()
    k_sum = ky_out[y].astype(F32)
    for d in range(1, NY):
        k_sum = k_sum + ky_in[(y + d) % NY].astype(F32)
    kv_out[0] = k_sum.astype(BF)
    each_peer(lambda p: kv_copy(p, 0, me).start())

    def q_in(p):
        q_copy(p, p).wait_recv()
        rotate_dq(p)

    each_peer(q_in)
    kv_in[0, me] = kv_out[0, me]
    kv_in[1, me] = kv_out[1, me]

    def kv_arrive(p):
        for which in range(2):
            kv_copy(p, which, p).wait_recv()

    each_peer(kv_arrive)
    for h in range(NP):
        cols = slice(h * HD, (h + 1) * HD)
        key_scale = stab_ref[0, sidx_ref[0, block, h]]
        value_scale = stab_ref[1, sidx_ref[1, block, h]]
        gk_ref[:, cols] = (turn(kv_in[0, h].astype(F32), cosine, sine) * key_scale).astype(BF)
        gv_ref[:, cols] = (kv_in[1, h].astype(F32) * value_scale).astype(BF)

    each_peer(lambda p: o_copy(p, p).wait_recv())
    own_o.wait()

    def sent(p):
        o_copy(p, me).wait_send()
        q_copy(p, me).wait_send()
        for which in range(2):
            kv_copy(p, which, me).wait_send()

    each_peer(sent)
    for d in range(1, NY):
        ky_copy(d, y).wait_send()
    for s in range(4):
        for copy in k_ring(s) + v_ring(s):
            copy.wait_send()

    def vy_sent(zz, carry):
        for d in range(1, NY):
            vy_copy(d, zz, y).wait_send()
        return carry

    lax.fori_loop(0, NZ, vy_sent, 0)


def body(queries, keys, values, grad_out, doc_lengths, block_pairs, scale_index, scale_table):
    half = np.arange(HD // 2, dtype=np.float32) * np.float32(-2.0 * math.log(500000.0) / HD)
    freq = np.exp(half.astype(np.float32)).astype(np.float32)
    freq = jnp.asarray(np.tile(np.concatenate([freq, freq])[None], (8, 1)))
    vmem = pl.BlockSpec(memory_space=pltpu.VMEM)
    smem = pl.BlockSpec(memory_space=pltpu.SMEM)
    dma = pltpu.SemaphoreType.DMA
    shape = jax.ShapeDtypeStruct
    qx, gox, ka, va, lists, cs = pl.pallas_call(
        gather_kernel,
        name="gather",
        out_shape=(
            shape((NP, ROWS, WIDE), BF),
            shape((NP, ROWS, WIDE), BF),
            shape((NZ, NY, NP, ROWS, HD), BF),
            shape((NY, NZ, NP, ROWS, HD), BF),
            shape((NP, BLK), jnp.int32),
            shape((2, ROWS, HD), F32),
        ),
        in_specs=[vmem] * 4 + [smem, vmem, smem, smem, vmem],
        out_specs=(vmem,) * 6,
        scratch_shapes=[
            pltpu.VMEM((NP, ROWS, WIDE), BF),
            pltpu.VMEM((NP, ROWS, HD), BF),
            pltpu.VMEM((NP, ROWS, HD), BF),
        ]
        + [dma((NP,))] * 8
        + [dma((NY,))] * 2
        + [dma((4,))] * 8
        + [dma((NY, NZ))] * 2
        + [dma],
        compiler_params=pltpu.CompilerParams(
            collective_id=0, has_side_effects=True, vmem_limit_bytes=VMEM_LIMIT
        ),
    )(queries, keys, values, grad_out, doc_lengths, block_pairs, scale_index, scale_table, freq)

    o, dq, dk, dv = pl.pallas_call(
        attend_kernel,
        name="attend",
        out_shape=(
            shape((NP, ROWS, WIDE), BF),
            shape((NP, ROWS, WIDE), BF),
            shape((NZ, NY, NP, ROWS, HD), BF),
            shape((NY, NZ, NP, ROWS, HD), BF),
        ),
        in_specs=[smem, smem] + [vmem] * 4,
        out_specs=(vmem,) * 4,
        scratch_shapes=[
            pltpu.VMEM((NBLK, BLK, GRP * ROWS), F32),
            pltpu.VMEM((NZ, NY, NP, ROWS, HD), F32),
            pltpu.VMEM((NY, NZ, NP, ROWS, HD), F32),
        ],
        compiler_params=pltpu.CompilerParams(vmem_limit_bytes=VMEM_LIMIT),
    )(lists, doc_lengths, qx, gox, ka, va)

    slab_k = (4, NY, NP, ROWS, HD)
    slab_v = (4, NP, ROWS, HD)
    return pl.pallas_call(
        scatter_kernel,
        name="scatter",
        out_shape=(
            shape((ROWS, NP * WIDE), BF),
            shape((ROWS, NP * WIDE), BF),
            shape((ROWS, NP * HD), BF),
            shape((ROWS, NP * HD), BF),
        ),
        in_specs=[vmem] * 5 + [smem, smem],
        out_specs=(vmem,) * 4,
        scratch_shapes=[pltpu.VMEM((NP, ROWS, WIDE), BF)]
        + [pltpu.VMEM(slab_k, BF)] * 4
        + [pltpu.VMEM(slab_v, BF)] * 4
        + [pltpu.VMEM((NY, NP, ROWS, HD), BF)] * 2
        + [pltpu.VMEM((NY, NZ, NP, ROWS, HD), BF)]
        + [pltpu.VMEM((2, NP, ROWS, HD), BF)] * 2
        + [dma((NP,))] * 4
        + [dma((4,))] * 8
        + [dma((NY,))] * 2
        + [dma((NY, NZ))] * 2
        + [dma((2, NP))] * 2
        + [dma],
        compiler_params=pltpu.CompilerParams(
            collective_id=1, has_side_effects=True, vmem_limit_bytes=VMEM_LIMIT
        ),
    )(o, dq, dk, dv, cs, scale_index, scale_table)


def solution(mesh):
    rows = P(("ctx", "head"), None)
    in_specs = (rows,) * 4 + (P(),) * 4
    return jax.shard_map(body, mesh=mesh, in_specs=in_specs, out_specs=(rows,) * 4, check_vma=False)
```

time: 391 us -> 119 us (0.30)
  waiting for transfers between devices: 206 us -> 0 us
  Pallas kernels: 0 us -> 112 us
  matrix products: 42.5 us -> 0 us
  starting transfers between devices: 38.7 us -> 0 us
  other arithmetic: 35.4 us -> 0 us
  local copies, waits for them, and re-layouts: 34.1 us -> 6.31 us
  loops' own time: 17.2 us -> 0 us
  between operations: 14.1 us -> 0.67 us
    pallas_call x0 -> x3, Pallas kernels: none -> 112 us  [the longest x1 49.4 us: body(): pl.pallas_call(scatter_kernel, name='scatter', out_shape=(shape((ROWS, NP...]
    reduce_scatter x1 -> x0, waiting for transfers between devices: 96.8 us -> none  [body(): lax.psum_scatter(terms, 'ctx', scatter_dimension=0, tiled=True)]
    all_gather x2 -> x0, waiting for transfers between devices: 56.7 us -> none  [the longest x1 47.2 us: body(): lax.all_gather(k_mid, 'ctx', axis=0, tiled=True)]
    all_to_all x7 -> x0, waiting for transfers between devices: 52.1 us -> none  [the longest x1 15.6 us: body(): lax.all_to_all(out_mid, 'head', split_axis=0, concat_axis=1, tiled=True)]
    dot_general x32 -> x0, matrix products: 42.5 us -> none  [the longest x24 33.4 us: visible(): lax.dot_general(row_listed, key_hot, (((1,), (1,)), ((), ())), preferred_...]
    all_to_all x7 -> x0, starting transfers between devices: 38.6 us -> none  [the longest x1 9.01 us: body(): lax.all_to_all(values, 'head', split_axis=1, concat_axis=0, tiled=True)]
    another operation x27 -> x0, loops' own time: 17.2 us -> none  [the longest x1 5.59 us: body(): dq_accum, key_terms = lax.scan(grad_step, zero_rows, key_blocks)]
    another operation x4 -> x0, other arithmetic: 12.5 us -> none
  transfers between devices with their start and end apart: 10 -> 0, of which waited for: 9 -> 0; matrix products, arithmetic and copies ran while one was open for 5% -> 0% of each run, Pallas kernels for 0% -> 0%
where the time goes in v1:
time: 119 us
  Pallas kernels  112 us (94%)
  local copies, waits for them, and re-layouts  6.31 us (5%)
    pallas_call x1, Pallas kernels, body(): pl.pallas_call(scatter_kernel, name='scatter', out_shape=(shape((ROWS, NP...  49.4 us
    pallas_call x1, Pallas kernels, body(): pl.pallas_call(gather_kernel, name='gather', out_shape=(shape((NP, ROWS,...  39.5 us
    pallas_call x1, Pallas kernels, body(): pl.pallas_call(attend_kernel, name='attend', out_shape=(shape((NP, ROWS,...  23 us
    unnamed x14, local copies, waits for them, and re-layouts  6.31 us

profile of v1, /device:TPU:1, one launch (start us, length us, event | category | flops | bytes accessed | tf_op | source)
XLA Modules:
  0.0 118.9 jit_solution(7337404066292934782)
XLA Ops:
  0.6 0.0 copy-start.3
  0.6 1.4 %copy.14.sidx_ref = s32[2,32,8]{2,1,0:T(8,128)} copy(s32[2,32,8]{1,2,0:T(8,128)} %param.15) | data formatting | bytes 4096 | tf_op args[6]
  2.0 0.0 copy-done.3
  2.0 0.8 copy.13.pairs_ref
  2.8 39.5 %gather.1 = (bf16[8,16,2048]{2,1,0:T(8,128)(2,1)}, bf16[8,16,2048]{2,1,0:T(8,128)(2,1)}, bf16[8,4,8,16,128]{4,3,2,1,0:T(8,128)(2,1)}, bf16[4,8,8,16,128]{4,3,2,1...) custom-call(bf16[16,16384]{1,0:T(8,128)(2,1)} %q_ref.1, bf16[16,1024]{1,0:T(8,128)(2,1)} %k_ref.1, ...), custom_call_target="tpu_custom_call" | custom-call | tf_op jit(solution)/shard_map/gather/pallas_call | solution.py:610
  42.3 23.0 %attend.1 = (bf16[8,16,2048]{2,1,0:T(8,128)(2,1)}, bf16[8,16,2048]{2,1,0:T(8,128)(2,1)}, bf16[8,4,8,16,128]{4,3,2,1,0:T(8,128)(2,1)}, bf16[4,8,8,16,128]{4,3,2,1,0:T(8,128)(2,1)}) custom-call(s32[8,128]{1,0:T(8,128)} %get-tuple-element.14.lists_ref, s32[8]{0:T(128)} %doc_ref.3, bf16[8,16,2048]{2,1,0:T(8,128)(2,1)} %get-tuple-element.15.q_ref, ...), custom_call_target="tpu_custom_call" | custom-call | tf_op jit(solution)/shard_map/attend/pallas_call | solution.py:638
  65.3 49.4 %scatter.1 = (bf16[16,16384]{1,0:T(8,128)(2,1)}, bf16[16,16384]{1,0:T(8,128)(2,1)}, bf16[16,1024]{1,0:T(8,128)(2,1)}, bf16[16,1024]{1,0:T(8,128)(2,1)}) custom-call(bf16[8,16,2048]{2,1,0:T(8,128)(2,1)} %get-tuple-element.19.o_ref, bf16[8,16,2048]{2,1,0:T(8,128)(2,1)} %get-tuple-element.20.dq_ref, bf16[8,4,8,16,128]{4,3,2,1,0:T(8,128)(2,1)} %get-tuple-element.21.dk_ref, ...), custom_call_target="tpu_custom_call" | custom-call | tf_op jit(solution)/shard_map/scatter/pallas_call | solution.py:659
  114.8 0.0 copy-start
  114.8 1.9 %copy.20 = bf16[16,16384]{1,0:T(8,128)(2,1)} copy(bf16[16,16384]{1,0:T(8,128)(2,1)} %get-tuple-element.28) | data formatting | bytes 1048576
  116.7 0.0 copy-done
  116.7 0.0 copy-start.2
  116.7 0.8 copy.21
  117.5 0.0 copy-done.2
  117.5 0.0 copy-start.1
  117.5 0.6 copy.22
  118.1 0.2 copy-done.1
  118.3 0.6 copy.23
Async XLA Ops:
  0.6 1.4 %copy-start.3 = (s32[248,2]{0,1:T(2,128)S(1)}, s32[248,2]{0,1:T(2,128)}, u32[]{:S(2)}) copy-start(s32[248,2]{0,1:T(2,128)} %param.14) | copy-start | bytes 5956
  114.8 1.9 %copy-start = (bf16[16,16384]{1,0:T(8,128)(2,1)S(1)}, bf16[16,16384]{1,0:T(8,128)(2,1)}, u32[]{:S(2)}) copy-start(bf16[16,16384]{1,0:T(8,128)(2,1)} %get-tuple-element.29) | copy-start | bytes 1572868
  116.7 0.8 copy-start.2
  117.5 0.8 copy-start.1

commit v2 on v1

v2 whole, which is shorter than its diff:
```python
import functools
import math

import jax
import jax.numpy as jnp
import numpy as np
from jax import lax
from jax.experimental import pallas as pl
from jax.experimental.pallas import tpu as pltpu
from jax.sharding import PartitionSpec as P

HD = 128
BLK = 128
ROWS = 16
GRP = 16
NX, NY, NC, NZ = 4, 4, 2, 8
NP = NX * NC
NBLK = 32
NDOC = 8
WIDE = GRP * HD
NEG = -1e30
CHUNK = 4
TWIN = 2
SCALE = 1.0 / math.sqrt(HD)
EXP2_SCALE = SCALE * math.log2(math.e)
MESH = pl.DeviceIdType.MESH
BF = jnp.bfloat16
F32 = jnp.float32
VMEM_LIMIT = 56 * 1024 * 1024


def place():
    ctx = lax.axis_index("ctx")
    return ctx // (NY * NC), (ctx // NC) % NY, ctx % NC, lax.axis_index("head")


def device(xx, yy, cc, zz):
    return {"ctx": xx * (NY * NC) + yy * NC + cc, "head": zz}


def peer(p, y, z):
    return device(p // NC, y, p % NC, z)


def remote(src, dst, send_sem, recv_sem, dev):
    return pltpu.make_async_remote_copy(
        src_ref=src, dst_ref=dst, send_sem=send_sem, recv_sem=recv_sem, device_id=dev, device_id_type=MESH
    )


def enter(me, x, y, c, z):
    barrier = pltpu.get_barrier_semaphore()

    def greet(dev):
        pl.semaphore_signal(barrier, inc=1, device_id=dev, device_id_type=MESH)

    for off in (2, NZ - 2, 1, NZ - 1):
        greet(device(x, y, c, (z + off) % NZ))

    def step(e, carry):
        greet(peer((me + e % NP) % NP, (y + e // NP) % NY, z))
        return carry

    lax.fori_loop(1, NP * NY, step, 0)
    return barrier


N_PARTNERS = NP * NY - 1 + 4


def loop(lo, hi, fn):
    def step(i, carry):
        fn(i)
        return carry

    lax.fori_loop(lo, hi, step, 0)


def turn(x, cosine, sine):
    return x * cosine + pltpu.roll(x, HD // 2, 1) * sine


def gather_kernel(
    q_ref, k_ref, v_ref, go_ref, doc_ref, pairs_ref, sidx_ref, stab_ref, freq_ref,
    qx_ref, gox_ref, ka_ref, va_ref, lists_ref, cs_ref,
    qs, ks, vs,
    q_s, q_r, go_s, go_r, k_s, k_r, v_s, v_r, kzr_s, kzr_r, kzl_s, kzl_r,
    va_s, va_r, vb_s, vb_r, vy_s, vy_r, own_s,
):
    x, y, c, z = place()
    me = NC * x + c
    block = lax.axis_index("ctx")
    barrier = enter(me, x, y, c, z)

    token = BLK * block + ROWS * z + lax.broadcasted_iota(jnp.int32, (ROWS, HD), 0)
    start = jnp.zeros((ROWS, HD), jnp.int32)
    end = 0
    for d in range(NDOC):
        end = end + doc_ref[d]
        start = start + jnp.where(token >= end, doc_ref[d], 0)
    angle = (token - start).astype(F32) * freq_ref[0:1, :]
    cosine = jnp.cos(angle)
    sine = jnp.sin(angle)
    sine = jnp.where(lax.broadcasted_iota(jnp.int32, (ROWS, HD), 1) < HD // 2, -sine, sine)
    cs_ref[0] = cosine
    cs_ref[1] = sine

    for h in range(NP):
        cols = slice(h * HD, (h + 1) * HD)
        key_scale = stab_ref[0, sidx_ref[0, h, block]]
        value_scale = stab_ref[1, sidx_ref[1, h, block]]
        ks[h] = turn(k_ref[:, cols].astype(F32) * key_scale, cosine, sine).astype(BF)
        vs[h] = (v_ref[:, cols].astype(F32) * value_scale).astype(BF)

    def rotate_q(p):
        for h in range(GRP):
            cols = pl.ds(pl.multiple_of(p * WIDE + h * HD, HD), HD)
            qs[p, :, h * HD:(h + 1) * HD] = turn(q_ref[:, cols].astype(F32), cosine, sine).astype(BF)

    loop(0, NP, rotate_q)
    qx_ref[me] = qs[me]
    ka_ref[z, y, me] = ks[me]
    va_ref[y, z, me] = vs[me]

    pl.semaphore_wait(barrier, N_PARTNERS)

    def each_peer(fn):
        loop(1, NP, lambda d: fn((me + d) % NP))

    def k_copy(e, arriving):
        p, yy = (me + e % NP) % NP, (y + e // NP) % NY
        ys, slot = (yy, p) if arriving else (y, me)
        return remote(ks.at[p], ka_ref.at[z, ys, slot], k_s.at[e], k_r.at[ys, slot], peer(p, yy, z))

    def v_copy(p, slot):
        return remote(vs.at[p], va_ref.at[y, z, slot], v_s.at[p], v_r.at[slot], peer(p, y, z))

    def go_cols(p):
        return go_ref.at[:, pl.ds(pl.multiple_of(p * WIDE, WIDE), WIDE)]

    def go_copy(p, slot):
        return remote(go_cols(p), gox_ref.at[slot], go_s.at[p], go_r.at[slot], peer(p, y, z))

    def q_copy(p, slot):
        return remote(qs.at[p], qx_ref.at[slot], q_s.at[p], q_r.at[slot], peer(p, y, z))

    each_peer(lambda p: v_copy(p, me).start())
    loop(1, NP * NY, lambda e: k_copy(e, False).start())
    each_peer(lambda p: go_copy(p, me).start())
    each_peer(lambda p: q_copy(p, me).start())
    own_go = pltpu.make_async_copy(go_cols(me), gox_ref.at[me], own_s)
    own_go.start()

    def along(off):
        return device(x, y, c, (z + off + NZ) % NZ)

    def k_ring(s, u, rightward, sending):
        far = s if sending else s + 1
        zz = (z + NZ - far) % NZ if rightward else (z + far) % NZ
        ref = ka_ref.at[zz, pl.ds(u * (NY // 2), NY // 2)]
        if rightward:
            return remote(ref, ref, kzr_s.at[s, u], kzr_r.at[s, u], along(1))
        return remote(ref, ref, kzl_s.at[s, u], kzl_r.at[s, u], along(-1))

    def k_sends(s):
        return [(u, r) for u in range(2) for r in (True, False) if s < 3 or (u == 0) == r]

    first_hops = (1, -1, 2, -2)

    def v_first(j, arriving):
        zz = (z + first_hops[j] + NZ) % NZ if arriving else z
        ref = va_ref.at[y, zz]
        return remote(ref, ref, va_s.at[j], va_r.at[j], along(-first_hops[j]))

    def v_second(j, arriving):
        off, part = ((2, None), (-2, None), (2, 0), (-2, 1))[j]
        hop = -1 if off > 0 else 1
        if part is not None:
            hop = 2 * hop
        zz = (z + off - (hop if arriving else 0) + NZ) % NZ
        ref = va_ref.at[y, zz]
        if part is not None:
            ref = va_ref.at[y, zz, pl.ds(part * (NP // 2), NP // 2)]
        return remote(ref, ref, vb_s.at[j], vb_r.at[j], along(hop))

    def v_spread(zz, d, arriving):
        yy = (y + d) % NY
        ys = yy if arriving else y
        return remote(va_ref.at[ys, zz], va_ref.at[ys, zz], vy_s.at[d, zz], vy_r.at[ys, zz], device(x, yy, c, z))

    def spread(off):
        for d in (2, 1, 3):
            v_spread((z + off + NZ) % NZ, d, False).start()

    each_peer(lambda p: v_copy(p, p).wait_recv())
    for j in (2, 3, 0, 1):
        v_first(j, False).start()
    spread(0)
    loop(1, NP * NY, lambda e: k_copy(e, True).wait_recv())
    for u, r in k_sends(0):
        k_ring(0, u, r, True).start()

    lane = lax.broadcasted_iota(jnp.int32, (NP, BLK), 1)
    row = lax.broadcasted_iota(jnp.int32, (NP, BLK), 0)
    own_block = NY * NC * (row // NC) + NC * y + row % NC
    first = BLK * own_block + ROWS * z
    doc_start = jnp.zeros((NP, BLK), jnp.int32)
    end = 0
    for d in range(NDOC):
        end = end + doc_ref[d]
        doc_start = doc_start + jnp.where(first >= end, doc_ref[d], 0)
    pairs = pairs_ref[...]
    n_pairs = pairs.shape[1]
    pair_row = lax.broadcasted_iota(jnp.int32, (NP, n_pairs), 0)
    pair_q = (pairs[0:1] == NY * NC * (pair_row // NC) + NC * y + pair_row % NC).astype(F32)
    pair_k = (pairs[1:2] == lax.broadcasted_iota(jnp.int32, (BLK, n_pairs), 0)).astype(F32)
    listed = lax.dot_general(pair_q, pair_k, (((1,), (1,)), ((), ())), preferred_element_type=F32)
    wanted = ((listed > 0.5) | (lane == own_block)) & (BLK * lane + BLK - 1 >= doc_start) & (lane <= own_block)
    wanted_f = wanted.astype(F32)
    upper = (
        lax.broadcasted_iota(jnp.int32, (BLK, BLK), 0) <= lax.broadcasted_iota(jnp.int32, (BLK, BLK), 1)
    ).astype(F32)
    rank = jnp.dot(wanted_f, upper, preferred_element_type=F32)
    lane_f = lane.astype(F32)

    def list_step(r, out):
        hit = wanted & (rank.astype(jnp.int32) == r + 1)
        entry = jnp.sum(jnp.where(hit, lane_f, 0.0), axis=1, keepdims=True)
        return jnp.where(lane == r, entry, out)

    out = lax.fori_loop(0, NBLK, list_step, jnp.zeros((NP, BLK), F32))
    out = jnp.where(lane == BLK - 1, jnp.sum(wanted_f, axis=1, keepdims=True), out)
    lists_ref[...] = out.astype(jnp.int32)

    def k_step(s):
        onward = k_sends(s) if s < 4 else []
        for u, r in k_sends(s - 1):
            k_ring(s - 1, u, r, False).wait_recv()
            if (u, r) in onward:
                k_ring(s, u, r, True).start()

    for j in (0, 1):
        v_first(j, True).wait_recv()
        spread(first_hops[j])
    for j in (2, 3):
        v_first(j, True).wait_recv()
        v_second(j, False).start()
        v_second(j - 2, False).start()
        spread(first_hops[j])
    k_step(1)
    for j in (0, 1):
        v_second(j, True).wait_recv()
        spread((3, -3)[j])
    for j in (2, 3):
        v_second(j, True).wait_recv()
    spread(4)
    k_step(2)
    k_step(3)
    k_step(4)

    def spread_in(zz):
        for d in range(1, NY):
            v_spread(zz, d, True).wait_recv()

    loop(0, NZ, spread_in)

    def qgo_in(p):
        go_copy(p, p).wait_recv()
        q_copy(p, p).wait_recv()

    each_peer(qgo_in)
    own_go.wait()

    def sent(p):
        v_copy(p, me).wait_send()
        go_copy(p, me).wait_send()
        q_copy(p, me).wait_send()

    each_peer(sent)
    loop(1, NP * NY, lambda e: k_copy(e, False).wait_send())
    for s in range(4):
        for u, r in k_sends(s):
            k_ring(s, u, r, True).wait_send()
    for j in range(4):
        v_first(j, False).wait_send()
        v_second(j, False).wait_send()

    def spread_sent(zz):
        for d in range(1, NY):
            v_spread(zz, d, False).wait_send()

    loop(0, NZ, spread_sent)


def heads_to_rows(ref, i):
    return jnp.concatenate([ref[i, :, h * HD:(h + 1) * HD] for h in range(GRP)], axis=0)


def rows_to_heads(ref, i, rows):
    for h in range(GRP):
        ref[i, :, h * HD:(h + 1) * HD] = rows[h * ROWS:(h + 1) * ROWS]


SPAN = CHUNK * BLK


def attend_kernel(lists_ref, doc_ref, q_ref, go_ref, k_ref, v_ref, o_ref, dq_ref, dk_ref, dv_ref,
                  s_ref, dp_ref, o_acc, dq_acc, dk_acc, dv_acc):
    _, y, _, z = place()
    rows = GRP*ROWS
    dk_acc[...] = jnp.zeros_like(dk_acc)
    dv_acc[...] = jnp.zeros_like(dv_acc)
    key_row = lax.broadcasted_iota(jnp.int32, (BLK, rows), 0)
    lane = lax.broadcasted_iota(jnp.int32, (1, rows), 1)
    nt = (((1,), (1,)), ((), ()))
    tn = (((0,), (0,)), ((), ()))

    def pair(pi, carry):
        gs = [pi*TWIN+j for j in range(TWIN)]
        counts = [lists_ref[g, BLK-1] for g in gs]
        most = functools.reduce(jnp.maximum, counts)
        chunks = (most + CHUNK - 1)//CHUNK
        queries = [heads_to_rows(q_ref, g) for g in gs]
        grads = [heads_to_rows(go_ref, g) for g in gs]
        tokens, starts = [], []
        for g in gs:
            own = NY*NC*(g//NC) + NC*y + g%NC
            token = BLK*own + ROWS*z + lane%ROWS
            start = jnp.zeros((1, rows), jnp.int32)
            end = 0
            for d in range(NDOC):
                end = end + doc_ref[d]
                start = start + jnp.where(token >= end, doc_ref[d], 0)
            tokens.append(token); starts.append(start)

        def spots(j, n):
            out = []
            for u in range(CHUNK):
                t = n*CHUNK + u
                b = lists_ref[gs[j], t]
                out.append((t < counts[j], b, (b//NC)%NY, (b//(NY*NC))*NC + b%NC))
            return out

        def keys_of(sp):
            return jnp.concatenate([k_ref[:, yb, ib].reshape(BLK, HD) for _, _, yb, ib in sp], axis=0)

        def values_of(sp):
            return jnp.concatenate([v_ref[yb, :, ib].reshape(BLK, HD) for _, _, yb, ib in sp], axis=0)

        def fold(x):
            return x.reshape(SPAN//8, 8, rows)

        def score_step(n, tops):
            out = []
            for j in range(TWIN):
                sp = spots(j, n)
                scores = lax.dot_general(keys_of(sp), queries[j], nt, preferred_element_type=F32)
                dp_ref[j, n] = lax.dot_general(values_of(sp), grads[j], nt, preferred_element_type=F32)
                top = tops[j]
                for u, (live, b, _, _) in enumerate(sp):
                    low = jnp.where(live, starts[j] - BLK*b, BLK)
                    allowed = (key_row >= low) & (key_row <= tokens[j] - BLK*b)
                    part = jnp.where(allowed, scores[u*BLK:(u+1)*BLK], NEG)
                    s_ref[j, n, u*BLK:(u+1)*BLK] = part
                    top = jnp.maximum(top, jnp.max(part.reshape(BLK//8, 8, rows), axis=0))
                out.append(top)
            return tuple(out)

        tops = lax.fori_loop(0, chunks, score_step, tuple(jnp.full((8, rows), NEG, F32) for _ in gs))
        tops = [jnp.max(t, axis=0, keepdims=True) for t in tops]
        for j in range(TWIN):
            o_acc[j] = jnp.zeros((HD, rows), F32)
            dq_acc[j] = jnp.zeros((HD, rows), F32)

        def out_step(n, carry):
            out = []
            for j in range(TWIN):
                total, mean = carry[j]
                sp = spots(j, n)
                weights = jnp.exp2((s_ref[j, n] - tops[j])*EXP2_SCALE)
                s_ref[j, n] = weights
                total = total + jnp.sum(fold(weights), axis=0)
                mean = mean + jnp.sum(fold(weights*dp_ref[j, n]), axis=0)
                o_acc[j] += lax.dot_general(values_of(sp), weights.astype(BF), tn, preferred_element_type=F32)
                out.append((total, mean))
            return tuple(out)

        zero = jnp.zeros((8, rows), F32)
        sums = lax.fori_loop(0, chunks, out_step, tuple((zero, zero) for _ in gs))
        inverses, deltas = [], []
        for j in range(TWIN):
            inverse = 1.0/jnp.sum(sums[j][0], axis=0, keepdims=True)
            inverses.append(inverse)
            deltas.append(jnp.sum(sums[j][1], axis=0, keepdims=True)*inverse)

        def grad_step(n, carry):
            for j in range(TWIN):
                sp = spots(j, n)
                probs = s_ref[j, n]*inverses[j]
                grad_scores = (probs*(dp_ref[j, n] - deltas[j])).astype(BF)
                dv = jnp.dot(probs.astype(BF), grads[j], preferred_element_type=F32)
                dk = jnp.dot(grad_scores, queries[j], preferred_element_type=F32)
                dq_acc[j] += lax.dot_general(keys_of(sp), grad_scores, tn, preferred_element_type=F32)
                for u, (_, _, yb, ib) in enumerate(sp):
                    dv_acc[yb, :, ib] += dv[u*BLK:(u+1)*BLK].reshape(NZ, ROWS, HD)
                    dk_acc[:, yb, ib] += dk[u*BLK:(u+1)*BLK].reshape(NZ, ROWS, HD)
            return carry

        lax.fori_loop(0, chunks, grad_step, 0)
        for j in range(TWIN):
            rows_to_heads(o_ref, gs[j], (o_acc[j]*inverses[j]).T.astype(BF))
            rows_to_heads(dq_ref, gs[j], (dq_acc[j]*SCALE).T.astype(BF))
        return carry

    lax.fori_loop(0, NP//TWIN, pair, 0)

    def finish(zz, carry):
        dk_ref[zz] = (dk_acc[zz]*SCALE).astype(BF)
        for yy in range(NY):
            dv_ref[yy, zz] = dv_acc[yy, zz].astype(BF)
        return carry
    lax.fori_loop(0, NZ, finish, 0)


def scatter_kernel(
    o_ref, dq_ref, dk_ref, dv_ref, cs_ref, sidx_ref, stab_ref,
    ao_ref, gq_ref, gk_ref, gv_ref,
    dqx, kr_out, kl_out, kr_in, kl_in, va_out, va_in, vb_out, vb_in, k_out, k_in, vy_in, v_out, v_in,
    o_s, o_r, q_s, q_r, kzr_s, kzr_r, kzl_s, kzl_r, va_s, va_r, vb_s, vb_r,
    vy_s, vy_r, k_s, k_r, v_s, v_r, own_s,
):
    x, y, c, z = place()
    me = NC * x + c
    block = lax.axis_index("ctx")
    barrier = enter(me, x, y, c, z)
    pl.semaphore_wait(barrier, N_PARTNERS)

    def each_peer(fn):
        loop(1, NP, lambda d: fn((me + d) % NP))

    def along(off):
        return device(x, y, c, (z + off + NZ) % NZ)

    def head_cols(ref, g):
        return ref.at[:, pl.ds(pl.multiple_of(g * WIDE, WIDE), WIDE)]

    def o_copy(p, slot):
        return remote(o_ref.at[p], head_cols(ao_ref, slot), o_s.at[p], o_r.at[slot], peer(p, y, z))

    def q_copy(p, slot):
        return remote(dq_ref.at[p], dqx.at[slot], q_s.at[p], q_r.at[slot], peer(p, y, z))

    def vy_copy(off, d, arriving):
        zz, yy = (z + off + NZ) % NZ, (y + d) % NY
        slot = yy if arriving else y
        return remote(dv_ref.at[yy, zz], vy_in.at[slot, zz], vy_s.at[d, zz], vy_r.at[slot, zz], device(x, yy, c, z))

    half = NY // 2

    def k_ring(s, u, rightward):
        if rightward:
            return remote(kr_out.at[s, u], kr_in.at[s, u], kzr_s.at[s, u], kzr_r.at[s, u], along(1))
        return remote(kl_out.at[s, u], kl_in.at[s, u], kzl_s.at[s, u], kzl_r.at[s, u], along(-1))

    def k_part(zz, u):
        return dk_ref[zz, u * half:(u + 1) * half].astype(F32)

    def k_send(s, u, rightward):
        zz = (z + 4 - s) % NZ if rightward else (z + 4 + s) % NZ
        total = k_part(zz, u)
        if s > 1 or (s == 1 and (u == 0) == rightward):
            k_ring(s - 1, u, rightward).wait_recv()
            total = total + (kr_in if rightward else kl_in)[s - 1, u].astype(F32)
        (kr_out if rightward else kl_out)[s, u] = total.astype(BF)
        k_ring(s, u, rightward).start()

    def v_part(off):
        zz = (z + off + NZ) % NZ
        total = dv_ref[y, zz].astype(F32)
        for d in range(1, NY):
            vy_copy(off, d, True).wait_recv()
            total = total + vy_in[(y + d) % NY, zz].astype(F32)
        return total

    cut = NP // 2

    def v_far(j):
        hop = (1, -1, 2, -2)[j]
        if j < 2:
            return remote(va_out.at[j], va_in.at[j], va_s.at[j], va_r.at[j], along(hop))
        part = pl.ds(0 if j == 2 else cut, cut)
        return remote(va_out.at[2, part], va_in.at[2, part], va_s.at[j], va_r.at[j], along(hop))

    near = (1, -1, 2, -2)

    def v_near(j):
        return remote(vb_out.at[j], vb_in.at[j], vb_s.at[j], vb_r.at[j], along(near[j]))

    k_send(0, 0, True)
    k_send(0, 1, False)
    k_send(1, 1, True)
    k_send(1, 0, False)
    order = (3, -3, 4, 2, -2, 1, -1, 0)
    for off in order:
        for d in (2, 1, 3):
            vy_copy(off, d, False).start()
    each_peer(lambda p: o_copy(p, me).start())
    each_peer(lambda p: q_copy(p, me).start())
    own_o = pltpu.make_async_copy(o_ref.at[me], head_cols(ao_ref, me), own_s)
    own_o.start()
    dqx[me] = dq_ref[me]

    k_send(1, 0, True)
    k_send(1, 1, False)
    va_out[0] = v_part(3).astype(BF)
    v_far(0).start()
    va_out[1] = v_part(-3).astype(BF)
    v_far(1).start()
    va_out[2] = v_part(4).astype(BF)
    v_far(2).start()
    v_far(3).start()
    for u, r in ((1, True), (0, False), (0, True), (1, False)):
        k_send(2, u, r)
    v_two = [v_part(2), v_part(-2)]
    for j in range(2):
        v_far(j).wait_recv()
        v_far(j + 2).wait_recv()
        total = v_two[j] + va_in[j].astype(F32)
        low, high = total[:cut], total[cut:]
        if j == 0:
            low = low + va_in[2, :cut].astype(F32)
        else:
            high = high + va_in[2, cut:].astype(F32)
        vb_out[j + 2, :cut] = low.astype(BF)
        vb_out[j + 2, cut:] = high.astype(BF)
        v_near(j + 2).start()
    for j in range(2):
        vb_out[j] = v_part(near[j]).astype(BF)
        v_near(j).start()
    for u, r in ((1, True), (0, False), (0, True), (1, False)):
        k_send(3, u, r)

    def k_copy(e, arriving):
        p, yy = (me + e % NP) % NP, (y + e // NP) % NY
        ys, slot = (yy, p) if arriving else (y, me)
        return remote(k_out.at[yy, p], k_in.at[ys, slot], k_s.at[e], k_r.at[ys, slot], peer(p, yy, z))

    def v_copy(p, slot):
        return remote(v_out.at[p], v_in.at[slot], v_s.at[p], v_r.at[slot], peer(p, y, z))

    cosine, sine = cs_ref[0], -cs_ref[1]

    def rotate_dq(p):
        for h in range(GRP):
            cols = pl.ds(pl.multiple_of(p * WIDE + h * HD, HD), HD)
            gq_ref[:, cols] = turn(dqx[p, :, h * HD:(h + 1) * HD].astype(F32), cosine, sine).astype(BF)

    v_total = v_part(0)
    for j in range(4):
        v_near(j).wait_recv()
        v_total = v_total + vb_in[j].astype(F32)
    v_out[...] = v_total.astype(BF)
    v_in[me] = v_out[me]
    each_peer(lambda p: v_copy(p, me).start())

    for u in range(2):
        k_ring(3, u, True).wait_recv()
        k_ring(3, u, False).wait_recv()
        total = k_part(z, u) + kr_in[3, u].astype(F32) + kl_in[3, u].astype(F32)
        k_out[u * half:(u + 1) * half] = total.astype(BF)
    k_in[y, me] = k_out[y, me]
    loop(1, NP * NY, lambda e: k_copy(e, False).start())

    rotate_dq(me)

    def q_in(p):
        q_copy(p, p).wait_recv()
        rotate_dq(p)

    each_peer(q_in)
    each_peer(lambda p: v_copy(p, p).wait_recv())
    for h in range(NP):
        value_scale = stab_ref[1, sidx_ref[1, h, block]]
        gv_ref[:, h * HD:(h + 1) * HD] = (v_in[h].astype(F32) * value_scale).astype(BF)
    loop(1, NP * NY, lambda e: k_copy(e, True).wait_recv())
    for h in range(NP):
        key_scale = stab_ref[0, sidx_ref[0, h, block]]
        total = k_in[0, h].astype(F32)
        for yy in range(1, NY):
            total = total + k_in[yy, h].astype(F32)
        gk_ref[:, h * HD:(h + 1) * HD] = (turn(total, cosine, sine) * key_scale).astype(BF)

    each_peer(lambda p: o_copy(p, p).wait_recv())
    own_o.wait()

    def sent(p):
        o_copy(p, me).wait_send()
        q_copy(p, me).wait_send()
        v_copy(p, me).wait_send()

    each_peer(sent)
    loop(1, NP * NY, lambda e: k_copy(e, False).wait_send())
    for s in range(4):
        for u in range(2):
            for r in (True, False):
                if s or (u == 0) == r:
                    k_ring(s, u, r).wait_send()
    for j in range(4):
        v_far(j).wait_send()
        v_near(j).wait_send()
    for off in order:
        for d in (2, 1, 3):
            vy_copy(off, d, False).wait_send()


def body(queries, keys, values, grad_out, doc_lengths, block_pairs, scale_index, scale_table):
    half = np.arange(HD // 2, dtype=np.float32) * np.float32(-2.0 * math.log(500000.0) / HD)
    freq = np.exp(half.astype(np.float32)).astype(np.float32)
    freq = jnp.asarray(np.tile(np.concatenate([freq, freq])[None], (8, 1)))
    scale_by_head = scale_index.transpose(0, 2, 1)
    vmem = pl.BlockSpec(memory_space=pltpu.VMEM)
    smem = pl.BlockSpec(memory_space=pltpu.SMEM)
    dma = pltpu.SemaphoreType.DMA
    shape = jax.ShapeDtypeStruct
    qx, gox, ka, va, lists, cs = pl.pallas_call(
        gather_kernel,
        name="gather",
        out_shape=(
            shape((NP, ROWS, WIDE), BF),
            shape((NP, ROWS, WIDE), BF),
            shape((NZ, NY, NP, ROWS, HD), BF),
            shape((NY, NZ, NP, ROWS, HD), BF),
            shape((NP, BLK), jnp.int32),
            shape((2, ROWS, HD), F32),
        ),
        in_specs=[vmem] * 4 + [smem, vmem, smem, smem, vmem],
        out_specs=(vmem,) * 6,
        scratch_shapes=[
            pltpu.VMEM((NP, ROWS, WIDE), BF),
            pltpu.VMEM((NP, ROWS, HD), BF),
            pltpu.VMEM((NP, ROWS, HD), BF),
        ]
        + [dma((NP,))] * 4
        + [dma((NP * NY,)), dma((NY, NP))]
        + [dma((NP,))] * 2
        + [dma((4, 2))] * 4
        + [dma((4,))] * 4
        + [dma((NY, NZ))] * 2
        + [dma],
        compiler_params=pltpu.CompilerParams(
            collective_id=0, has_side_effects=True, vmem_limit_bytes=VMEM_LIMIT
        ),
    )(queries, keys, values, grad_out, doc_lengths, block_pairs.T, scale_by_head, scale_table, freq)

    o, dq, dk, dv = pl.pallas_call(
        attend_kernel,
        name="attend",
        out_shape=(
            shape((NP, ROWS, WIDE), BF),
            shape((NP, ROWS, WIDE), BF),
            shape((NZ, NY, NP, ROWS, HD), BF),
            shape((NY, NZ, NP, ROWS, HD), BF),
        ),
        in_specs=[smem, smem] + [vmem] * 4,
        out_specs=(vmem,) * 4,
        scratch_shapes=[
            pltpu.VMEM((TWIN, NBLK // CHUNK, SPAN, GRP * ROWS), F32),
            pltpu.VMEM((TWIN, NBLK // CHUNK, SPAN, GRP * ROWS), F32),
            pltpu.VMEM((TWIN, HD, GRP * ROWS), F32),
            pltpu.VMEM((TWIN, HD, GRP * ROWS), F32),
            pltpu.VMEM((NZ, NY, NP, ROWS, HD), F32),
            pltpu.VMEM((NY, NZ, NP, ROWS, HD), F32),
        ],
        compiler_params=pltpu.CompilerParams(vmem_limit_bytes=VMEM_LIMIT),
    )(lists, doc_lengths, qx, gox, ka, va)

    return pl.pallas_call(
        scatter_kernel,
        name="scatter",
        out_shape=(
            shape((ROWS, NP * WIDE), BF),
            shape((ROWS, NP * WIDE), BF),
            shape((ROWS, NP * HD), BF),
            shape((ROWS, NP * HD), BF),
        ),
        in_specs=[vmem] * 5 + [smem, smem],
        out_specs=(vmem,) * 4,
        scratch_shapes=[pltpu.VMEM((NP, ROWS, WIDE), BF)]
        + [pltpu.VMEM((4, 2, NY // 2, NP, ROWS, HD), BF)] * 4
        + [pltpu.VMEM((3, NP, ROWS, HD), BF)] * 2
        + [pltpu.VMEM((4, NP, ROWS, HD), BF)] * 2
        + [pltpu.VMEM((NY, NP, ROWS, HD), BF)] * 2
        + [pltpu.VMEM((NY, NZ, NP, ROWS, HD), BF)]
        + [pltpu.VMEM((NP, ROWS, HD), BF)] * 2
        + [dma((NP,))] * 4
        + [dma((4, 2))] * 4
        + [dma((4,))] * 4
        + [dma((NY, NZ))] * 2
        + [dma((NP * NY,)), dma((NY, NP))]
        + [dma((NP,))] * 2
        + [dma],
        compiler_params=pltpu.CompilerParams(
            collective_id=1, has_side_effects=True, vmem_limit_bytes=VMEM_LIMIT
        ),
    )(o, dq, dk, dv, cs, scale_by_head, scale_table)


def solution(mesh):
    rows = P(("ctx", "head"), None)
    in_specs = (rows,) * 4 + (P(),) * 4
    return jax.shard_map(body, mesh=mesh, in_specs=in_specs, out_specs=(rows,) * 4, check_vma=False)
```

time: 119 us -> 96.2 us (0.81)
  Pallas kernels: 112 us -> 91.1 us
  local copies, waits for them, and re-layouts: 6.31 us -> 4.11 us
    pallas_call x1, Pallas kernels: 23 us -> 12.1 us  [body(): pl.pallas_call(attend_kernel, name='attend', out_shape=(shape((NP, ROWS,...]
    pallas_call x1, Pallas kernels: 49.4 us -> 41.3 us  [body(): pl.pallas_call(scatter_kernel, name='scatter', out_shape=(shape((ROWS, NP...]
    unnamed x14 -> x10, local copies, waits for them, and re-layouts: 6.31 us -> 4.11 us
    pallas_call x1, Pallas kernels: 39.5 us -> 37.7 us  [body(): pl.pallas_call(gather_kernel, name='gather', out_shape=(shape((NP, ROWS,...]
where the time goes in v2:
time: 96.2 us; the launch traced here: 95.9 us
  Pallas kernels  91.1 us (95%)
  local copies, waits for them, and re-layouts  4.11 us (4%)
    pallas_call x1, Pallas kernels, body(): pl.pallas_call(scatter_kernel, name='scatter', out_shape=(shape((ROWS, NP...  41.3 us
    pallas_call x1, Pallas kernels, body(): pl.pallas_call(gather_kernel, name='gather', out_shape=(shape((NP, ROWS,...  37.7 us
    pallas_call x1, Pallas kernels, body(): pl.pallas_call(attend_kernel, name='attend', out_shape=(shape((NP, ROWS,...  12.1 us
    unnamed x10, local copies, waits for them, and re-layouts  4.11 us

profile of v2, /device:TPU:1, one launch (start us, length us, event | category | flops | bytes accessed | tf_op | source)
XLA Modules:
  0.0 95.9 jit_solution(5712212106751966065)
XLA Ops:
  0.6 37.7 %gather.1 = (bf16[8,16,2048]{2,1,0:T(8,128)(2,1)}, bf16[8,16,2048]{2,1,0:T(8,128)(2,1)}, bf16[8,4,8,16,128]{4,3,2,1,0:T(8,128)(2,1)}, bf16[4,8,8,16,128]{4,3,2,1...) custom-call(bf16[16,16384]{1,0:T(8,128)(2,1)} %q_ref.1, bf16[16,1024]{1,0:T(8,128)(2,1)} %k_ref.1, ...), custom_call_target="tpu_custom_call" | custom-call | tf_op jit(solution)/shard_map/gather/pallas_call | solution.py:625
  38.4 12.1 %attend.1 = (bf16[8,16,2048]{2,1,0:T(8,128)(2,1)}, bf16[8,16,2048]{2,1,0:T(8,128)(2,1)}, bf16[8,4,8,16,128]{4,3,2,1,0:T(8,128)(2,1)}, bf16[4,8,8,16,128]{4,3,2,1,0:T(8,128)(2,1)}) custom-call(s32[8,128]{1,0:T(8,128)} %get-tuple-element.14.lists_ref, s32[8]{0:T(128)} %doc_ref.3, bf16[8,16,2048]{2,1,0:T(8,128)(2,1)} %get-tuple-element.15.q_ref, ...), custom_call_target="tpu_custom_call" | custom-call | tf_op jit(solution)/shard_map/attend/pallas_call | solution.py:655
  50.5 41.3 %scatter.1 = (bf16[16,16384]{1,0:T(8,128)(2,1)}, bf16[16,16384]{1,0:T(8,128)(2,1)}, bf16[16,1024]{1,0:T(8,128)(2,1)}, bf16[16,1024]{1,0:T(8,128)(2,1)}) custom-call(bf16[8,16,2048]{2,1,0:T(8,128)(2,1)} %get-tuple-element.19.o_ref, bf16[8,16,2048]{2,1,0:T(8,128)(2,1)} %get-tuple-element.20.dq_ref, bf16[8,4,8,16,128]{4,3,2,1,0:T(8,128)(2,1)} %get-tuple-element.21.dk_ref, ...), custom_call_target="tpu_custom_call" | custom-call | tf_op jit(solution)/shard_map/scatter/pallas_call | solution.py:677
  91.8 0.0 copy-start
  91.8 1.9 %copy.17 = bf16[16,16384]{1,0:T(8,128)(2,1)} copy(bf16[16,16384]{1,0:T(8,128)(2,1)} %get-tuple-element.28) | data formatting | bytes 1048576
  93.7 0.0 copy-done
  93.7 0.0 copy-start.2
  93.7 0.8 copy.18
  94.5 0.0 copy-done.2
  94.5 0.0 copy-start.1
  94.5 0.6 copy.19
  95.1 0.2 copy-done.1
  95.3 0.6 copy.20
Async XLA Ops:
  91.8 1.9 %copy-start = (bf16[16,16384]{1,0:T(8,128)(2,1)S(1)}, bf16[16,16384]{1,0:T(8,128)(2,1)}, u32[]{:S(2)}) copy-start(bf16[16,16384]{1,0:T(8,128)(2,1)} %get-tuple-element.29) | copy-start | bytes 1572868
  93.7 0.8 copy-start.2
  94.5 0.8 copy-start.1

commit v3 on v2

--- a/solution.py
+++ b/solution.py
@@ -76,21 +76,27 @@
     lax.fori_loop(lo, hi, step, 0)
 
 
+def settle(ref, sem):
+    pltpu.make_async_copy(ref, ref, sem).wait()
+
+
 def turn(x, cosine, sine):
     return x * cosine + pltpu.roll(x, HD // 2, 1) * sine
 
 
 def gather_kernel(
     q_ref, k_ref, v_ref, go_ref, doc_ref, pairs_ref, sidx_ref, stab_ref, freq_ref,
-    qx_ref, gox_ref, ka_ref, va_ref, lists_ref, cs_ref,
-    qs, ks, vs,
+    qx_ref, gox_ref, ka_out, va_out, lists_ref, cs_ref,
+    q_in, qs, ks, vs, ka_ref, va_ref,
     q_s, q_r, go_s, go_r, k_s, k_r, v_s, v_r, kzr_s, kzr_r, kzl_s, kzl_r,
-    va_s, va_r, vb_s, vb_r, vy_s, vy_r, own_s,
+    va_s, va_r, vb_s, vb_r, vy_s, vy_r, own_s, kout_s, vout_s,
 ):
     x, y, c, z = place()
     me = NC * x + c
     block = lax.axis_index("ctx")
     barrier = enter(me, x, y, c, z)
+    q_load = pltpu.make_async_copy(q_ref, q_in, own_s.at[0])
+    q_load.start()
 
     token = BLK * block + ROWS * z + lax.broadcasted_iota(jnp.int32, (ROWS, HD), 0)
     start = jnp.zeros((ROWS, HD), jnp.int32)
@@ -115,10 +121,8 @@
     def rotate_q(p):
         for h in range(GRP):
             cols = pl.ds(pl.multiple_of(p * WIDE + h * HD, HD), HD)
-            qs[p, :, h * HD:(h + 1) * HD] = turn(q_ref[:, cols].astype(F32), cosine, sine).astype(BF)
-
-    loop(0, NP, rotate_q)
-    qx_ref[me] = qs[me]
+            qs[p, :, h * HD:(h + 1) * HD] = turn(q_in[:, cols].astype(F32), cosine, sine).astype(BF)
+
     ka_ref[z, y, me] = ks[me]
     va_ref[y, z, me] = vs[me]
 
@@ -127,29 +131,38 @@
     def each_peer(fn):
         loop(1, NP, lambda d: fn((me + d) % NP))
 
-    def k_copy(e, arriving):
+    def k_copy(e, far):
         p, yy = (me + e % NP) % NP, (y + e // NP) % NY
-        ys, slot = (yy, p) if arriving else (y, me)
-        return remote(ks.at[p], ka_ref.at[z, ys, slot], k_s.at[e], k_r.at[ys, slot], peer(p, yy, z))
+        return remote(ks.at[p], ka_ref.at[z, y, me], k_s.at[far], k_r.at[far], peer(p, yy, z))
 
     def v_copy(p, slot):
-        return remote(vs.at[p], va_ref.at[y, z, slot], v_s.at[p], v_r.at[slot], peer(p, y, z))
+        return remote(vs.at[p], va_ref.at[y, z, slot], v_s, v_r, peer(p, y, z))
 
     def go_cols(p):
         return go_ref.at[:, pl.ds(pl.multiple_of(p * WIDE, WIDE), WIDE)]
 
     def go_copy(p, slot):
-        return remote(go_cols(p), gox_ref.at[slot], go_s.at[p], go_r.at[slot], peer(p, y, z))
+        return remote(go_cols(p), gox_ref.at[slot], go_s, go_r, peer(p, y, z))
 
     def q_copy(p, slot):
-        return remote(qs.at[p], qx_ref.at[slot], q_s.at[p], q_r.at[slot], peer(p, y, z))
+        return remote(qs.at[p], qx_ref.at[slot], q_s, q_r, peer(p, y, z))
 
     each_peer(lambda p: v_copy(p, me).start())
-    loop(1, NP * NY, lambda e: k_copy(e, False).start())
+    loop(1, NP, lambda e: k_copy(e, 0).start())
+    loop(NP, NP * NY, lambda e: k_copy(e, 1).start())
     each_peer(lambda p: go_copy(p, me).start())
-    each_peer(lambda p: q_copy(p, me).start())
-    own_go = pltpu.make_async_copy(go_cols(me), gox_ref.at[me], own_s)
+    q_load.wait()
+
+    def rotate_and_send(p):
+        rotate_q(p)
+        q_copy(p, me).start()
+
+    each_peer(rotate_and_send)
+    rotate_q(me)
+    own_go = pltpu.make_async_copy(go_cols(me), gox_ref.at[me], own_s.at[1])
+    own_q = pltpu.make_async_copy(qs.at[me], qx_ref.at[me], own_s.at[2])
     own_go.start()
+    own_q.start()
 
     def along(off):
         return device(x, y, c, (z + off + NZ) % NZ)
@@ -164,6 +177,16 @@
 
     def k_sends(s):
         return [(u, r) for u in range(2) for r in (True, False) if s < 3 or (u == 0) == r]
+
+    def k_store(s, u, rightward):
+        zz = (z + NZ - s) % NZ if rightward else (z + s) % NZ
+        part = pl.ds(u * (NY // 2), NY // 2)
+        return pltpu.make_async_copy(
+            ka_ref.at[zz, part], ka_out.at[zz, part], kout_s.at[s, u if rightward else 1 - u, 0 if rightward else 1]
+        )
+
+    def v_store(yy):
+        return pltpu.make_async_copy(va_ref.at[yy], va_out.at[yy], vout_s.at[yy])
 
     first_hops = (1, -1, 2, -2)
 
@@ -186,19 +209,22 @@
     def v_spread(zz, d, arriving):
         yy = (y + d) % NY
         ys = yy if arriving else y
-        return remote(va_ref.at[ys, zz], va_ref.at[ys, zz], vy_s.at[d, zz], vy_r.at[ys, zz], device(x, yy, c, z))
+        return remote(va_ref.at[ys, zz], va_ref.at[ys, zz], vy_s, vy_r.at[ys], device(x, yy, c, z))
 
     def spread(off):
         for d in (2, 1, 3):
             v_spread((z + off + NZ) % NZ, d, False).start()
 
-    each_peer(lambda p: v_copy(p, p).wait_recv())
+    settle(va_ref.at[y, z, pl.ds(0, NP - 1)], v_r)
     for j in (2, 3, 0, 1):
         v_first(j, False).start()
     spread(0)
-    loop(1, NP * NY, lambda e: k_copy(e, True).wait_recv())
+    settle(ka_ref.at[z, 0, pl.ds(0, NP - 1)], k_r.at[0])
+    settle(ka_ref.at[z, pl.ds(0, NY - 1)], k_r.at[1])
     for u, r in k_sends(0):
         k_ring(0, u, r, True).start()
+    for u in range(2):
+        k_store(0, u, True).start()
 
     lane = lax.broadcasted_iota(jnp.int32, (NP, BLK), 1)
     row = lax.broadcasted_iota(jnp.int32, (NP, BLK), 0)
@@ -238,6 +264,7 @@
             k_ring(s - 1, u, r, False).wait_recv()
             if (u, r) in onward:
                 k_ring(s, u, r, True).start()
+            k_store(s, u, r).start()
 
     for j in (0, 1):
         v_first(j, True).wait_recv()
@@ -254,30 +281,26 @@
     for j in (2, 3):
         v_second(j, True).wait_recv()
     spread(4)
+    v_store(y).start()
     k_step(2)
     k_step(3)
     k_step(4)
 
-    def spread_in(zz):
-        for d in range(1, NY):
-            v_spread(zz, d, True).wait_recv()
-
-    loop(0, NZ, spread_in)
-
-    def qgo_in(p):
-        go_copy(p, p).wait_recv()
-        q_copy(p, p).wait_recv()
-
-    each_peer(qgo_in)
+    for d in (1, 3, 2):
+        settle(va_ref.at[(y + d) % NY], vy_r.at[(y + d) % NY])
+        v_store((y + d) % NY).start()
+
+    settle(gox_ref.at[pl.ds(0, NP - 1)], go_r)
+    settle(qx_ref.at[pl.ds(0, NP - 1)], q_r)
     own_go.wait()
-
-    def sent(p):
-        v_copy(p, me).wait_send()
-        go_copy(p, me).wait_send()
-        q_copy(p, me).wait_send()
-
-    each_peer(sent)
-    loop(1, NP * NY, lambda e: k_copy(e, False).wait_send())
+    own_q.wait()
+
+    settle(vs.at[pl.ds(0, NP - 1)], v_s)
+    settle(go_ref.at[:, pl.ds(0, (NP - 1) * WIDE)], go_s)
+    settle(qs.at[pl.ds(0, NP - 1)], q_s)
+    settle(ks.at[pl.ds(0, NP - 1)], k_s.at[0])
+    settle(ka_ref.at[z, pl.ds(0, NY - 1)], k_s.at[1])
+    settle(va_ref.at[pl.ds(0, NY - 1)], vy_s)
     for s in range(4):
         for u, r in k_sends(s):
             k_ring(s, u, r, True).wait_send()
@@ -285,11 +308,12 @@
         v_first(j, False).wait_send()
         v_second(j, False).wait_send()
 
-    def spread_sent(zz):
-        for d in range(1, NY):
-            v_spread(zz, d, False).wait_send()
-
-    loop(0, NZ, spread_sent)
+    for u in range(2):
+        k_store(0, u, True).wait()
+    for s in range(1, 5):
+        for u, r in k_sends(s - 1):
+            k_store(s, u, r).wait()
+    loop(0, NY, lambda yy: v_store(yy).wait())
 
 
 def heads_to_rows(ref, i):
@@ -304,12 +328,49 @@
 SPAN = CHUNK * BLK
 
 
-def attend_kernel(lists_ref, doc_ref, q_ref, go_ref, k_ref, v_ref, o_ref, dq_ref, dk_ref, dv_ref,
-                  s_ref, dp_ref, o_acc, dq_acc, dk_acc, dv_acc):
+def attend_kernel(
+    lists_ref, doc_ref, q_in, go_in, k_in, v_in, o_out, dq_out, dk_out, dv_out,
+    q_ref, go_ref, k_ref, v_ref, o_ref, dq_ref, dk_ref, dv_ref,
+    s_ref, dp_ref, o_acc, dq_acc, dk_acc, dv_acc,
+    kv_s, q_s, go_s, o_s, dq_s, dk_s, dv_s,
+):
     _, y, _, z = place()
     rows = GRP*ROWS
+
+    def twins(ref, pi):
+        return ref.at[pl.ds(pi*TWIN, TWIN)]
+
+    def q_load(pi):
+        return pltpu.make_async_copy(twins(q_in, pi), twins(q_ref, pi), q_s.at[pi])
+
+    def go_load(pi):
+        return pltpu.make_async_copy(twins(go_in, pi), twins(go_ref, pi), go_s.at[pi])
+
+    def o_store(pi):
+        return pltpu.make_async_copy(twins(o_ref, pi), twins(o_out, pi), o_s.at[pi])
+
+    def dq_store(pi):
+        return pltpu.make_async_copy(twins(dq_ref, pi), twins(dq_out, pi), dq_s.at[pi])
+
+    def dk_store(zz):
+        return pltpu.make_async_copy(dk_ref.at[zz], dk_out.at[zz], dk_s.at[zz])
+
+    def dv_store(yy):
+        return pltpu.make_async_copy(dv_ref.at[yy], dv_out.at[yy], dv_s.at[yy])
+
+    k_load = pltpu.make_async_copy(k_in, k_ref, kv_s.at[0])
+    v_load = pltpu.make_async_copy(v_in, v_ref, kv_s.at[1])
+    q_load(0).start()
+    go_load(0).start()
+    k_load.start()
+    v_load.start()
+    for pi in range(1, NP//TWIN):
+        q_load(pi).start()
+        go_load(pi).start()
     dk_acc[...] = jnp.zeros_like(dk_acc)
     dv_acc[...] = jnp.zeros_like(dv_acc)
+    k_load.wait()
+    v_load.wait()
     key_row = lax.broadcasted_iota(jnp.int32, (BLK, rows), 0)
     lane = lax.broadcasted_iota(jnp.int32, (1, rows), 1)
     nt = (((1,), (1,)), ((), ()))
@@ -320,6 +381,8 @@
         counts = [lists_ref[g, BLK-1] for g in gs]
         most = functools.reduce(jnp.maximum, counts)
         chunks = (most + CHUNK - 1)//CHUNK
+        q_load(pi).wait()
+        go_load(pi).wait()
         queries = [heads_to_rows(q_ref, g) for g in gs]
         grads = [heads_to_rows(go_ref, g) for g in gs]
         tokens, starts = [], []
@@ -410,22 +473,33 @@
         for j in range(TWIN):
             rows_to_heads(o_ref, gs[j], (o_acc[j]*inverses[j]).T.astype(BF))
             rows_to_heads(dq_ref, gs[j], (dq_acc[j]*SCALE).T.astype(BF))
+        o_store(pi).start()
+        dq_store(pi).start()
         return carry
 
     lax.fori_loop(0, NP//TWIN, pair, 0)
 
-    def finish(zz, carry):
+    def finish_k(zz):
         dk_ref[zz] = (dk_acc[zz]*SCALE).astype(BF)
-        for yy in range(NY):
-            dv_ref[yy, zz] = dv_acc[yy, zz].astype(BF)
-        return carry
-    lax.fori_loop(0, NZ, finish, 0)
+        dk_store(zz).start()
+
+    def finish_v(yy):
+        dv_ref[yy] = dv_acc[yy].astype(BF)
+        dv_store(yy).start()
+
+    loop(0, NZ, finish_k)
+    loop(0, NY, finish_v)
+    for pi in range(NP//TWIN):
+        o_store(pi).wait()
+        dq_store(pi).wait()
+    loop(0, NZ, lambda zz: dk_store(zz).wait())
+    loop(0, NY, lambda yy: dv_store(yy).wait())
 
 
 def scatter_kernel(
-    o_ref, dq_ref, dk_ref, dv_ref, cs_ref, sidx_ref, stab_ref,
-    ao_ref, gq_ref, gk_ref, gv_ref,
-    dqx, kr_out, kl_out, kr_in, kl_in, va_out, va_in, vb_out, vb_in, k_out, k_in, vy_in, v_out, v_in,
+    o_ref, dq_ref, dk_hbm, dv_ref, cs_ref, sidx_ref, stab_ref,
+    ao_ref, dqx, gk_ref, gv_ref,
+    dk_ref, dv_own, kr_out, kl_out, kr_in, kl_in, va_out, va_in, vb_out, vb_in, k_out, k_in, vy_in, v_out, v_in,
     o_s, o_r, q_s, q_r, kzr_s, kzr_r, kzl_s, kzl_r, va_s, va_r, vb_s, vb_r,
     vy_s, vy_r, k_s, k_r, v_s, v_r, own_s,
 ):
@@ -433,6 +507,10 @@
     me = NC * x + c
     block = lax.axis_index("ctx")
     barrier = enter(me, x, y, c, z)
+    dk_load = pltpu.make_async_copy(dk_hbm, dk_ref, own_s.at[2])
+    dv_load = pltpu.make_async_copy(dv_ref.at[y], dv_own, own_s.at[3])
+    dk_load.start()
+    dv_load.start()
     pl.semaphore_wait(barrier, N_PARTNERS)
 
     def each_peer(fn):
@@ -445,15 +523,15 @@
         return ref.at[:, pl.ds(pl.multiple_of(g * WIDE, WIDE), WIDE)]
 
     def o_copy(p, slot):
-        return remote(o_ref.at[p], head_cols(ao_ref, slot), o_s.at[p], o_r.at[slot], peer(p, y, z))
+        return remote(o_ref.at[p], head_cols(ao_ref, slot), o_s, o_r, peer(p, y, z))
 
     def q_copy(p, slot):
-        return remote(dq_ref.at[p], dqx.at[slot], q_s.at[p], q_r.at[slot], peer(p, y, z))
+        return remote(dq_ref.at[p], dqx.at[slot], q_s, q_r, peer(p, y, z))
 
     def vy_copy(off, d, arriving):
         zz, yy = (z + off + NZ) % NZ, (y + d) % NY
         slot = yy if arriving else y
-        return remote(dv_ref.at[yy, zz], vy_in.at[slot, zz], vy_s.at[d, zz], vy_r.at[slot, zz], device(x, yy, c, z))
+        return remote(dv_ref.at[yy, zz], vy_in.at[slot, zz], vy_s, vy_r.at[zz], device(x, yy, c, z))
 
     half = NY // 2
 
@@ -476,9 +554,9 @@
 
     def v_part(off):
         zz = (z + off + NZ) % NZ
-        total = dv_ref[y, zz].astype(F32)
+        total = dv_own[zz].astype(F32)
+        settle(dv_own.at[pl.ds(0, NY - 1)], vy_r.at[zz])
         for d in range(1, NY):
-            vy_copy(off, d, True).wait_recv()
             total = total + vy_in[(y + d) % NY, zz].astype(F32)
         return total
 
@@ -496,20 +574,26 @@
     def v_near(j):
         return remote(vb_out.at[j], vb_in.at[j], vb_s.at[j], vb_r.at[j], along(near[j]))
 
+    order = (3, -3, 4, 2, -2, 1, -1, 0)
+    for off in order[:3]:
+        for d in (2, 1, 3):
+            vy_copy(off, d, False).start()
+    dk_load.wait()
     k_send(0, 0, True)
     k_send(0, 1, False)
     k_send(1, 1, True)
     k_send(1, 0, False)
-    order = (3, -3, 4, 2, -2, 1, -1, 0)
-    for off in order:
+    for off in order[3:]:
         for d in (2, 1, 3):
             vy_copy(off, d, False).start()
     each_peer(lambda p: o_copy(p, me).start())
     each_peer(lambda p: q_copy(p, me).start())
-    own_o = pltpu.make_async_copy(o_ref.at[me], head_cols(ao_ref, me), own_s)
+    own_o = pltpu.make_async_copy(o_ref.at[me], head_cols(ao_ref, me), own_s.at[0])
+    own_q = pltpu.make_async_copy(dq_ref.at[me], dqx.at[me], own_s.at[1])
     own_o.start()
-    dqx[me] = dq_ref[me]
-
+    own_q.start()
+
+    dv_load.wait()
     k_send(1, 0, True)
     k_send(1, 1, False)
     va_out[0] = v_part(3).astype(BF)
@@ -540,20 +624,14 @@
     for u, r in ((1, True), (0, False), (0, True), (1, False)):
         k_send(3, u, r)
 
-    def k_copy(e, arriving):
+    def k_copy(e, far):
         p, yy = (me + e % NP) % NP, (y + e // NP) % NY
-        ys, slot = (yy, p) if arriving else (y, me)
-        return remote(k_out.at[yy, p], k_in.at[ys, slot], k_s.at[e], k_r.at[ys, slot], peer(p, yy, z))
+        return remote(k_out.at[yy, p], k_in.at[y, me], k_s.at[far], k_r.at[far], peer(p, yy, z))
 
     def v_copy(p, slot):
-        return remote(v_out.at[p], v_in.at[slot], v_s.at[p], v_r.at[slot], peer(p, y, z))
+        return remote(v_out.at[p], v_in.at[slot], v_s, v_r, peer(p, y, z))
 
     cosine, sine = cs_ref[0], -cs_ref[1]
-
-    def rotate_dq(p):
-        for h in range(GRP):
-            cols = pl.ds(pl.multiple_of(p * WIDE + h * HD, HD), HD)
-            gq_ref[:, cols] = turn(dqx[p, :, h * HD:(h + 1) * HD].astype(F32), cosine, sine).astype(BF)
 
     v_total = v_part(0)
     for j in range(4):
@@ -569,20 +647,15 @@
         total = k_part(z, u) + kr_in[3, u].astype(F32) + kl_in[3, u].astype(F32)
         k_out[u * half:(u + 1) * half] = total.astype(BF)
     k_in[y, me] = k_out[y, me]
-    loop(1, NP * NY, lambda e: k_copy(e, False).start())
-
-    rotate_dq(me)
-
-    def q_in(p):
-        q_copy(p, p).wait_recv()
-        rotate_dq(p)
-
-    each_peer(q_in)
-    each_peer(lambda p: v_copy(p, p).wait_recv())
+    loop(1, NP, lambda e: k_copy(e, 0).start())
+    loop(NP, NP * NY, lambda e: k_copy(e, 1).start())
+
+    settle(v_in.at[pl.ds(0, NP - 1)], v_r)
     for h in range(NP):
         value_scale = stab_ref[1, sidx_ref[1, h, block]]
         gv_ref[:, h * HD:(h + 1) * HD] = (v_in[h].astype(F32) * value_scale).astype(BF)
-    loop(1, NP * NY, lambda e: k_copy(e, True).wait_recv())
+    settle(k_in.at[0, pl.ds(0, NP - 1)], k_r.at[0])
+    settle(k_in.at[pl.ds(0, NY - 1)], k_r.at[1])
     for h in range(NP):
         key_scale = stab_ref[0, sidx_ref[0, h, block]]
         total = k_in[0, h].astype(F32)
@@ -590,16 +663,17 @@
             total = total + k_in[yy, h].astype(F32)
         gk_ref[:, h * HD:(h + 1) * HD] = (turn(total, cosine, sine) * key_scale).astype(BF)
 
-    each_peer(lambda p: o_copy(p, p).wait_recv())
+    settle(o_ref.at[pl.ds(0, NP - 1)], o_r)
+    settle(dqx.at[pl.ds(0, NP - 1)], q_r)
     own_o.wait()
-
-    def sent(p):
-        o_copy(p, me).wait_send()
-        q_copy(p, me).wait_send()
-        v_copy(p, me).wait_send()
-
-    each_peer(sent)
-    loop(1, NP * NY, lambda e: k_copy(e, False).wait_send())
+    own_q.wait()
+
+    settle(o_ref.at[pl.ds(0, NP - 1)], o_s)
+    settle(dq_ref.at[pl.ds(0, NP - 1)], q_s)
+    settle(v_out.at[pl.ds(0, NP - 1)], v_s)
+    settle(k_out.at[0, pl.ds(0, NP - 1)], k_s.at[0])
+    settle(k_out.at[pl.ds(0, NY - 1)], k_s.at[1])
+    settle(dv_ref.at[pl.ds(0, NY - 1)], vy_s)
     for s in range(4):
         for u in range(2):
             for r in (True, False):
@@ -608,9 +682,31 @@
     for j in range(4):
         v_far(j).wait_send()
         v_near(j).wait_send()
-    for off in order:
-        for d in (2, 1, 3):
-            vy_copy(off, d, False).wait_send()
+
+
+def finish_kernel(ao_in, dqx_ref, gk_in, gv_in, cs_ref, ao_out, gq_out, gk_out, gv_out, gq_ref, sems, gq_s):
+    copies = [
+        pltpu.make_async_copy(src, dst, sems.at[i])
+        for i, (src, dst) in enumerate(((ao_in, ao_out), (gk_in, gk_out), (gv_in, gv_out)))
+    ]
+    for copy in copies:
+        copy.start()
+    cosine, sine = cs_ref[0], -cs_ref[1]
+
+    def store(p):
+        cols = pl.ds(pl.multiple_of(p * WIDE, WIDE), WIDE)
+        return pltpu.make_async_copy(gq_ref.at[:, cols], gq_out.at[:, cols], gq_s.at[p])
+
+    def rotate_back(p):
+        for h in range(GRP):
+            cols = pl.ds(pl.multiple_of(p * WIDE + h * HD, HD), HD)
+            gq_ref[:, cols] = turn(dqx_ref[p, :, h * HD:(h + 1) * HD].astype(F32), cosine, sine).astype(BF)
+        store(p).start()
+
+    loop(0, NP, rotate_back)
+    for copy in copies:
+        copy.wait()
+    loop(0, NP, lambda p: store(p).wait())
 
 
 def body(queries, keys, values, grad_out, doc_lengths, block_pairs, scale_index, scale_table):
@@ -619,6 +715,7 @@
     freq = jnp.asarray(np.tile(np.concatenate([freq, freq])[None], (8, 1)))
     scale_by_head = scale_index.transpose(0, 2, 1)
     vmem = pl.BlockSpec(memory_space=pltpu.VMEM)
+    anywhere = pl.BlockSpec(memory_space=pl.ANY)
     smem = pl.BlockSpec(memory_space=pltpu.SMEM)
     dma = pltpu.SemaphoreType.DMA
     shape = jax.ShapeDtypeStruct
@@ -633,20 +730,23 @@
             shape((NP, BLK), jnp.int32),
             shape((2, ROWS, HD), F32),
         ),
-        in_specs=[vmem] * 4 + [smem, vmem, smem, smem, vmem],
-        out_specs=(vmem,) * 6,
+        in_specs=[anywhere, vmem, vmem, anywhere, smem, vmem, smem, smem, vmem],
+        out_specs=(anywhere,) * 4 + (vmem,) * 2,
         scratch_shapes=[
+            pltpu.VMEM((ROWS, NP * WIDE), BF),
             pltpu.VMEM((NP, ROWS, WIDE), BF),
             pltpu.VMEM((NP, ROWS, HD), BF),
             pltpu.VMEM((NP, ROWS, HD), BF),
+            pltpu.VMEM((NZ, NY, NP, ROWS, HD), BF),
+            pltpu.VMEM((NY, NZ, NP, ROWS, HD), BF),
         ]
-        + [dma((NP,))] * 4
-        + [dma((NP * NY,)), dma((NY, NP))]
-        + [dma((NP,))] * 2
+        + [dma] * 4
+        + [dma((2,))] * 2
+        + [dma] * 2
         + [dma((4, 2))] * 4
         + [dma((4,))] * 4
-        + [dma((NY, NZ))] * 2
-        + [dma],
+        + [dma, dma((NY,))]
+        + [dma((3,)), dma((5, 2, 2)), dma((NY,))],
         compiler_params=pltpu.CompilerParams(
             collective_id=0, has_side_effects=True, vmem_limit_bytes=VMEM_LIMIT
         ),
@@ -661,48 +761,68 @@
             shape((NZ, NY, NP, ROWS, HD), BF),
             shape((NY, NZ, NP, ROWS, HD), BF),
         ),
-        in_specs=[smem, smem] + [vmem] * 4,
-        out_specs=(vmem,) * 4,
-        scratch_shapes=[
+        in_specs=[smem, smem] + [anywhere] * 4,
+        out_specs=(anywhere,) * 4,
+        scratch_shapes=([pltpu.VMEM((NP, ROWS, WIDE), BF)] * 2
+        + [pltpu.VMEM((NZ, NY, NP, ROWS, HD), BF), pltpu.VMEM((NY, NZ, NP, ROWS, HD), BF)]) * 2
+        + [
             pltpu.VMEM((TWIN, NBLK // CHUNK, SPAN, GRP * ROWS), F32),
             pltpu.VMEM((TWIN, NBLK // CHUNK, SPAN, GRP * ROWS), F32),
             pltpu.VMEM((TWIN, HD, GRP * ROWS), F32),
             pltpu.VMEM((TWIN, HD, GRP * ROWS), F32),
             pltpu.VMEM((NZ, NY, NP, ROWS, HD), F32),
             pltpu.VMEM((NY, NZ, NP, ROWS, HD), F32),
-        ],
+        ]
+        + [dma((2,))]
+        + [dma((NP // TWIN,))] * 4
+        + [dma((NZ,)), dma((NY,))],
         compiler_params=pltpu.CompilerParams(vmem_limit_bytes=VMEM_LIMIT),
     )(lists, doc_lengths, qx, gox, ka, va)
 
-    return pl.pallas_call(
+    ao, dqx, gk, gv = pl.pallas_call(
         scatter_kernel,
         name="scatter",
+        out_shape=(
+            shape((ROWS, NP * WIDE), BF),
+            shape((NP, ROWS, WIDE), BF),
+            shape((ROWS, NP * HD), BF),
+            shape((ROWS, NP * HD), BF),
+        ),
+        in_specs=[anywhere] * 4 + [vmem, smem, smem],
+        out_specs=(anywhere,) * 2 + (vmem,) * 2,
+        scratch_shapes=[pltpu.VMEM((NZ, NY, NP, ROWS, HD), BF), pltpu.VMEM((NZ, NP, ROWS, HD), BF)]
+        + [pltpu.VMEM((4, 2, NY // 2, NP, ROWS, HD), BF)] * 4
+        + [pltpu.VMEM((3, NP, ROWS, HD), BF)] * 2
+        + [pltpu.VMEM((4, NP, ROWS, HD), BF)] * 2
+        + [pltpu.VMEM((NY, NP, ROWS, HD), BF)] * 2
+        + [pltpu.VMEM((NY, NZ, NP, ROWS, HD), BF)]
+        + [pltpu.VMEM((NP, ROWS, HD), BF)] * 2
+        + [dma] * 4
+        + [dma((4, 2))] * 4
+        + [dma((4,))] * 4
+        + [dma, dma((NZ,))]
+        + [dma((2,))] * 2
+        + [dma] * 2
+        + [dma((4,))],
+        compiler_params=pltpu.CompilerParams(
+            collective_id=1, has_side_effects=True, vmem_limit_bytes=VMEM_LIMIT
+        ),
+    )(o, dq, dk, dv, cs, scale_by_head, scale_table)
+
+    return pl.pallas_call(
+        finish_kernel,
+        name="finish",
         out_shape=(
             shape((ROWS, NP * WIDE), BF),
             shape((ROWS, NP * WIDE), BF),
             shape((ROWS, NP * HD), BF),
             shape((ROWS, NP * HD), BF),
         ),
-        in_specs=[vmem] * 5 + [smem, smem],
-        out_specs=(vmem,) * 4,
-        scratch_shapes=[pltpu.VMEM((NP, ROWS, WIDE), BF)]
-        + [pltpu.VMEM((4, 2, NY // 2, NP, ROWS, HD), BF)] * 4
-        + [pltpu.VMEM((3, NP, ROWS, HD), BF)] * 2
-        + [pltpu.VMEM((4, NP, ROWS, HD), BF)] * 2
-        + [pltpu.VMEM((NY, NP, ROWS, HD), BF)] * 2
-        + [pltpu.VMEM((NY, NZ, NP, ROWS, HD), BF)]
-        + [pltpu.VMEM((NP, ROWS, HD), BF)] * 2
-        + [dma((NP,))] * 4
-        + [dma((4, 2))] * 4
-        + [dma((4,))] * 4
-        + [dma((NY, NZ))] * 2
-        + [dma((NP * NY,)), dma((NY, NP))]
-        + [dma((NP,))] * 2
-        + [dma],
-        compiler_params=pltpu.CompilerParams(
-            collective_id=1, has_side_effects=True, vmem_limit_bytes=VMEM_LIMIT
-        ),
-    )(o, dq, dk, dv, cs, scale_by_head, scale_table)
+        in_specs=[vmem] * 5,
+        out_specs=(anywhere,) * 4,
+        scratch_shapes=[pltpu.VMEM((ROWS, NP * WIDE), BF), dma((3,)), dma((NP,))],
+        compiler_params=pltpu.CompilerParams(vmem_limit_bytes=VMEM_LIMIT),
+    )(ao, dqx, gk, gv, cs)
 
 
 def solution(mesh):

time: 96.2 us -> 86.8 us (0.902)
  Pallas kernels: 91.1 us -> 85.8 us
  local copies, waits for them, and re-layouts: 4.11 us -> 0 us
    pallas_call x1, Pallas kernels: 41.3 us -> 33.8 us  [body(): pl.pallas_call(scatter_kernel, name='scatter', out_shape=(shape((ROWS, NP...]
    unnamed x10 -> x0, local copies, waits for them, and re-layouts: 4.11 us -> none
    pallas_call x0 -> x1, Pallas kernels: none -> 2.68 us  [body(): pl.pallas_call(finish_kernel, name='finish', out_shape=(shape((ROWS, NP *...]
    pallas_call x1, Pallas kernels: 37.7 us -> 35.6 us  [body(): pl.pallas_call(gather_kernel, name='gather', out_shape=(shape((NP, ROWS,...]
    pallas_call x1, Pallas kernels: 12.1 us -> 13.7 us  [body(): pl.pallas_call(attend_kernel, name='attend', out_shape=(shape((NP, ROWS,...]
where the time goes in v3:
time: 86.8 us; the launch traced here: 86.4 us
  Pallas kernels  85.8 us (99%)
    pallas_call x1, Pallas kernels, body(): pl.pallas_call(gather_kernel, name='gather', out_shape=(shape((NP, ROWS,...  35.6 us
    pallas_call x1, Pallas kernels, body(): pl.pallas_call(scatter_kernel, name='scatter', out_shape=(shape((ROWS, NP...  33.8 us
    pallas_call x1, Pallas kernels, body(): pl.pallas_call(attend_kernel, name='attend', out_shape=(shape((NP, ROWS,...  13.7 us
    pallas_call x1, Pallas kernels, body(): pl.pallas_call(finish_kernel, name='finish', out_shape=(shape((ROWS, NP *...  2.68 us

profile of v3, /device:TPU:1, one launch (start us, length us, event | category | flops | bytes accessed | tf_op | source)
XLA Modules:
  0.0 86.4 jit_solution(16756132478073355838)
XLA Ops:
  0.6 35.6 %gather.1 = (bf16[8,16,2048]{2,1,0:T(8,128)(2,1)}, bf16[8,16,2048]{2,1,0:T(8,128)(2,1)}, bf16[8,4,8,16,128]{4,3,2,1,0:T(8,128)(2,1)}, bf16[4,8,8,16,128]{4,3,2,1...) custom-call(bf16[16,16384]{1,0:T(8,128)(2,1)} %q_ref.1, bf16[16,1024]{1,0:T(8,128)(2,1)} %k_ref.1, ...), custom_call_target="tpu_custom_call" | custom-call | tf_op jit(solution)/shard_map/gather/pallas_call | solution.py:722
  36.2 13.7 %attend.1 = (bf16[8,16,2048]{2,1,0:T(8,128)(2,1)}, bf16[8,16,2048]{2,1,0:T(8,128)(2,1)}, bf16[8,4,8,16,128]{4,3,2,1,0:T(8,128)(2,1)}, bf16[4,8,8,16,128]{4,3,2,1,0:T(8,128)(2,1)}) custom-call(s32[8,128]{1,0:T(8,128)} %get-tuple-element.18.lists_ref, s32[8]{0:T(128)} %doc_ref.3, bf16[8,16,2048]{2,1,0:T(8,128)(2,1)} %get-tuple-element.19.q_in, ...), custom_call_target="tpu_custom_call" | custom-call | tf_op jit(solution)/shard_map/attend/pallas_call | solution.py:755
  49.9 33.8 %scatter.1 = (bf16[16,16384]{1,0:T(8,128)(2,1)}, bf16[8,16,2048]{2,1,0:T(8,128)(2,1)}, bf16[16,1024]{1,0:T(8,128)(2,1)}, bf16[16,1024]{1,0:T(8,128)(2,1)}) custom-call(bf16[8,16,2048]{2,1,0:T(8,128)(2,1)} %get-tuple-element.23.o_ref, bf16[8,16,2048]{2,1,0:T(8,128)(2,1)} %get-tuple-element.24.dq_ref, bf16[8,4,8,16,128]{4,3,2,1,0:T(8,128)(2,1)} %get-tuple-element.25.dk_hbm, ...), custom_call_target="tpu_custom_call" | custom-call | tf_op jit(solution)/shard_map/scatter/pallas_call | solution.py:782
  83.8 2.7 %finish.1 = (bf16[16,16384]{1,0:T(8,128)(2,1)}, bf16[16,16384]{1,0:T(8,128)(2,1)}, bf16[16,1024]{1,0:T(8,128)(2,1)}, bf16[16,1024]{1,0:T(8,128)(2,1)}) custom-call(bf16[16,16384]{1,0:T(8,128)(2,1)} %get-tuple-element.28.ao_in, bf16[8,16,2048]{2,1,0:T(8,128)(2,1)} %get-tuple-element.29.dqx_ref, bf16[16,1024]{1,0:T(8,128)(2,1)} %get-tuple-element.30.gk_in, ...), custom_call_target="tpu_custom_call" | custom-call | tf_op jit(solution)/shard_map/finish/pallas_call | solution.py:812

commit v4 on v3

--- a/solution.py
+++ b/solution.py
@@ -19,8 +19,7 @@
 NDOC = 8
 WIDE = GRP * HD
 NEG = -1e30
-CHUNK = 4
-TWIN = 2
+UNROLL = 6
 SCALE = 1.0 / math.sqrt(HD)
 EXP2_SCALE = SCALE * math.log2(math.e)
 MESH = pl.DeviceIdType.MESH
@@ -85,18 +84,29 @@
 
 
 def gather_kernel(
-    q_ref, k_ref, v_ref, go_ref, doc_ref, pairs_ref, sidx_ref, stab_ref, freq_ref,
-    qx_ref, gox_ref, ka_out, va_out, lists_ref, cs_ref,
-    q_in, qs, ks, vs, ka_ref, va_ref,
+    q_ref, k_hbm, v_hbm, go_ref, doc_hbm, pairs_hbm, sidx_hbm, stab_hbm, freq_hbm,
+    qx_ref, gox_ref, ka_out, va_out, lists_out, cs_out,
+    k_ref, v_ref, doc_ref, pairs_ref, sidx_ref, stab_ref, freq_ref, lists_ref, cs_ref, q_in, qs, ks, vs, ka_ref, va_ref,
     q_s, q_r, go_s, go_r, k_s, k_r, v_s, v_r, kzr_s, kzr_r, kzl_s, kzl_r,
-    va_s, va_r, vb_s, vb_r, vy_s, vy_r, own_s, kout_s, vout_s,
+    va_s, va_r, vb_s, vb_r, vy_s, vy_r, own_s, kout_s, vout_s, load_s,
 ):
     x, y, c, z = place()
     me = NC * x + c
     block = lax.axis_index("ctx")
-    barrier = enter(me, x, y, c, z)
+    loads = [
+        pltpu.make_async_copy(src, dst, load_s.at[n])
+        for n, (src, dst) in enumerate((
+            (doc_hbm, doc_ref), (freq_hbm, freq_ref), (k_hbm, k_ref), (v_hbm, v_ref),
+            (sidx_hbm, sidx_ref), (stab_hbm, stab_ref), (pairs_hbm, pairs_ref),
+        ))
+    ]
+    for load in loads:
+        load.start()
     q_load = pltpu.make_async_copy(q_ref, q_in, own_s.at[0])
     q_load.start()
+    barrier = enter(me, x, y, c, z)
+    for load in loads:
+        load.wait()
 
     token = BLK * block + ROWS * z + lax.broadcasted_iota(jnp.int32, (ROWS, HD), 0)
     start = jnp.zeros((ROWS, HD), jnp.int32)
@@ -110,6 +120,8 @@
     sine = jnp.where(lax.broadcasted_iota(jnp.int32, (ROWS, HD), 1) < HD // 2, -sine, sine)
     cs_ref[0] = cosine
     cs_ref[1] = sine
+    cs_store = pltpu.make_async_copy(cs_ref, cs_out, own_s.at[3])
+    cs_store.start()
 
     for h in range(NP):
         cols = slice(h * HD, (h + 1) * HD)
@@ -257,6 +269,8 @@
     out = lax.fori_loop(0, NBLK, list_step, jnp.zeros((NP, BLK), F32))
     out = jnp.where(lane == BLK - 1, jnp.sum(wanted_f, axis=1, keepdims=True), out)
     lists_ref[...] = out.astype(jnp.int32)
+    lists_store = pltpu.make_async_copy(lists_ref, lists_out, own_s.at[4])
+    lists_store.start()
 
     def k_step(s):
         onward = k_sends(s) if s < 4 else []
@@ -294,6 +308,8 @@
     settle(qx_ref.at[pl.ds(0, NP - 1)], q_r)
     own_go.wait()
     own_q.wait()
+    cs_store.wait()
+    lists_store.wait()
 
     settle(vs.at[pl.ds(0, NP - 1)], v_s)
     settle(go_ref.at[:, pl.ds(0, (NP - 1) * WIDE)], go_s)
@@ -325,32 +341,35 @@
         ref[i, :, h * HD:(h + 1) * HD] = rows[h * ROWS:(h + 1) * ROWS]
 
 
-SPAN = CHUNK * BLK
+WIDTH = 2
+SPAN = WIDTH * BLK
+MOST_UNITS = NP * (NBLK // 2 // WIDTH + 1)
 
 
 def attend_kernel(
-    lists_ref, doc_ref, q_in, go_in, k_in, v_in, o_out, dq_out, dk_out, dv_out,
-    q_ref, go_ref, k_ref, v_ref, o_ref, dq_ref, dk_ref, dv_ref,
-    s_ref, dp_ref, o_acc, dq_acc, dk_acc, dv_acc,
-    kv_s, q_s, go_s, o_s, dq_s, dk_s, dv_s,
+    lists_in, doc_in, q_in, go_in, k_in, v_in, o_out, dq_out, dk_out, dv_out,
+    lists_ref, doc_ref, q_ref, go_ref, k_ref, v_ref, o_ref, dq_ref, dk_ref, dv_ref,
+    s_ref, dp_ref, o_acc, dq_acc, dk_acc, dv_acc, bounds_ref, top_ref, total_ref, mean_ref, flat_ref,
+    load_s, o_s, dq_s, dk_s, dv_s,
 ):
     _, y, _, z = place()
-    rows = GRP*ROWS
-
-    def twins(ref, pi):
-        return ref.at[pl.ds(pi*TWIN, TWIN)]
-
-    def q_load(pi):
-        return pltpu.make_async_copy(twins(q_in, pi), twins(q_ref, pi), q_s.at[pi])
-
-    def go_load(pi):
-        return pltpu.make_async_copy(twins(go_in, pi), twins(go_ref, pi), go_s.at[pi])
-
-    def o_store(pi):
-        return pltpu.make_async_copy(twins(o_ref, pi), twins(o_out, pi), o_s.at[pi])
-
-    def dq_store(pi):
-        return pltpu.make_async_copy(twins(dq_ref, pi), twins(dq_out, pi), dq_s.at[pi])
+    rows = GRP * ROWS
+    loads = [
+        pltpu.make_async_copy(src, dst, load_s.at[n])
+        for n, (src, dst) in enumerate(((q_in, q_ref), (k_in, k_ref), (go_in, go_ref), (v_in, v_ref)))
+    ]
+    small = [
+        pltpu.make_async_copy(src, dst, load_s.at[n])
+        for n, (src, dst) in ((4, (lists_in, lists_ref)), (5, (doc_in, doc_ref)))
+    ]
+    for load in small + loads:
+        load.start()
+
+    def o_store(g):
+        return pltpu.make_async_copy(o_ref.at[g], o_out.at[g], o_s.at[g])
+
+    def dq_store(g):
+        return pltpu.make_async_copy(dq_ref.at[g], dq_out.at[g], dq_s.at[g])
 
     def dk_store(zz):
         return pltpu.make_async_copy(dk_ref.at[zz], dk_out.at[zz], dk_s.at[zz])
@@ -358,129 +377,113 @@
     def dv_store(yy):
         return pltpu.make_async_copy(dv_ref.at[yy], dv_out.at[yy], dv_s.at[yy])
 
-    k_load = pltpu.make_async_copy(k_in, k_ref, kv_s.at[0])
-    v_load = pltpu.make_async_copy(v_in, v_ref, kv_s.at[1])
-    q_load(0).start()
-    go_load(0).start()
-    k_load.start()
-    v_load.start()
-    for pi in range(1, NP//TWIN):
-        q_load(pi).start()
-        go_load(pi).start()
-    dk_acc[...] = jnp.zeros_like(dk_acc)
-    dv_acc[...] = jnp.zeros_like(dv_acc)
-    k_load.wait()
-    v_load.wait()
+    for ref in (total_ref, mean_ref, o_acc, dq_acc, dk_acc, dv_acc):
+        ref[...] = jnp.zeros_like(ref)
+    top_ref[...] = jnp.full_like(top_ref, NEG)
+    for load in small:
+        load.wait()
+
+    def list_group(g, base):
+        count = (lists_ref[g, BLK - 1] + WIDTH - 1) // WIDTH
+
+        def put(n):
+            flat_ref[base + n] = n * NP + g
+
+        loop(0, count, put)
+        return base + count
+
+    units = lax.fori_loop(0, NP, list_group, 0)
+    for u in range(UNROLL):
+        flat_ref[units + u] = NBLK * NP
+    steps = (units + UNROLL - 1) // UNROLL
+
+    lane = lax.broadcasted_iota(jnp.int32, (1, rows), 1)
+    for g in range(NP):
+        token = BLK * (NY * NC * (g // NC) + NC * y + g % NC) + ROWS * z + lane % ROWS
+        start = jnp.zeros((1, rows), jnp.int32)
+        end = 0
+        for d in range(NDOC):
+            end = end + doc_ref[d]
+            start = start + jnp.where(token >= end, doc_ref[d], 0)
+        bounds_ref[g, 0:1] = start
+        bounds_ref[g, 1:2] = token
     key_row = lax.broadcasted_iota(jnp.int32, (BLK, rows), 0)
-    lane = lax.broadcasted_iota(jnp.int32, (1, rows), 1)
     nt = (((1,), (1,)), ((), ()))
     tn = (((0,), (0,)), ((), ()))
-
-    def pair(pi, carry):
-        gs = [pi*TWIN+j for j in range(TWIN)]
-        counts = [lists_ref[g, BLK-1] for g in gs]
-        most = functools.reduce(jnp.maximum, counts)
-        chunks = (most + CHUNK - 1)//CHUNK
-        q_load(pi).wait()
-        go_load(pi).wait()
-        queries = [heads_to_rows(q_ref, g) for g in gs]
-        grads = [heads_to_rows(go_ref, g) for g in gs]
-        tokens, starts = [], []
-        for g in gs:
-            own = NY*NC*(g//NC) + NC*y + g%NC
-            token = BLK*own + ROWS*z + lane%ROWS
-            start = jnp.zeros((1, rows), jnp.int32)
-            end = 0
-            for d in range(NDOC):
-                end = end + doc_ref[d]
-                start = start + jnp.where(token >= end, doc_ref[d], 0)
-            tokens.append(token); starts.append(start)
-
-        def spots(j, n):
-            out = []
-            for u in range(CHUNK):
-                t = n*CHUNK + u
-                b = lists_ref[gs[j], t]
-                out.append((t < counts[j], b, (b//NC)%NY, (b//(NY*NC))*NC + b%NC))
-            return out
-
-        def keys_of(sp):
-            return jnp.concatenate([k_ref[:, yb, ib].reshape(BLK, HD) for _, _, yb, ib in sp], axis=0)
-
-        def values_of(sp):
-            return jnp.concatenate([v_ref[yb, :, ib].reshape(BLK, HD) for _, _, yb, ib in sp], axis=0)
-
-        def fold(x):
-            return x.reshape(SPAN//8, 8, rows)
-
-        def score_step(n, tops):
-            out = []
-            for j in range(TWIN):
-                sp = spots(j, n)
-                scores = lax.dot_general(keys_of(sp), queries[j], nt, preferred_element_type=F32)
-                dp_ref[j, n] = lax.dot_general(values_of(sp), grads[j], nt, preferred_element_type=F32)
-                top = tops[j]
-                for u, (live, b, _, _) in enumerate(sp):
-                    low = jnp.where(live, starts[j] - BLK*b, BLK)
-                    allowed = (key_row >= low) & (key_row <= tokens[j] - BLK*b)
-                    part = jnp.where(allowed, scores[u*BLK:(u+1)*BLK], NEG)
-                    s_ref[j, n, u*BLK:(u+1)*BLK] = part
-                    top = jnp.maximum(top, jnp.max(part.reshape(BLK//8, 8, rows), axis=0))
-                out.append(top)
-            return tuple(out)
-
-        tops = lax.fori_loop(0, chunks, score_step, tuple(jnp.full((8, rows), NEG, F32) for _ in gs))
-        tops = [jnp.max(t, axis=0, keepdims=True) for t in tops]
-        for j in range(TWIN):
-            o_acc[j] = jnp.zeros((HD, rows), F32)
-            dq_acc[j] = jnp.zeros((HD, rows), F32)
-
-        def out_step(n, carry):
-            out = []
-            for j in range(TWIN):
-                total, mean = carry[j]
-                sp = spots(j, n)
-                weights = jnp.exp2((s_ref[j, n] - tops[j])*EXP2_SCALE)
-                s_ref[j, n] = weights
-                total = total + jnp.sum(fold(weights), axis=0)
-                mean = mean + jnp.sum(fold(weights*dp_ref[j, n]), axis=0)
-                o_acc[j] += lax.dot_general(values_of(sp), weights.astype(BF), tn, preferred_element_type=F32)
-                out.append((total, mean))
-            return tuple(out)
-
-        zero = jnp.zeros((8, rows), F32)
-        sums = lax.fori_loop(0, chunks, out_step, tuple((zero, zero) for _ in gs))
-        inverses, deltas = [], []
-        for j in range(TWIN):
-            inverse = 1.0/jnp.sum(sums[j][0], axis=0, keepdims=True)
-            inverses.append(inverse)
-            deltas.append(jnp.sum(sums[j][1], axis=0, keepdims=True)*inverse)
-
-        def grad_step(n, carry):
-            for j in range(TWIN):
-                sp = spots(j, n)
-                probs = s_ref[j, n]*inverses[j]
-                grad_scores = (probs*(dp_ref[j, n] - deltas[j])).astype(BF)
-                dv = jnp.dot(probs.astype(BF), grads[j], preferred_element_type=F32)
-                dk = jnp.dot(grad_scores, queries[j], preferred_element_type=F32)
-                dq_acc[j] += lax.dot_general(keys_of(sp), grad_scores, tn, preferred_element_type=F32)
-                for u, (_, _, yb, ib) in enumerate(sp):
-                    dv_acc[yb, :, ib] += dv[u*BLK:(u+1)*BLK].reshape(NZ, ROWS, HD)
-                    dk_acc[:, yb, ib] += dk[u*BLK:(u+1)*BLK].reshape(NZ, ROWS, HD)
-            return carry
-
-        lax.fori_loop(0, chunks, grad_step, 0)
-        for j in range(TWIN):
-            rows_to_heads(o_ref, gs[j], (o_acc[j]*inverses[j]).T.astype(BF))
-            rows_to_heads(dq_ref, gs[j], (dq_acc[j]*SCALE).T.astype(BF))
-        o_store(pi).start()
-        dq_store(pi).start()
-        return carry
-
-    lax.fori_loop(0, NP//TWIN, pair, 0)
+    for load in loads:
+        load.wait()
+
+    def units_of(n):
+        out = []
+        for u in range(UNROLL):
+            entry = flat_ref[n * UNROLL + u]
+            g, first = entry % NP, entry // NP * WIDTH
+            count = lists_ref[g, BLK - 1]
+            parts = []
+            for w in range(WIDTH):
+                live = first + w < count
+                b = lists_ref[g, jnp.where(live, first + w, 0)]
+                parts.append((live, b, (b // NC) % NY, (b // (NY * NC)) * NC + b % NC))
+            out.append((n * UNROLL + u, g, parts))
+        return out
+
+    def keys_at(parts):
+        return jnp.concatenate([k_ref[:, yb, ib].reshape(BLK, HD) for _, _, yb, ib in parts], axis=0)
+
+    def values_at(parts):
+        return jnp.concatenate([v_ref[yb, :, ib].reshape(BLK, HD) for _, _, yb, ib in parts], axis=0)
+
+    def fold(x):
+        return x.reshape(x.shape[0] // 8, 8, rows)
+
+    def score_step(n):
+        for t, g, parts in units_of(n):
+            scores = lax.dot_general(keys_at(parts), heads_to_rows(q_ref, g), nt, preferred_element_type=F32)
+            dp_ref[t] = lax.dot_general(values_at(parts), heads_to_rows(go_ref, g), nt, preferred_element_type=F32)
+            top = top_ref[g]
+            for w, (live, b, _, _) in enumerate(parts):
+                low = jnp.where(live, bounds_ref[g, 0:1] - BLK * b, BLK)
+                allowed = (key_row >= low) & (key_row <= bounds_ref[g, 1:2] - BLK * b)
+                part = jnp.where(allowed, scores[w * BLK:(w + 1) * BLK], NEG)
+                s_ref[t, w * BLK:(w + 1) * BLK] = part
+                top = jnp.maximum(top, jnp.max(fold(part), axis=0))
+            top_ref[g] = top
+
+    loop(0, steps, score_step)
+    for g in range(NP):
+        top_ref[g] = jnp.broadcast_to(jnp.max(top_ref[g], axis=0, keepdims=True), (8, rows))
+
+    def out_step(n):
+        for t, g, parts in units_of(n):
+            weights = jnp.exp2((s_ref[t] - top_ref[g, 0:1]) * EXP2_SCALE)
+            s_ref[t] = weights
+            total_ref[g] += jnp.sum(fold(weights), axis=0)
+            mean_ref[g] += jnp.sum(fold(weights * dp_ref[t]), axis=0)
+            o_acc[g] += lax.dot_general(values_at(parts), weights.astype(BF), tn, preferred_element_type=F32)
+
+    loop(0, steps, out_step)
+    for g in range(NP):
+        inverse = 1.0 / jnp.sum(total_ref[g], axis=0, keepdims=True)
+        total_ref[g, 0:1] = inverse
+        mean_ref[g, 0:1] = jnp.sum(mean_ref[g], axis=0, keepdims=True) * inverse
+        rows_to_heads(o_ref, g, (o_acc[g] * inverse).astype(BF).T)
+        o_store(g).start()
+
+    def grad_step(n):
+        for t, g, parts in units_of(n):
+            probs = s_ref[t] * total_ref[g, 0:1]
+            grad_scores = (probs * (dp_ref[t] - mean_ref[g, 0:1])).astype(BF)
+            dv = jnp.dot(probs.astype(BF), heads_to_rows(go_ref, g), preferred_element_type=F32)
+            dk = jnp.dot(grad_scores, heads_to_rows(q_ref, g), preferred_element_type=F32)
+            dq_acc[g] += lax.dot_general(keys_at(parts), grad_scores, tn, preferred_element_type=F32)
+            for w, (_, _, yb, ib) in enumerate(parts):
+                dv_acc[yb, :, ib] += dv[w * BLK:(w + 1) * BLK].reshape(NZ, ROWS, HD)
+                dk_acc[:, yb, ib] += dk[w * BLK:(w + 1) * BLK].reshape(NZ, ROWS, HD)
+
+    loop(0, steps, grad_step)
 
     def finish_k(zz):
-        dk_ref[zz] = (dk_acc[zz]*SCALE).astype(BF)
+        dk_ref[zz] = (dk_acc[zz] * SCALE).astype(BF)
         dk_store(zz).start()
 
     def finish_v(yy):
@@ -489,28 +492,30 @@
 
     loop(0, NZ, finish_k)
     loop(0, NY, finish_v)
-    for pi in range(NP//TWIN):
-        o_store(pi).wait()
-        dq_store(pi).wait()
+    for g in range(NP):
+        rows_to_heads(dq_ref, g, (dq_acc[g] * SCALE).astype(BF).T)
+        dq_store(g).start()
+    for g in range(NP):
+        o_store(g).wait()
+        dq_store(g).wait()
     loop(0, NZ, lambda zz: dk_store(zz).wait())
     loop(0, NY, lambda yy: dv_store(yy).wait())
 
 
 def scatter_kernel(
-    o_ref, dq_ref, dk_hbm, dv_ref, cs_ref, sidx_ref, stab_ref,
-    ao_ref, dqx, gk_ref, gv_ref,
-    dk_ref, dv_own, kr_out, kl_out, kr_in, kl_in, va_out, va_in, vb_out, vb_in, k_out, k_in, vy_in, v_out, v_in,
+    o_ref, dq_ref, dk_hbm, dv_ref,
+    ao_ref, dqx, k_in, v_in,
+    dk_ref, dv_own, kr_out, kl_out, kr_in, kl_in, va_out, va_in, vb_out, vb_in, k_out, vy_in, v_out,
     o_s, o_r, q_s, q_r, kzr_s, kzr_r, kzl_s, kzl_r, va_s, va_r, vb_s, vb_r,
     vy_s, vy_r, k_s, k_r, v_s, v_r, own_s,
 ):
     x, y, c, z = place()
     me = NC * x + c
-    block = lax.axis_index("ctx")
-    barrier = enter(me, x, y, c, z)
     dk_load = pltpu.make_async_copy(dk_hbm, dk_ref, own_s.at[2])
     dv_load = pltpu.make_async_copy(dv_ref.at[y], dv_own, own_s.at[3])
     dk_load.start()
     dv_load.start()
+    barrier = enter(me, x, y, c, z)
     pl.semaphore_wait(barrier, N_PARTNERS)
 
     def each_peer(fn):
@@ -631,42 +636,32 @@
     def v_copy(p, slot):
         return remote(v_out.at[p], v_in.at[slot], v_s, v_r, peer(p, y, z))
 
-    cosine, sine = cs_ref[0], -cs_ref[1]
-
     v_total = v_part(0)
     for j in range(4):
         v_near(j).wait_recv()
         v_total = v_total + vb_in[j].astype(F32)
     v_out[...] = v_total.astype(BF)
-    v_in[me] = v_out[me]
     each_peer(lambda p: v_copy(p, me).start())
+    own_v = pltpu.make_async_copy(v_out.at[me], v_in.at[me], own_s.at[4])
+    own_v.start()
 
     for u in range(2):
         k_ring(3, u, True).wait_recv()
         k_ring(3, u, False).wait_recv()
         total = k_part(z, u) + kr_in[3, u].astype(F32) + kl_in[3, u].astype(F32)
         k_out[u * half:(u + 1) * half] = total.astype(BF)
-    k_in[y, me] = k_out[y, me]
     loop(1, NP, lambda e: k_copy(e, 0).start())
     loop(NP, NP * NY, lambda e: k_copy(e, 1).start())
 
+    own_k = pltpu.make_async_copy(k_out.at[y, me], k_in.at[y, me], own_s.at[5])
+    own_k.start()
     settle(v_in.at[pl.ds(0, NP - 1)], v_r)
-    for h in range(NP):
-        value_scale = stab_ref[1, sidx_ref[1, h, block]]
-        gv_ref[:, h * HD:(h + 1) * HD] = (v_in[h].astype(F32) * value_scale).astype(BF)
-    settle(k_in.at[0, pl.ds(0, NP - 1)], k_r.at[0])
-    settle(k_in.at[pl.ds(0, NY - 1)], k_r.at[1])
-    for h in range(NP):
-        key_scale = stab_ref[0, sidx_ref[0, h, block]]
-        total = k_in[0, h].astype(F32)
-        for yy in range(1, NY):
-            total = total + k_in[yy, h].astype(F32)
-        gk_ref[:, h * HD:(h + 1) * HD] = (turn(total, cosine, sine) * key_scale).astype(BF)
-
     settle(o_ref.at[pl.ds(0, NP - 1)], o_r)
     settle(dqx.at[pl.ds(0, NP - 1)], q_r)
     own_o.wait()
     own_q.wait()
+    own_v.wait()
+    own_k.wait()
 
     settle(o_ref.at[pl.ds(0, NP - 1)], o_s)
     settle(dq_ref.at[pl.ds(0, NP - 1)], q_s)
@@ -682,31 +677,50 @@
     for j in range(4):
         v_far(j).wait_send()
         v_near(j).wait_send()
-
-
-def finish_kernel(ao_in, dqx_ref, gk_in, gv_in, cs_ref, ao_out, gq_out, gk_out, gv_out, gq_ref, sems, gq_s):
-    copies = [
-        pltpu.make_async_copy(src, dst, sems.at[i])
-        for i, (src, dst) in enumerate(((ao_in, ao_out), (gk_in, gk_out), (gv_in, gv_out)))
+    settle(k_in.at[0, pl.ds(0, NP - 1)], k_r.at[0])
+    settle(k_in.at[pl.ds(0, NY - 1)], k_r.at[1])
+
+
+def finish_kernel(
+    ao_ref, dq_ref, k_ref, v_ref, cs_ref, sidx_ref, stab_ref,
+    ao_out, gq_out, gk_out, gv_out,
+    gq_ref, gk_ref, gv_ref, sems, gq_s,
+):
+    block = lax.axis_index("ctx")
+    ao_store, gk_store, gv_store = [
+        pltpu.make_async_copy(src, dst, sems.at[n])
+        for n, (src, dst) in enumerate(((ao_ref, ao_out), (gk_ref, gk_out), (gv_ref, gv_out)))
     ]
-    for copy in copies:
-        copy.start()
-    cosine, sine = cs_ref[0], -cs_ref[1]
+    ao_store.start()
 
     def store(p):
         cols = pl.ds(pl.multiple_of(p * WIDE, WIDE), WIDE)
         return pltpu.make_async_copy(gq_ref.at[:, cols], gq_out.at[:, cols], gq_s.at[p])
 
+    cosine, sine = cs_ref[0], -cs_ref[1]
+
     def rotate_back(p):
         for h in range(GRP):
             cols = pl.ds(pl.multiple_of(p * WIDE + h * HD, HD), HD)
-            gq_ref[:, cols] = turn(dqx_ref[p, :, h * HD:(h + 1) * HD].astype(F32), cosine, sine).astype(BF)
+            gq_ref[:, cols] = turn(dq_ref[p, :, h * HD:(h + 1) * HD].astype(F32), cosine, sine).astype(BF)
         store(p).start()
 
     loop(0, NP, rotate_back)
-    for copy in copies:
-        copy.wait()
+    for h in range(NP):
+        cols = slice(h * HD, (h + 1) * HD)
+        value_scale = stab_ref[1, sidx_ref[1, h, block]]
+        gv_ref[:, cols] = (v_ref[h].astype(F32) * value_scale).astype(BF)
+        key_scale = stab_ref[0, sidx_ref[0, h, block]]
+        total = k_ref[0, h].astype(F32)
+        for yy in range(1, NY):
+            total = total + k_ref[yy, h].astype(F32)
+        gk_ref[:, cols] = (turn(total, cosine, sine) * key_scale).astype(BF)
+    gv_store.start()
+    gk_store.start()
+    ao_store.wait()
     loop(0, NP, lambda p: store(p).wait())
+    gv_store.wait()
+    gk_store.wait()
 
 
 def body(queries, keys, values, grad_out, doc_lengths, block_pairs, scale_index, scale_table):
@@ -730,9 +744,18 @@
             shape((NP, BLK), jnp.int32),
             shape((2, ROWS, HD), F32),
         ),
-        in_specs=[anywhere, vmem, vmem, anywhere, smem, vmem, smem, smem, vmem],
-        out_specs=(anywhere,) * 4 + (vmem,) * 2,
+        in_specs=[anywhere] * 9,
+        out_specs=(anywhere,) * 6,
         scratch_shapes=[
+            pltpu.VMEM((ROWS, NP * HD), BF),
+            pltpu.VMEM((ROWS, NP * HD), BF),
+            pltpu.SMEM(doc_lengths.shape, jnp.int32),
+            pltpu.VMEM(block_pairs.shape[::-1], jnp.int32),
+            pltpu.SMEM(scale_by_head.shape, jnp.int32),
+            pltpu.SMEM(scale_table.shape, F32),
+            pltpu.VMEM(freq.shape, F32),
+            pltpu.VMEM((NP, BLK), jnp.int32),
+            pltpu.VMEM((2, ROWS, HD), F32),
             pltpu.VMEM((ROWS, NP * WIDE), BF),
             pltpu.VMEM((NP, ROWS, WIDE), BF),
             pltpu.VMEM((NP, ROWS, HD), BF),
@@ -746,7 +769,7 @@
         + [dma((4, 2))] * 4
         + [dma((4,))] * 4
         + [dma, dma((NY,))]
-        + [dma((3,)), dma((5, 2, 2)), dma((NY,))],
+        + [dma((5,)), dma((5, 2, 2)), dma((NY,)), dma((7,))],
         compiler_params=pltpu.CompilerParams(
             collective_id=0, has_side_effects=True, vmem_limit_bytes=VMEM_LIMIT
         ),
@@ -761,53 +784,50 @@
             shape((NZ, NY, NP, ROWS, HD), BF),
             shape((NY, NZ, NP, ROWS, HD), BF),
         ),
-        in_specs=[smem, smem] + [anywhere] * 4,
+        in_specs=[anywhere] * 6,
         out_specs=(anywhere,) * 4,
-        scratch_shapes=([pltpu.VMEM((NP, ROWS, WIDE), BF)] * 2
+        scratch_shapes=[pltpu.SMEM((NP, BLK), jnp.int32), pltpu.SMEM(doc_lengths.shape, jnp.int32)]
+        + ([pltpu.VMEM((NP, ROWS, WIDE), BF)] * 2
         + [pltpu.VMEM((NZ, NY, NP, ROWS, HD), BF), pltpu.VMEM((NY, NZ, NP, ROWS, HD), BF)]) * 2
-        + [
-            pltpu.VMEM((TWIN, NBLK // CHUNK, SPAN, GRP * ROWS), F32),
-            pltpu.VMEM((TWIN, NBLK // CHUNK, SPAN, GRP * ROWS), F32),
-            pltpu.VMEM((TWIN, HD, GRP * ROWS), F32),
-            pltpu.VMEM((TWIN, HD, GRP * ROWS), F32),
-            pltpu.VMEM((NZ, NY, NP, ROWS, HD), F32),
-            pltpu.VMEM((NY, NZ, NP, ROWS, HD), F32),
-        ]
-        + [dma((2,))]
-        + [dma((NP // TWIN,))] * 4
-        + [dma((NZ,)), dma((NY,))],
+        + [pltpu.VMEM((MOST_UNITS + UNROLL, SPAN, GRP * ROWS), F32)] * 2
+        + [pltpu.VMEM((NP, HD, GRP * ROWS), F32)] * 2
+        + [pltpu.VMEM((NZ, NY, NP, ROWS, HD), F32), pltpu.VMEM((NY, NZ, NP, ROWS, HD), F32)]
+        + [pltpu.VMEM((NP, 8, GRP * ROWS), jnp.int32)]
+        + [pltpu.VMEM((NP, 8, GRP * ROWS), F32)] * 3
+        + [pltpu.SMEM((MOST_UNITS + UNROLL,), jnp.int32)]
+        + [dma((6,)), dma((NP,)), dma((NP,)), dma((NZ,)), dma((NY,))],
         compiler_params=pltpu.CompilerParams(vmem_limit_bytes=VMEM_LIMIT),
     )(lists, doc_lengths, qx, gox, ka, va)
 
-    ao, dqx, gk, gv = pl.pallas_call(
+    ao, dqx, k_terms, v_sums = pl.pallas_call(
         scatter_kernel,
         name="scatter",
         out_shape=(
             shape((ROWS, NP * WIDE), BF),
             shape((NP, ROWS, WIDE), BF),
-            shape((ROWS, NP * HD), BF),
-            shape((ROWS, NP * HD), BF),
+            shape((NY, NP, ROWS, HD), BF),
+            shape((NP, ROWS, HD), BF),
         ),
-        in_specs=[anywhere] * 4 + [vmem, smem, smem],
-        out_specs=(anywhere,) * 2 + (vmem,) * 2,
+        in_specs=[anywhere] * 4,
+        out_specs=(anywhere,) * 4,
         scratch_shapes=[pltpu.VMEM((NZ, NY, NP, ROWS, HD), BF), pltpu.VMEM((NZ, NP, ROWS, HD), BF)]
         + [pltpu.VMEM((4, 2, NY // 2, NP, ROWS, HD), BF)] * 4
         + [pltpu.VMEM((3, NP, ROWS, HD), BF)] * 2
         + [pltpu.VMEM((4, NP, ROWS, HD), BF)] * 2
-        + [pltpu.VMEM((NY, NP, ROWS, HD), BF)] * 2
+        + [pltpu.VMEM((NY, NP, ROWS, HD), BF)]
         + [pltpu.VMEM((NY, NZ, NP, ROWS, HD), BF)]
-        + [pltpu.VMEM((NP, ROWS, HD), BF)] * 2
+        + [pltpu.VMEM((NP, ROWS, HD), BF)]
         + [dma] * 4
         + [dma((4, 2))] * 4
         + [dma((4,))] * 4
         + [dma, dma((NZ,))]
         + [dma((2,))] * 2
         + [dma] * 2
-        + [dma((4,))],
+        + [dma((6,))],
         compiler_params=pltpu.CompilerParams(
             collective_id=1, has_side_effects=True, vmem_limit_bytes=VMEM_LIMIT
         ),
-    )(o, dq, dk, dv, cs, scale_by_head, scale_table)
+    )(o, dq, dk, dv)
 
     return pl.pallas_call(
         finish_kernel,
@@ -818,11 +838,17 @@
             shape((ROWS, NP * HD), BF),
             shape((ROWS, NP * HD), BF),
         ),
-        in_specs=[vmem] * 5,
+        in_specs=[vmem] * 5 + [smem] * 2,
         out_specs=(anywhere,) * 4,
-        scratch_shapes=[pltpu.VMEM((ROWS, NP * WIDE), BF), dma((3,)), dma((NP,))],
+        scratch_shapes=[
+            pltpu.VMEM((ROWS, NP * WIDE), BF),
+            pltpu.VMEM((ROWS, NP * HD), BF),
+            pltpu.VMEM((ROWS, NP * HD), BF),
+            dma((3,)),
+            dma((NP,)),
+        ],
         compiler_params=pltpu.CompilerParams(vmem_limit_bytes=VMEM_LIMIT),
-    )(ao, dqx, gk, gv, cs)
+    )(ao, dqx, k_terms, v_sums, cs, scale_by_head, scale_table)
 
 
 def solution(mesh):

time: 86.8 us -> 79.5 us (0.916)
  Pallas kernels: 85.8 us -> 78.7 us
    pallas_call x1, Pallas kernels: 13.7 us -> 7.74 us  [body(): pl.pallas_call(attend_kernel, name='attend', out_shape=(shape((NP, ROWS,...]
    pallas_call x1, Pallas kernels: 35.6 us -> 34.1 us  [body(): pl.pallas_call(gather_kernel, name='gather', out_shape=(shape((NP, ROWS,...]
where the time goes in v4:
time: 79.5 us; the launch traced here: 79.4 us
  Pallas kernels  78.7 us (99%)
    pallas_call x1, Pallas kernels, body(): pl.pallas_call(scatter_kernel, name='scatter', out_shape=(shape((ROWS, NP...  34.1 us
    pallas_call x1, Pallas kernels, body(): pl.pallas_call(gather_kernel, name='gather', out_shape=(shape((NP, ROWS,...  34.1 us
    pallas_call x1, Pallas kernels, body(): pl.pallas_call(attend_kernel, name='attend', out_shape=(shape((NP, ROWS,...  7.74 us
    pallas_call x1, Pallas kernels, body(): pl.pallas_call(finish_kernel, name='finish', out_shape=(shape((ROWS, NP *...  2.8 us

profile of v4, /device:TPU:1, one launch (start us, length us, event | category | flops | bytes accessed | tf_op | source)
XLA Modules:
  0.0 79.4 jit_solution(2227647884876750925)
XLA Ops:
  0.6 34.1 %gather.1 = (bf16[8,16,2048]{2,1,0:T(8,128)(2,1)}, bf16[8,16,2048]{2,1,0:T(8,128)(2,1)}, bf16[8,4,8,16,128]{4,3,2,1,0:T(8,128)(2,1)}, bf16[4,8,8,16,128]{4,3,2,1...) custom-call(bf16[16,16384]{1,0:T(8,128)(2,1)} %q_ref.1, bf16[16,1024]{1,0:T(8,128)(2,1)} %k_hbm.1, ...), custom_call_target="tpu_custom_call" | custom-call | tf_op jit(solution)/shard_map/gather/pallas_call | solution.py:736
  34.7 7.7 %attend.1 = (bf16[8,16,2048]{2,1,0:T(8,128)(2,1)}, bf16[8,16,2048]{2,1,0:T(8,128)(2,1)}, bf16[8,4,8,16,128]{4,3,2,1,0:T(8,128)(2,1)}, bf16[4,8,8,16,128]{4,3,2,1,0:T(8,128)(2,1)}) custom-call(s32[8,128]{1,0:T(8,128)} %get-tuple-element.18.lists_in, s32[8]{0:T(128)} %doc_in.1, bf16[8,16,2048]{2,1,0:T(8,128)(2,1)} %get-tuple-element.19.q_in, ...), custom_call_target="tpu_custom_call" | custom-call | tf_op jit(solution)/shard_map/attend/pallas_call | solution.py:778
  42.5 34.1 %scatter.1 = (bf16[16,16384]{1,0:T(8,128)(2,1)}, bf16[8,16,2048]{2,1,0:T(8,128)(2,1)}, bf16[4,8,16,128]{3,2,1,0:T(8,128)(2,1)}, bf16[8,16,128]{2,1,0:T(8,128)(2,1)}) custom-call(bf16[8,16,2048]{2,1,0:T(8,128)(2,1)} %get-tuple-element.23.o_ref, bf16[8,16,2048]{2,1,0:T(8,128)(2,1)} %get-tuple-element.24.dq_ref, ...), custom_call_target="tpu_custom_call" | custom-call | tf_op jit(solution)/shard_map/scatter/pallas_call | solution.py:802
  76.6 2.8 %finish.1 = (bf16[16,16384]{1,0:T(8,128)(2,1)}, bf16[16,16384]{1,0:T(8,128)(2,1)}, bf16[16,1024]{1,0:T(8,128)(2,1)}, bf16[16,1024]{1,0:T(8,128)(2,1)}) custom-call(bf16[16,16384]{1,0:T(8,128)(2,1)} %get-tuple-element.27.ao_ref, bf16[8,16,2048]{2,1,0:T(8,128)(2,1)} %get-tuple-element.28.dq_ref, bf16[4,8,16,128]{3,2,1,0:T(8,128)(2,1)} %get-tuple-element.29.k_ref, ...), custom_call_target="tpu_custom_call" | custom-call | tf_op jit(solution)/shard_map/finish/pallas_call | solution.py:832

commit v5 on v4

--- a/solution.py
+++ b/solution.py
@@ -19,7 +19,7 @@
 NDOC = 8
 WIDE = GRP * HD
 NEG = -1e30
-UNROLL = 6
+UNROLL = 7
 SCALE = 1.0 / math.sqrt(HD)
 EXP2_SCALE = SCALE * math.log2(math.e)
 MESH = pl.DeviceIdType.MESH
@@ -73,6 +73,11 @@
         return carry
 
     lax.fori_loop(lo, hi, step, 0)
+
+
+def by_reach(less, fn):
+    pl.when(less)(lambda: fn(NP - NC))
+    pl.when(jnp.logical_not(less))(lambda: fn(NP))
 
 
 def settle(ref, sem):
@@ -93,6 +98,7 @@
     x, y, c, z = place()
     me = NC * x + c
     block = lax.axis_index("ctx")
+    va_ref[:, :, NP - NC:] = jnp.zeros((NY, NZ, NC, ROWS, HD), BF)
     loads = [
         pltpu.make_async_copy(src, dst, load_s.at[n])
         for n, (src, dst) in enumerate((
@@ -218,14 +224,18 @@
             ref = va_ref.at[y, zz, pl.ds(part * (NP // 2), NP // 2)]
         return remote(ref, ref, vb_s.at[j], vb_r.at[j], along(hop))
 
-    def v_spread(zz, d, arriving):
+    def v_spread(zz, d):
         yy = (y + d) % NY
-        ys = yy if arriving else y
-        return remote(va_ref.at[ys, zz], va_ref.at[ys, zz], vy_s, vy_r.at[ys], device(x, yy, c, z))
+
+        def start(n):
+            ref = va_ref.at[y, zz, pl.ds(0, n)]
+            remote(ref, ref, vy_s.at[d], vy_r.at[y], device(x, yy, c, z)).start()
+
+        by_reach(yy < y, start)
 
     def spread(off):
         for d in (2, 1, 3):
-            v_spread((z + off + NZ) % NZ, d, False).start()
+            v_spread((z + off + NZ) % NZ, d)
 
     settle(va_ref.at[y, z, pl.ds(0, NP - 1)], v_r)
     for j in (2, 3, 0, 1):
@@ -301,8 +311,9 @@
     k_step(4)
 
     for d in (1, 3, 2):
-        settle(va_ref.at[(y + d) % NY], vy_r.at[(y + d) % NY])
-        v_store((y + d) % NY).start()
+        yy = (y + d) % NY
+        by_reach(y < yy, lambda n: settle(va_ref.at[yy, :, pl.ds(0, n)], vy_r.at[yy]))
+        v_store(yy).start()
 
     settle(gox_ref.at[pl.ds(0, NP - 1)], go_r)
     settle(qx_ref.at[pl.ds(0, NP - 1)], q_r)
@@ -316,7 +327,8 @@
     settle(qs.at[pl.ds(0, NP - 1)], q_s)
     settle(ks.at[pl.ds(0, NP - 1)], k_s.at[0])
     settle(ka_ref.at[z, pl.ds(0, NY - 1)], k_s.at[1])
-    settle(va_ref.at[pl.ds(0, NY - 1)], vy_s)
+    for d in range(1, NY):
+        by_reach((y + d) % NY < y, lambda n: settle(va_ref.at[y, :, pl.ds(0, n)], vy_s.at[d]))
     for s in range(4):
         for u, r in k_sends(s):
             k_ring(s, u, r, True).wait_send()
@@ -515,6 +527,7 @@
     dv_load = pltpu.make_async_copy(dv_ref.at[y], dv_own, own_s.at[3])
     dk_load.start()
     dv_load.start()
+    vy_in[:, :, NP - NC:] = jnp.zeros((NY, NZ, NC, ROWS, HD), BF)
     barrier = enter(me, x, y, c, z)
     pl.semaphore_wait(barrier, N_PARTNERS)
 
@@ -533,10 +546,20 @@
     def q_copy(p, slot):
         return remote(dq_ref.at[p], dqx.at[slot], q_s, q_r, peer(p, y, z))
 
-    def vy_copy(off, d, arriving):
+    def vy_send(off, d):
         zz, yy = (z + off + NZ) % NZ, (y + d) % NY
-        slot = yy if arriving else y
-        return remote(dv_ref.at[yy, zz], vy_in.at[slot, zz], vy_s, vy_r.at[zz], device(x, yy, c, z))
+
+        def start(n):
+            part = pl.ds(0, n)
+            remote(
+                dv_ref.at[yy, zz, part], vy_in.at[y, zz, part], vy_s.at[d], vy_r.at[NY - d, zz], device(x, yy, c, z)
+            ).start()
+
+        by_reach(yy > y, start)
+
+    def vy_arrive(zz, d):
+        yy = (y + d) % NY
+        by_reach(y > yy, lambda n: settle(vy_in.at[yy, zz, pl.ds(0, n)], vy_r.at[d, zz]))
 
     half = NY // 2
 
@@ -560,8 +583,8 @@
     def v_part(off):
         zz = (z + off + NZ) % NZ
         total = dv_own[zz].astype(F32)
-        settle(dv_own.at[pl.ds(0, NY - 1)], vy_r.at[zz])
         for d in range(1, NY):
+            vy_arrive(zz, d)
             total = total + vy_in[(y + d) % NY, zz].astype(F32)
         return total
 
@@ -582,7 +605,7 @@
     order = (3, -3, 4, 2, -2, 1, -1, 0)
     for off in order[:3]:
         for d in (2, 1, 3):
-            vy_copy(off, d, False).start()
+            vy_send(off, d)
     dk_load.wait()
     k_send(0, 0, True)
     k_send(0, 1, False)
@@ -590,7 +613,7 @@
     k_send(1, 0, False)
     for off in order[3:]:
         for d in (2, 1, 3):
-            vy_copy(off, d, False).start()
+            vy_send(off, d)
     each_peer(lambda p: o_copy(p, me).start())
     each_peer(lambda p: q_copy(p, me).start())
     own_o = pltpu.make_async_copy(o_ref.at[me], head_cols(ao_ref, me), own_s.at[0])
@@ -605,11 +628,13 @@
     v_far(0).start()
     va_out[1] = v_part(-3).astype(BF)
     v_far(1).start()
+    for u, r in ((1, True), (0, False), (0, True), (1, False)):
+        k_send(2, u, r)
     va_out[2] = v_part(4).astype(BF)
     v_far(2).start()
     v_far(3).start()
     for u, r in ((1, True), (0, False), (0, True), (1, False)):
-        k_send(2, u, r)
+        k_send(3, u, r)
     v_two = [v_part(2), v_part(-2)]
     for j in range(2):
         v_far(j).wait_recv()
@@ -626,8 +651,6 @@
     for j in range(2):
         vb_out[j] = v_part(near[j]).astype(BF)
         v_near(j).start()
-    for u, r in ((1, True), (0, False), (0, True), (1, False)):
-        k_send(3, u, r)
 
     def k_copy(e, far):
         p, yy = (me + e % NP) % NP, (y + e // NP) % NY
@@ -636,6 +659,16 @@
     def v_copy(p, slot):
         return remote(v_out.at[p], v_in.at[slot], v_s, v_r, peer(p, y, z))
 
+    for u in range(2):
+        k_ring(3, u, True).wait_recv()
+        k_ring(3, u, False).wait_recv()
+        total = k_part(z, u) + kr_in[3, u].astype(F32) + kl_in[3, u].astype(F32)
+        k_out[u * half:(u + 1) * half] = total.astype(BF)
+    loop(1, NP, lambda e: k_copy(e, 0).start())
+    loop(NP, NP * NY, lambda e: k_copy(e, 1).start())
+
+    own_k = pltpu.make_async_copy(k_out.at[y, me], k_in.at[y, me], own_s.at[5])
+    own_k.start()
     v_total = v_part(0)
     for j in range(4):
         v_near(j).wait_recv()
@@ -645,16 +678,6 @@
     own_v = pltpu.make_async_copy(v_out.at[me], v_in.at[me], own_s.at[4])
     own_v.start()
 
-    for u in range(2):
-        k_ring(3, u, True).wait_recv()
-        k_ring(3, u, False).wait_recv()
-        total = k_part(z, u) + kr_in[3, u].astype(F32) + kl_in[3, u].astype(F32)
-        k_out[u * half:(u + 1) * half] = total.astype(BF)
-    loop(1, NP, lambda e: k_copy(e, 0).start())
-    loop(NP, NP * NY, lambda e: k_copy(e, 1).start())
-
-    own_k = pltpu.make_async_copy(k_out.at[y, me], k_in.at[y, me], own_s.at[5])
-    own_k.start()
     settle(v_in.at[pl.ds(0, NP - 1)], v_r)
     settle(o_ref.at[pl.ds(0, NP - 1)], o_r)
     settle(dqx.at[pl.ds(0, NP - 1)], q_r)
@@ -668,7 +691,8 @@
     settle(v_out.at[pl.ds(0, NP - 1)], v_s)
     settle(k_out.at[0, pl.ds(0, NP - 1)], k_s.at[0])
     settle(k_out.at[pl.ds(0, NY - 1)], k_s.at[1])
-    settle(dv_ref.at[pl.ds(0, NY - 1)], vy_s)
+    for d in range(1, NY):
+        by_reach((y + d) % NY > y, lambda n: settle(dv_ref.at[y, :, pl.ds(0, n)], vy_s.at[d]))
     for s in range(4):
         for u in range(2):
             for r in (True, False):
@@ -768,7 +792,7 @@
         + [dma] * 2
         + [dma((4, 2))] * 4
         + [dma((4,))] * 4
-        + [dma, dma((NY,))]
+        + [dma((NY,)), dma((NY,))]
         + [dma((5,)), dma((5, 2, 2)), dma((NY,)), dma((7,))],
         compiler_params=pltpu.CompilerParams(
             collective_id=0, has_side_effects=True, vmem_limit_bytes=VMEM_LIMIT
@@ -820,7 +844,7 @@
         + [dma] * 4
         + [dma((4, 2))] * 4
         + [dma((4,))] * 4
-        + [dma, dma((NZ,))]
+        + [dma((NY,)), dma((NY, NZ))]
         + [dma((2,))] * 2
         + [dma] * 2
         + [dma((6,))],

time: 79.5 us -> 80.2 us (level)
    pallas_call x1, Pallas kernels: 7.74 us -> 10.5 us  [body(): pl.pallas_call(attend_kernel, name='attend', out_shape=(shape((NP, ROWS,...]
    pallas_call x1, Pallas kernels: 34.1 us -> 32.1 us  [body(): pl.pallas_call(scatter_kernel, name='scatter', out_shape=(shape((ROWS, NP...]
where the time goes in v5:
time: 80.2 us; the launch traced here: 80.1 us
  Pallas kernels  79.4 us (99%)
    pallas_call x1, Pallas kernels, body(): pl.pallas_call(gather_kernel, name='gather', out_shape=(shape((NP, ROWS,...  34.1 us
    pallas_call x1, Pallas kernels, body(): pl.pallas_call(scatter_kernel, name='scatter', out_shape=(shape((ROWS, NP...  32.1 us
    pallas_call x1, Pallas kernels, body(): pl.pallas_call(attend_kernel, name='attend', out_shape=(shape((NP, ROWS,...  10.5 us
    pallas_call x1, Pallas kernels, body(): pl.pallas_call(finish_kernel, name='finish', out_shape=(shape((ROWS, NP *...  2.8 us

profile of v5, /device:TPU:1, one launch (start us, length us, event | category | flops | bytes accessed | tf_op | source)
XLA Modules:
  0.0 80.1 jit_solution(9395803237095690412)
XLA Ops:
  0.6 34.1 %gather.1 = (bf16[8,16,2048]{2,1,0:T(8,128)(2,1)}, bf16[8,16,2048]{2,1,0:T(8,128)(2,1)}, bf16[8,4,8,16,128]{4,3,2,1,0:T(8,128)(2,1)}, bf16[4,8,8,16,128]{4,3,2,1...) custom-call(bf16[16,16384]{1,0:T(8,128)(2,1)} %q_ref.1, bf16[16,1024]{1,0:T(8,128)(2,1)} %k_hbm.1, ...), custom_call_target="tpu_custom_call" | custom-call | tf_op jit(solution)/shard_map/gather/pallas_call | solution.py:760
  34.7 10.5 %attend.1 = (bf16[8,16,2048]{2,1,0:T(8,128)(2,1)}, bf16[8,16,2048]{2,1,0:T(8,128)(2,1)}, bf16[8,4,8,16,128]{4,3,2,1,0:T(8,128)(2,1)}, bf16[4,8,8,16,128]{4,3,2,1,0:T(8,128)(2,1)}) custom-call(s32[8,128]{1,0:T(8,128)} %get-tuple-element.18.lists_in, s32[8]{0:T(128)} %doc_in.1, bf16[8,16,2048]{2,1,0:T(8,128)(2,1)} %get-tuple-element.19.q_in, ...), custom_call_target="tpu_custom_call" | custom-call | tf_op jit(solution)/shard_map/attend/pallas_call | solution.py:802
  45.2 32.1 %scatter.1 = (bf16[16,16384]{1,0:T(8,128)(2,1)}, bf16[8,16,2048]{2,1,0:T(8,128)(2,1)}, bf16[4,8,16,128]{3,2,1,0:T(8,128)(2,1)}, bf16[8,16,128]{2,1,0:T(8,128)(2,1)}) custom-call(bf16[8,16,2048]{2,1,0:T(8,128)(2,1)} %get-tuple-element.23.o_ref, bf16[8,16,2048]{2,1,0:T(8,128)(2,1)} %get-tuple-element.24.dq_ref, ...), custom_call_target="tpu_custom_call" | custom-call | tf_op jit(solution)/shard_map/scatter/pallas_call | solution.py:826
  77.3 2.8 %finish.1 = (bf16[16,16384]{1,0:T(8,128)(2,1)}, bf16[16,16384]{1,0:T(8,128)(2,1)}, bf16[16,1024]{1,0:T(8,128)(2,1)}, bf16[16,1024]{1,0:T(8,128)(2,1)}) custom-call(bf16[16,16384]{1,0:T(8,128)(2,1)} %get-tuple-element.27.ao_ref, bf16[8,16,2048]{2,1,0:T(8,128)(2,1)} %get-tuple-element.28.dq_ref, bf16[4,8,16,128]{3,2,1,0:T(8,128)(2,1)} %get-tuple-element.29.k_ref, ...), custom_call_target="tpu_custom_call" | custom-call | tf_op jit(solution)/shard_map/finish/pallas_call | solution.py:856

commit v6 on v5

--- a/solution.py
+++ b/solution.py
@@ -19,6 +19,7 @@
 NDOC = 8
 WIDE = GRP * HD
 NEG = -1e30
+SUB = 4
 UNROLL = 7
 SCALE = 1.0 / math.sqrt(HD)
 EXP2_SCALE = SCALE * math.log2(math.e)
@@ -114,6 +115,21 @@
     for load in loads:
         load.wait()
 
+    for h in range(NP):
+        value_scale = stab_ref[1, sidx_ref[1, h, block]]
+        vs[h] = (v_ref[:, h * HD:(h + 1) * HD].astype(F32) * value_scale).astype(BF)
+    va_ref[y, z, me] = vs[me]
+
+    pl.semaphore_wait(barrier, N_PARTNERS)
+
+    def each_peer(fn):
+        loop(1, NP, lambda d: fn((me + d) % NP))
+
+    def v_copy(p, slot):
+        return remote(vs.at[p], va_ref.at[y, z, slot], v_s, v_r, peer(p, y, z))
+
+    each_peer(lambda p: v_copy(p, me).start())
+
     token = BLK * block + ROWS * z + lax.broadcasted_iota(jnp.int32, (ROWS, HD), 0)
     start = jnp.zeros((ROWS, HD), jnp.int32)
     end = 0
@@ -130,32 +146,20 @@
     cs_store.start()
 
     for h in range(NP):
-        cols = slice(h * HD, (h + 1) * HD)
         key_scale = stab_ref[0, sidx_ref[0, h, block]]
-        value_scale = stab_ref[1, sidx_ref[1, h, block]]
-        ks[h] = turn(k_ref[:, cols].astype(F32) * key_scale, cosine, sine).astype(BF)
-        vs[h] = (v_ref[:, cols].astype(F32) * value_scale).astype(BF)
+        keys = k_ref[:, h * HD:(h + 1) * HD].astype(F32) * key_scale
+        ks[h] = turn(keys, cosine, sine).astype(BF)
+    ka_ref[z, y, me] = ks[me]
 
     def rotate_q(p):
         for h in range(GRP):
             cols = pl.ds(pl.multiple_of(p * WIDE + h * HD, HD), HD)
             qs[p, :, h * HD:(h + 1) * HD] = turn(q_in[:, cols].astype(F32), cosine, sine).astype(BF)
 
-    ka_ref[z, y, me] = ks[me]
-    va_ref[y, z, me] = vs[me]
-
-    pl.semaphore_wait(barrier, N_PARTNERS)
-
-    def each_peer(fn):
-        loop(1, NP, lambda d: fn((me + d) % NP))
-
     def k_copy(e, far):
         p, yy = (me + e % NP) % NP, (y + e // NP) % NY
         return remote(ks.at[p], ka_ref.at[z, y, me], k_s.at[far], k_r.at[far], peer(p, yy, z))
 
-    def v_copy(p, slot):
-        return remote(vs.at[p], va_ref.at[y, z, slot], v_s, v_r, peer(p, y, z))
-
     def go_cols(p):
         return go_ref.at[:, pl.ds(pl.multiple_of(p * WIDE, WIDE), WIDE)]
 
@@ -165,7 +169,6 @@
     def q_copy(p, slot):
         return remote(qs.at[p], qx_ref.at[slot], q_s, q_r, peer(p, y, z))
 
-    each_peer(lambda p: v_copy(p, me).start())
     loop(1, NP, lambda e: k_copy(e, 0).start())
     loop(NP, NP * NY, lambda e: k_copy(e, 1).start())
     each_peer(lambda p: go_copy(p, me).start())
@@ -188,19 +191,19 @@
     def k_ring(s, u, rightward, sending):
         far = s if sending else s + 1
         zz = (z + NZ - far) % NZ if rightward else (z + far) % NZ
-        ref = ka_ref.at[zz, pl.ds(u * (NY // 2), NY // 2)]
+        ref = ka_ref.at[zz, pl.ds(u * (NY // SUB), NY // SUB)]
         if rightward:
             return remote(ref, ref, kzr_s.at[s, u], kzr_r.at[s, u], along(1))
         return remote(ref, ref, kzl_s.at[s, u], kzl_r.at[s, u], along(-1))
 
     def k_sends(s):
-        return [(u, r) for u in range(2) for r in (True, False) if s < 3 or (u == 0) == r]
+        return [(u, r) for u in range(SUB) for r in (True, False) if s < 3 or (u < SUB // 2) == r]
 
     def k_store(s, u, rightward):
         zz = (z + NZ - s) % NZ if rightward else (z + s) % NZ
-        part = pl.ds(u * (NY // 2), NY // 2)
+        part = pl.ds(u * (NY // SUB), NY // SUB)
         return pltpu.make_async_copy(
-            ka_ref.at[zz, part], ka_out.at[zz, part], kout_s.at[s, u if rightward else 1 - u, 0 if rightward else 1]
+            ka_ref.at[zz, part], ka_out.at[zz, part], kout_s.at[s, u, 0 if rightward else 1]
         )
 
     def v_store(yy):
@@ -245,7 +248,7 @@
     settle(ka_ref.at[z, pl.ds(0, NY - 1)], k_r.at[1])
     for u, r in k_sends(0):
         k_ring(0, u, r, True).start()
-    for u in range(2):
+    for u in range(SUB):
         k_store(0, u, True).start()
 
     lane = lax.broadcasted_iota(jnp.int32, (NP, BLK), 1)
@@ -336,7 +339,7 @@
         v_first(j, False).wait_send()
         v_second(j, False).wait_send()
 
-    for u in range(2):
+    for u in range(SUB):
         k_store(0, u, True).wait()
     for s in range(1, 5):
         for u, r in k_sends(s - 1):
@@ -561,7 +564,9 @@
         yy = (y + d) % NY
         by_reach(y > yy, lambda n: settle(vy_in.at[yy, zz, pl.ds(0, n)], vy_r.at[d, zz]))
 
-    half = NY // 2
+    part_y = NY // SUB
+    early = [(u, u >= SUB // 2) for u in range(SUB)]
+    late = [(u, u < SUB // 2) for u in range(SUB)]
 
     def k_ring(s, u, rightward):
         if rightward:
@@ -569,12 +574,12 @@
         return remote(kl_out.at[s, u], kl_in.at[s, u], kzl_s.at[s, u], kzl_r.at[s, u], along(-1))
 
     def k_part(zz, u):
-        return dk_ref[zz, u * half:(u + 1) * half].astype(F32)
+        return dk_ref[zz, u * part_y:(u + 1) * part_y].astype(F32)
 
     def k_send(s, u, rightward):
         zz = (z + 4 - s) % NZ if rightward else (z + 4 + s) % NZ
         total = k_part(zz, u)
-        if s > 1 or (s == 1 and (u == 0) == rightward):
+        if s > 1 or (s == 1 and (u < SUB // 2) == rightward):
             k_ring(s - 1, u, rightward).wait_recv()
             total = total + (kr_in if rightward else kl_in)[s - 1, u].astype(F32)
         (kr_out if rightward else kl_out)[s, u] = total.astype(BF)
@@ -607,10 +612,10 @@
         for d in (2, 1, 3):
             vy_send(off, d)
     dk_load.wait()
-    k_send(0, 0, True)
-    k_send(0, 1, False)
-    k_send(1, 1, True)
-    k_send(1, 0, False)
+    for u, r in late:
+        k_send(0, u, r)
+    for u, r in early:
+        k_send(1, u, r)
     for off in order[3:]:
         for d in (2, 1, 3):
             vy_send(off, d)
@@ -622,18 +627,18 @@
     own_q.start()
 
     dv_load.wait()
-    k_send(1, 0, True)
-    k_send(1, 1, False)
+    for u, r in late:
+        k_send(1, u, r)
     va_out[0] = v_part(3).astype(BF)
     v_far(0).start()
     va_out[1] = v_part(-3).astype(BF)
     v_far(1).start()
-    for u, r in ((1, True), (0, False), (0, True), (1, False)):
+    for u, r in early + late:
         k_send(2, u, r)
     va_out[2] = v_part(4).astype(BF)
     v_far(2).start()
     v_far(3).start()
-    for u, r in ((1, True), (0, False), (0, True), (1, False)):
+    for u, r in early + late:
         k_send(3, u, r)
     v_two = [v_part(2), v_part(-2)]
     for j in range(2):
@@ -659,11 +664,11 @@
     def v_copy(p, slot):
         return remote(v_out.at[p], v_in.at[slot], v_s, v_r, peer(p, y, z))
 
-    for u in range(2):
+    for u in range(SUB):
         k_ring(3, u, True).wait_recv()
         k_ring(3, u, False).wait_recv()
         total = k_part(z, u) + kr_in[3, u].astype(F32) + kl_in[3, u].astype(F32)
-        k_out[u * half:(u + 1) * half] = total.astype(BF)
+        k_out[u * part_y:(u + 1) * part_y] = total.astype(BF)
     loop(1, NP, lambda e: k_copy(e, 0).start())
     loop(NP, NP * NY, lambda e: k_copy(e, 1).start())
 
@@ -694,9 +699,9 @@
     for d in range(1, NY):
         by_reach((y + d) % NY > y, lambda n: settle(dv_ref.at[y, :, pl.ds(0, n)], vy_s.at[d]))
     for s in range(4):
-        for u in range(2):
+        for u in range(SUB):
             for r in (True, False):
-                if s or (u == 0) == r:
+                if s or (u < SUB // 2) == r:
                     k_ring(s, u, r).wait_send()
     for j in range(4):
         v_far(j).wait_send()
@@ -706,30 +711,52 @@
 
 
 def finish_kernel(
+    ao_in, dq_in, k_in, v_in, cs_in, sidx_in, stab_in,
+    ao_out, gq_out, gk_out, gv_out,
     ao_ref, dq_ref, k_ref, v_ref, cs_ref, sidx_ref, stab_ref,
-    ao_out, gq_out, gk_out, gv_out,
-    gq_ref, gk_ref, gv_ref, sems, gq_s,
+    gq_ref, gk_ref, gv_ref, sems, gq_s, dq_s, load_s,
 ):
     block = lax.axis_index("ctx")
+
+    def dq_load(p):
+        return pltpu.make_async_copy(dq_in.at[p], dq_ref.at[p], dq_s.at[p])
+
+    cs_load, ao_load, *rest = [
+        pltpu.make_async_copy(src, dst, load_s.at[n])
+        for n, (src, dst) in enumerate((
+            (cs_in, cs_ref), (ao_in, ao_ref), (k_in, k_ref), (v_in, v_ref), (sidx_in, sidx_ref), (stab_in, stab_ref)
+        ))
+    ]
+    cs_load.start()
+    loop(0, NP, lambda p: dq_load(p).start())
+    ao_load.start()
+    for load in rest:
+        load.start()
     ao_store, gk_store, gv_store = [
         pltpu.make_async_copy(src, dst, sems.at[n])
         for n, (src, dst) in enumerate(((ao_ref, ao_out), (gk_ref, gk_out), (gv_ref, gv_out)))
     ]
-    ao_store.start()
 
     def store(p):
         cols = pl.ds(pl.multiple_of(p * WIDE, WIDE), WIDE)
         return pltpu.make_async_copy(gq_ref.at[:, cols], gq_out.at[:, cols], gq_s.at[p])
 
+    cs_load.wait()
     cosine, sine = cs_ref[0], -cs_ref[1]
 
     def rotate_back(p):
+        dq_load(p).wait()
         for h in range(GRP):
             cols = pl.ds(pl.multiple_of(p * WIDE + h * HD, HD), HD)
             gq_ref[:, cols] = turn(dq_ref[p, :, h * HD:(h + 1) * HD].astype(F32), cosine, sine).astype(BF)
         store(p).start()
 
-    loop(0, NP, rotate_back)
+    loop(0, NP // 2, rotate_back)
+    ao_load.wait()
+    ao_store.start()
+    loop(NP // 2, NP, rotate_back)
+    for load in rest:
+        load.wait()
     for h in range(NP):
         cols = slice(h * HD, (h + 1) * HD)
         value_scale = stab_ref[1, sidx_ref[1, h, block]]
@@ -752,9 +779,7 @@
     freq = np.exp(half.astype(np.float32)).astype(np.float32)
     freq = jnp.asarray(np.tile(np.concatenate([freq, freq])[None], (8, 1)))
     scale_by_head = scale_index.transpose(0, 2, 1)
-    vmem = pl.BlockSpec(memory_space=pltpu.VMEM)
     anywhere = pl.BlockSpec(memory_space=pl.ANY)
-    smem = pl.BlockSpec(memory_space=pltpu.SMEM)
     dma = pltpu.SemaphoreType.DMA
     shape = jax.ShapeDtypeStruct
     qx, gox, ka, va, lists, cs = pl.pallas_call(
@@ -790,10 +815,10 @@
         + [dma] * 4
         + [dma((2,))] * 2
         + [dma] * 2
-        + [dma((4, 2))] * 4
+        + [dma((4, SUB))] * 4
         + [dma((4,))] * 4
         + [dma((NY,)), dma((NY,))]
-        + [dma((5,)), dma((5, 2, 2)), dma((NY,)), dma((7,))],
+        + [dma((5,)), dma((5, SUB, 2)), dma((NY,)), dma((7,))],
         compiler_params=pltpu.CompilerParams(
             collective_id=0, has_side_effects=True, vmem_limit_bytes=VMEM_LIMIT
         ),
@@ -835,14 +860,14 @@
         in_specs=[anywhere] * 4,
         out_specs=(anywhere,) * 4,
         scratch_shapes=[pltpu.VMEM((NZ, NY, NP, ROWS, HD), BF), pltpu.VMEM((NZ, NP, ROWS, HD), BF)]
-        + [pltpu.VMEM((4, 2, NY // 2, NP, ROWS, HD), BF)] * 4
+        + [pltpu.VMEM((4, SUB, NY // SUB, NP, ROWS, HD), BF)] * 4
         + [pltpu.VMEM((3, NP, ROWS, HD), BF)] * 2
         + [pltpu.VMEM((4, NP, ROWS, HD), BF)] * 2
         + [pltpu.VMEM((NY, NP, ROWS, HD), BF)]
         + [pltpu.VMEM((NY, NZ, NP, ROWS, HD), BF)]
         + [pltpu.VMEM((NP, ROWS, HD), BF)]
         + [dma] * 4
-        + [dma((4, 2))] * 4
+        + [dma((4, SUB))] * 4
         + [dma((4,))] * 4
         + [dma((NY,)), dma((NY, NZ))]
         + [dma((2,))] * 2
@@ -862,14 +887,23 @@
             shape((ROWS, NP * HD), BF),
             shape((ROWS, NP * HD), BF),
         ),
-        in_specs=[vmem] * 5 + [smem] * 2,
+        in_specs=[anywhere] * 7,
         out_specs=(anywhere,) * 4,
         scratch_shapes=[
+            pltpu.VMEM((ROWS, NP * WIDE), BF),
+            pltpu.VMEM((NP, ROWS, WIDE), BF),
+            pltpu.VMEM((NY, NP, ROWS, HD), BF),
+            pltpu.VMEM((NP, ROWS, HD), BF),
+            pltpu.VMEM((2, ROWS, HD), F32),
+            pltpu.SMEM(scale_by_head.shape, jnp.int32),
+            pltpu.SMEM(scale_table.shape, F32),
             pltpu.VMEM((ROWS, NP * WIDE), BF),
             pltpu.VMEM((ROWS, NP * HD), BF),
             pltpu.VMEM((ROWS, NP * HD), BF),
             dma((3,)),
             dma((NP,)),
+            dma((NP,)),
+            dma((6,)),
         ],
         compiler_params=pltpu.CompilerParams(vmem_limit_bytes=VMEM_LIMIT),
     )(ao, dqx, k_terms, v_sums, cs, scale_by_head, scale_table)

time: 80.2 us -> 78.2 us (0.975)
  Pallas kernels: 79.4 us -> 77.3 us
    pallas_call x1, Pallas kernels: 32.1 us -> 30.8 us  [body(): pl.pallas_call(scatter_kernel, name='scatter', out_shape=(shape((ROWS, NP...]
where the time goes in v6:
time: 78.2 us; the launch traced here: 78 us
  Pallas kernels  77.3 us (99%)
    pallas_call x1, Pallas kernels, body(): pl.pallas_call(gather_kernel, name='gather', out_shape=(shape((NP, ROWS,...  33.3 us
    pallas_call x1, Pallas kernels, body(): pl.pallas_call(scatter_kernel, name='scatter', out_shape=(shape((ROWS, NP...  30.8 us
    pallas_call x1, Pallas kernels, body(): pl.pallas_call(attend_kernel, name='attend', out_shape=(shape((NP, ROWS,...  10.5 us
    pallas_call x1, Pallas kernels, body(): pl.pallas_call(finish_kernel, name='finish', out_shape=(shape((ROWS, NP *...  2.66 us

profile of v6, /device:TPU:1, one launch (start us, length us, event | category | flops | bytes accessed | tf_op | source)
XLA Modules:
  0.0 78.0 jit_solution(16275675709703516799)
XLA Ops:
  0.6 33.3 %gather.1 = (bf16[8,16,2048]{2,1,0:T(8,128)(2,1)}, bf16[8,16,2048]{2,1,0:T(8,128)(2,1)}, bf16[8,4,8,16,128]{4,3,2,1,0:T(8,128)(2,1)}, bf16[4,8,8,16,128]{4,3,2,1...) custom-call(bf16[16,16384]{1,0:T(8,128)(2,1)} %q_ref.1, bf16[16,1024]{1,0:T(8,128)(2,1)} %k_hbm.1, ...), custom_call_target="tpu_custom_call" | custom-call | tf_op jit(solution)/shard_map/gather/pallas_call | solution.py:785
  34.0 10.5 %attend.1 = (bf16[8,16,2048]{2,1,0:T(8,128)(2,1)}, bf16[8,16,2048]{2,1,0:T(8,128)(2,1)}, bf16[8,4,8,16,128]{4,3,2,1,0:T(8,128)(2,1)}, bf16[4,8,8,16,128]{4,3,2,1,0:T(8,128)(2,1)}) custom-call(s32[8,128]{1,0:T(8,128)} %get-tuple-element.18.lists_in, s32[8]{0:T(128)} %doc_in.1, bf16[8,16,2048]{2,1,0:T(8,128)(2,1)} %get-tuple-element.19.q_in, ...), custom_call_target="tpu_custom_call" | custom-call | tf_op jit(solution)/shard_map/attend/pallas_call | solution.py:827
  44.5 30.8 %scatter.1 = (bf16[16,16384]{1,0:T(8,128)(2,1)}, bf16[8,16,2048]{2,1,0:T(8,128)(2,1)}, bf16[4,8,16,128]{3,2,1,0:T(8,128)(2,1)}, bf16[8,16,128]{2,1,0:T(8,128)(2,1)}) custom-call(bf16[8,16,2048]{2,1,0:T(8,128)(2,1)} %get-tuple-element.23.o_ref, bf16[8,16,2048]{2,1,0:T(8,128)(2,1)} %get-tuple-element.24.dq_ref, ...), custom_call_target="tpu_custom_call" | custom-call | tf_op jit(solution)/shard_map/scatter/pallas_call | solution.py:851
  75.3 2.7 %finish.1 = (bf16[16,16384]{1,0:T(8,128)(2,1)}, bf16[16,16384]{1,0:T(8,128)(2,1)}, bf16[16,1024]{1,0:T(8,128)(2,1)}, bf16[16,1024]{1,0:T(8,128)(2,1)}) custom-call(bf16[16,16384]{1,0:T(8,128)(2,1)} %get-tuple-element.27.ao_in, bf16[8,16,2048]{2,1,0:T(8,128)(2,1)} %get-tuple-element.28.dq_in, bf16[4,8,16,128]{3,2,1,0:T(8,128)(2,1)} %get-tuple-element.29.k_in, ...), custom_call_target="tpu_custom_call" | custom-call | tf_op jit(solution)/shard_map/finish/pallas_call | solution.py:881
